TPU v7x, 256 devices: a whole 4x4x8 slice. The times are simulated.
256 devices in a mesh: tm: 64 (over z_hi, y, x), space: 4 (over z_lo, core).
Axes of the slice: x: 4, y: 4, z: 8 (z_hi: 4, z_lo: 2; z = z_hi * 2 + z_lo), core: 2. Of those that a mesh axis runs over, the one named last changes fastest.
Arguments:
- node_fields: float32 [64, 5, 32, 128, 128], P('tm', None, 'space'), may hold values from -6 to 6
- region_label: int32 [32, 128, 128], P('space'), may hold values from 0 to 3
- sheet_shift: int32 [64, 128], P('tm'), may hold values from 0 to 1
- diffusivity: float32 [4], replicated, may hold values from 0.02 to 0.15
Outputs:
- updated_nodes: float32 [64, 5, 32, 128, 128], P('tm', None, 'space')
All inputs are finite; a program needn't handle non-finite values.
Results may differ from a plain program's by a relative error of at most 0.00002.
Values sent between devices are 32-bit elements; how exact they have to be, the bound alone decides.
No kernel may reach another device: no remote copies, remote signals or barrier semaphores. Data moves between devices by JAX's collectives and lax.ppermute only.
A program may use at most 64 MiB of HBM per device.

v0:
```python
import math

import jax
import jax.numpy as jnp
import numpy as np
from jax import lax
from jax.sharding import PartitionSpec as P

NODES = 5
FINE_SWEEPS = 2


slice_length = 1.0


def with_halo(block, sides, width):
    for axis, dim in sides:
        count = lax.axis_size(axis)
        forward = [(i, i + 1) for i in range(count - 1)]
        backward = [(target, source) for source, target in forward]
        low = lax.ppermute(
            lax.slice_in_dim(block, block.shape[dim] - width, None, axis=dim), axis, forward
        )
        high = lax.ppermute(lax.slice_in_dim(block, 0, width, axis=dim), axis, backward)
        block = jnp.concatenate([low, block, high], axis=dim)
    return block


def from_behind(value, axis, by):
    peers = lax.axis_size(axis)
    pairs = [(i, i + by) for i in range(peers) if 0 <= i + by < peers]
    return lax.ppermute(value, axis, pairs)


def node_tables():
    radius = math.sqrt(3.0 / 7.0)
    points = [0.0, (1.0 - radius) / 2.0, 0.5, (1.0 + radius) / 2.0, 1.0]
    integrals = np.zeros((4, 5))
    for column in range(5):
        coeffs = [1.0]
        divisor = 1.0
        for other in range(5):
            if other != column:
                anchor = points[other]
                product = [0.0] * (len(coeffs) + 1)
                for degree in range(len(coeffs)):
                    product[degree + 1] = product[degree + 1] + coeffs[degree]
                    product[degree] = product[degree] - anchor * coeffs[degree]
                coeffs = product
                divisor = divisor * (points[column] - anchor)
        for row in range(4):
            bottom = points[row]
            summit = points[row + 1]
            amount = 0.0
            for degree in range(len(coeffs)):
                amount = amount + coeffs[degree] / (degree + 1) * (
                    summit ** (degree + 1) - bottom ** (degree + 1)
                )
            integrals[row, column] = amount / divisor
    return (np.array(points), integrals)


def combine(coefficients, stack):
    total = float(coefficients[0]) * stack[0]
    for index in range(1, len(coefficients)):
        total = total + float(coefficients[index]) * stack[index]
    return total


def lookup(labels, table):
    result = jnp.zeros(labels.shape, jnp.float32)
    for region in range(table.shape[0]):
        result = result + jnp.where(labels == region, table[region], 0.0)
    return result


def restrict(field):
    shape = field.shape
    blocks = field.reshape(shape[:-3] + (shape[-3] // 4, 4, shape[-2] // 2, 2, shape[-1]))
    return jnp.mean(blocks, axis=(-4, -2))


def prolong(coarse):
    return jnp.repeat(jnp.repeat(coarse, 4, axis=-3), 2, axis=-2)


def pad_rows(field):
    return jnp.pad(field, [(0, 0)] * (field.ndim - 3) + [(1, 1), (0, 0), (0, 0)])


def fine_rims(stack):
    return with_halo(stack, (("space", 1),), 1)


def neighbours(padded):
    center = padded[..., 1:-1, :, :]
    vertical = padded[..., 2:, :, :] + padded[..., :-2, :, :]
    across = jnp.roll(center, 1, -2) + jnp.roll(center, -1, -2)
    sideways = jnp.pad(center, [(0, 0)] * (center.ndim - 1) + [(1, 1)])
    lateral = sideways[..., 2:] + sideways[..., :-2]
    return (center, vertical, across, lateral)


def fine_rate(padded, kappa, advect):
    center, vertical, across, lateral = neighbours(padded)
    diffusion = kappa * (vertical + across + lateral - 6.0 * center)
    return diffusion - advect * (center - jnp.roll(center, 1, -2))


def coarse_rate(padded, kappa, advect):
    center, vertical, across, lateral = neighbours(padded)
    diffusion = kappa * (
        (vertical - 2.0 * center) / 16.0 + (across - 2.0 * center) / 4.0 + (lateral - 2.0 * center)
    )
    return diffusion - 0.5 * advect * (center - jnp.roll(center, 1, -2))


def coarse_advance(initial, padded, kappa, advect, constant):
    return initial + slice_length * coarse_rate(padded, kappa, advect) + constant


def apply_correction(fields, delta_start, delta_end):
    times_table, integral_table = node_tables()
    pieces = []
    for node in range(NODES):
        weight = float(times_table[node])
        pieces.append(fields[node] + prolong((1.0 - weight) * delta_start + weight * delta_end))
    return jnp.stack(pieces)


def fine_sweeps(corrected, rates, kappa, advect, rims):
    times_table, integral_table = node_tables()
    old_values, old_rates = (corrected, rates)
    for sweep in range(FINE_SWEEPS):
        values = [old_values[0]]
        new_rates = [old_rates[0]]
        for node in range(NODES - 1):
            spacing = float(times_table[node + 1] - times_table[node]) * slice_length
            value = (
                values[node]
                + spacing * (new_rates[node] - old_rates[node])
                + slice_length * combine(integral_table[node], old_rates)
            )
            values.append(value)
            if node < NODES - 2 or sweep < FINE_SWEEPS - 1:
                new_rates.append(fine_rate(rims(value[None]), kappa, advect)[0])
        old_values = jnp.stack(values)
        if sweep < FINE_SWEEPS - 1:
            old_rates = jnp.stack(new_rates)
    return old_values


def shards(node_fields, region_label, sheet_shift, diffusivity):
    times_table, integral_table = node_tables()
    weight_table = integral_table.sum(axis=0)
    fields = node_fields[0]
    kappa = lookup(region_label, diffusivity)
    kappa_coarse = restrict(kappa)
    advect = sheet_shift[0].astype(jnp.float32) / slice_length
    first = lax.axis_index("tm") == 0
    arrived = from_behind(fields[NODES - 1], "tm", 1)
    start = jnp.where(first, fields[0], arrived)
    fields = jnp.concatenate([start[None], fields[1:]], 0)
    rates = fine_rate(fine_rims(fields), kappa, advect)
    coarse_start = restrict(start)
    coarse_end = restrict(fields[NODES - 1])
    moved = restrict(slice_length * combine(weight_table, rates))
    whole_start, whole_moved, whole_kappa = (
        lax.all_gather(coarse_start, "space", axis=0, tiled=True),
        lax.all_gather(moved, "space", axis=0, tiled=True),
        lax.all_gather(kappa_coarse, "space", axis=0, tiled=True),
    )
    constant = whole_moved - slice_length * coarse_rate(pad_rows(whole_start), whole_kappa, advect)

    def advance_whole(initial):
        return coarse_advance(initial, pad_rows(initial), whole_kappa, advect, constant)

    def turn_whole(index, carry):
        received = from_behind(carry[1], "tm", 1)
        begin_value = jnp.where(first, whole_start, received)
        return (begin_value, advance_whole(begin_value))

    whole_begin, whole_end = lax.fori_loop(
        0, lax.axis_size("tm") - 1, turn_whole, (whole_start, advance_whole(whole_start))
    )
    rows = coarse_start.shape[0]
    offset = lax.axis_index("space") * rows
    begin = lax.dynamic_slice_in_dim(whole_begin, offset, rows, 0)
    ending = lax.dynamic_slice_in_dim(whole_end, offset, rows, 0)
    corrected = apply_correction(fields, begin - coarse_start, ending - coarse_end)
    corrected_rates = fine_rate(fine_rims(corrected), kappa, advect)
    result = fine_sweeps(corrected, corrected_rates, kappa, advect, fine_rims)
    return result[None]


def solution(mesh):
    in_specs = (P("tm", None, "space", None, None), P("space", None, None), P("tm", None), P())
    out_specs = P("tm", None, "space", None, None)
    return jax.shard_map(shards, mesh=mesh, in_specs=in_specs, out_specs=out_specs, check_vma=False)
```

profile of v0, /device:TPU:160, one launch (start us, length us, event | category | flops | bytes accessed | tf_op | source)
XLA Modules:
  0.0 1304.4 jit_solution(15347443665020702311)
XLA Ops:
  19.4 14.0 %collective-permute-done.1 = f32[8,128,128]{2,1,0:T(8,128)} collective-permute-done((f32[8,128,128]{2,1,0:T(8,128)}, f32[8,128,128]{2,1,0:T(8,128)}, u32[]{:S(2)}, u32[]{:S(2)}) %collective-permute-start.1) | collective-permute-done | bytes 524320 | tf_op jit(solution)/shard_map/ppermute | solution.py:32
  68.0 1115.7 %while.14 = (s32[]{:T(128)}, f32[8,64,128]{2,1,0:T(8,128)}, f32[8,64,128]{2,1,0:T(8,128)S(1)}, pred[]{:T(512)}, f32[8,64,128]{2,1,0:T(8,128)S(1)}, /*index=5*/f3...) while((s32[]{:T(128)}, f32[8,64,128]{2,1,0:T(8,128)}, ...), condition=%wide.region_4.5_spmd, body=%wide.region_3.4_spmd.sunk | while | flops 1310850 | bytes 5506722 | solution.py:183
  70.0 20.4 %collective-permute-done = f32[8,64,128]{2,1,0:T(8,128)S(1)} collective-permute-done((f32[8,64,128]{2,1,0:T(8,128)S(1)}, f32[8,64,128]{2,1,0:T(8,128)S(1)}, u32[]{:S(2)}, u32[]{:S(2)}) %collective-permute-start) | collective-permute-done | bytes 262176 | tf_op jit(solution)/shard_map/while/body/eval_jaxpr/ppermute | solution.py:32
  93.1 17.8 %collective-permute-done = f32[8,64,128]{2,1,0:T(8,128)S(1)} collective-permute-done((f32[8,64,128]{2,1,0:T(8,128)S(1)}, f32[8,64,128]{2,1,0:T(8,128)S(1)}, u32[]{:S(2)}, u32[]{:S(2)}) %collective-permute-start) | collective-permute-done | bytes 262176 | tf_op jit(solution)/shard_map/while/body/eval_jaxpr/ppermute | solution.py:32
  113.5 15.1 %collective-permute-done = f32[8,64,128]{2,1,0:T(8,128)S(1)} collective-permute-done((f32[8,64,128]{2,1,0:T(8,128)S(1)}, f32[8,64,128]{2,1,0:T(8,128)S(1)}, u32[]{:S(2)}, u32[]{:S(2)}) %collective-permute-start) | collective-permute-done | bytes 262176 | tf_op jit(solution)/shard_map/while/body/eval_jaxpr/ppermute | solution.py:32
  131.3 16.4 %collective-permute-done = f32[8,64,128]{2,1,0:T(8,128)S(1)} collective-permute-done((f32[8,64,128]{2,1,0:T(8,128)S(1)}, f32[8,64,128]{2,1,0:T(8,128)S(1)}, u32[]{:S(2)}, u32[]{:S(2)}) %collective-permute-start) | collective-permute-done | bytes 262176 | tf_op jit(solution)/shard_map/while/body/eval_jaxpr/ppermute | solution.py:32
  150.4 18.9 %collective-permute-done = f32[8,64,128]{2,1,0:T(8,128)S(1)} collective-permute-done((f32[8,64,128]{2,1,0:T(8,128)S(1)}, f32[8,64,128]{2,1,0:T(8,128)S(1)}, u32[]{:S(2)}, u32[]{:S(2)}) %collective-permute-start) | collective-permute-done | bytes 262176 | tf_op jit(solution)/shard_map/while/body/eval_jaxpr/ppermute | solution.py:32
  171.9 17.0 %collective-permute-done = f32[8,64,128]{2,1,0:T(8,128)S(1)} collective-permute-done((f32[8,64,128]{2,1,0:T(8,128)S(1)}, f32[8,64,128]{2,1,0:T(8,128)S(1)}, u32[]{:S(2)}, u32[]{:S(2)}) %collective-permute-start) | collective-permute-done | bytes 262176 | tf_op jit(solution)/shard_map/while/body/eval_jaxpr/ppermute | solution.py:32
  191.6 17.4 %collective-permute-done = f32[8,64,128]{2,1,0:T(8,128)S(1)} collective-permute-done((f32[8,64,128]{2,1,0:T(8,128)S(1)}, f32[8,64,128]{2,1,0:T(8,128)S(1)}, u32[]{:S(2)}, u32[]{:S(2)}) %collective-permute-start) | collective-permute-done | bytes 262176 | tf_op jit(solution)/shard_map/while/body/eval_jaxpr/ppermute | solution.py:32
  211.7 17.1 %collective-permute-done = f32[8,64,128]{2,1,0:T(8,128)S(1)} collective-permute-done((f32[8,64,128]{2,1,0:T(8,128)S(1)}, f32[8,64,128]{2,1,0:T(8,128)S(1)}, u32[]{:S(2)}, u32[]{:S(2)}) %collective-permute-start) | collective-permute-done | bytes 262176 | tf_op jit(solution)/shard_map/while/body/eval_jaxpr/ppermute | solution.py:32
  231.4 13.9 %collective-permute-done = f32[8,64,128]{2,1,0:T(8,128)S(1)} collective-permute-done((f32[8,64,128]{2,1,0:T(8,128)S(1)}, f32[8,64,128]{2,1,0:T(8,128)S(1)}, u32[]{:S(2)}, u32[]{:S(2)}) %collective-permute-start) | collective-permute-done | bytes 262176 | tf_op jit(solution)/shard_map/while/body/eval_jaxpr/ppermute | solution.py:32
  248.0 13.7 %collective-permute-done = f32[8,64,128]{2,1,0:T(8,128)S(1)} collective-permute-done((f32[8,64,128]{2,1,0:T(8,128)S(1)}, f32[8,64,128]{2,1,0:T(8,128)S(1)}, u32[]{:S(2)}, u32[]{:S(2)}) %collective-permute-start) | collective-permute-done | bytes 262176 | tf_op jit(solution)/shard_map/while/body/eval_jaxpr/ppermute | solution.py:32
  310.2 14.6 %collective-permute-done = f32[8,64,128]{2,1,0:T(8,128)S(1)} collective-permute-done((f32[8,64,128]{2,1,0:T(8,128)S(1)}, f32[8,64,128]{2,1,0:T(8,128)S(1)}, u32[]{:S(2)}, u32[]{:S(2)}) %collective-permute-start) | collective-permute-done | bytes 262176 | tf_op jit(solution)/shard_map/while/body/eval_jaxpr/ppermute | solution.py:32
  327.4 16.2 %collective-permute-done = f32[8,64,128]{2,1,0:T(8,128)S(1)} collective-permute-done((f32[8,64,128]{2,1,0:T(8,128)S(1)}, f32[8,64,128]{2,1,0:T(8,128)S(1)}, u32[]{:S(2)}, u32[]{:S(2)}) %collective-permute-start) | collective-permute-done | bytes 262176 | tf_op jit(solution)/shard_map/while/body/eval_jaxpr/ppermute | solution.py:32
  346.3 18.6 %collective-permute-done = f32[8,64,128]{2,1,0:T(8,128)S(1)} collective-permute-done((f32[8,64,128]{2,1,0:T(8,128)S(1)}, f32[8,64,128]{2,1,0:T(8,128)S(1)}, u32[]{:S(2)}, u32[]{:S(2)}) %collective-permute-start) | collective-permute-done | bytes 262176 | tf_op jit(solution)/shard_map/while/body/eval_jaxpr/ppermute | solution.py:32
  367.5 15.1 %collective-permute-done = f32[8,64,128]{2,1,0:T(8,128)S(1)} collective-permute-done((f32[8,64,128]{2,1,0:T(8,128)S(1)}, f32[8,64,128]{2,1,0:T(8,128)S(1)}, u32[]{:S(2)}, u32[]{:S(2)}) %collective-permute-start) | collective-permute-done | bytes 262176 | tf_op jit(solution)/shard_map/while/body/eval_jaxpr/ppermute | solution.py:32
  385.3 18.3 %collective-permute-done = f32[8,64,128]{2,1,0:T(8,128)S(1)} collective-permute-done((f32[8,64,128]{2,1,0:T(8,128)S(1)}, f32[8,64,128]{2,1,0:T(8,128)S(1)}, u32[]{:S(2)}, u32[]{:S(2)}) %collective-permute-start) | collective-permute-done | bytes 262176 | tf_op jit(solution)/shard_map/while/body/eval_jaxpr/ppermute | solution.py:32
  406.3 15.8 %collective-permute-done = f32[8,64,128]{2,1,0:T(8,128)S(1)} collective-permute-done((f32[8,64,128]{2,1,0:T(8,128)S(1)}, f32[8,64,128]{2,1,0:T(8,128)S(1)}, u32[]{:S(2)}, u32[]{:S(2)}) %collective-permute-start) | collective-permute-done | bytes 262176 | tf_op jit(solution)/shard_map/while/body/eval_jaxpr/ppermute | solution.py:32
  424.7 14.6 %collective-permute-done = f32[8,64,128]{2,1,0:T(8,128)S(1)} collective-permute-done((f32[8,64,128]{2,1,0:T(8,128)S(1)}, f32[8,64,128]{2,1,0:T(8,128)S(1)}, u32[]{:S(2)}, u32[]{:S(2)}) %collective-permute-start) | collective-permute-done | bytes 262176 | tf_op jit(solution)/shard_map/while/body/eval_jaxpr/ppermute | solution.py:32
  442.0 13.5 %collective-permute-done = f32[8,64,128]{2,1,0:T(8,128)S(1)} collective-permute-done((f32[8,64,128]{2,1,0:T(8,128)S(1)}, f32[8,64,128]{2,1,0:T(8,128)S(1)}, u32[]{:S(2)}, u32[]{:S(2)}) %collective-permute-start) | collective-permute-done | bytes 262176 | tf_op jit(solution)/shard_map/while/body/eval_jaxpr/ppermute | solution.py:32
  458.1 13.1 %collective-permute-done = f32[8,64,128]{2,1,0:T(8,128)S(1)} collective-permute-done((f32[8,64,128]{2,1,0:T(8,128)S(1)}, f32[8,64,128]{2,1,0:T(8,128)S(1)}, u32[]{:S(2)}, u32[]{:S(2)}) %collective-permute-start) | collective-permute-done | bytes 262176 | tf_op jit(solution)/shard_map/while/body/eval_jaxpr/ppermute | solution.py:32
  473.9 15.9 %collective-permute-done = f32[8,64,128]{2,1,0:T(8,128)S(1)} collective-permute-done((f32[8,64,128]{2,1,0:T(8,128)S(1)}, f32[8,64,128]{2,1,0:T(8,128)S(1)}, u32[]{:S(2)}, u32[]{:S(2)}) %collective-permute-start) | collective-permute-done | bytes 262176 | tf_op jit(solution)/shard_map/while/body/eval_jaxpr/ppermute | solution.py:32
  492.5 15.4 %collective-permute-done = f32[8,64,128]{2,1,0:T(8,128)S(1)} collective-permute-done((f32[8,64,128]{2,1,0:T(8,128)S(1)}, f32[8,64,128]{2,1,0:T(8,128)S(1)}, u32[]{:S(2)}, u32[]{:S(2)}) %collective-permute-start) | collective-permute-done | bytes 262176 | tf_op jit(solution)/shard_map/while/body/eval_jaxpr/ppermute | solution.py:32
  510.6 17.3 %collective-permute-done = f32[8,64,128]{2,1,0:T(8,128)S(1)} collective-permute-done((f32[8,64,128]{2,1,0:T(8,128)S(1)}, f32[8,64,128]{2,1,0:T(8,128)S(1)}, u32[]{:S(2)}, u32[]{:S(2)}) %collective-permute-start) | collective-permute-done | bytes 262176 | tf_op jit(solution)/shard_map/while/body/eval_jaxpr/ppermute | solution.py:32
  530.5 19.2 %collective-permute-done = f32[8,64,128]{2,1,0:T(8,128)S(1)} collective-permute-done((f32[8,64,128]{2,1,0:T(8,128)S(1)}, f32[8,64,128]{2,1,0:T(8,128)S(1)}, u32[]{:S(2)}, u32[]{:S(2)}) %collective-permute-start) | collective-permute-done | bytes 262176 | tf_op jit(solution)/shard_map/while/body/eval_jaxpr/ppermute | solution.py:32
  552.4 19.4 %collective-permute-done = f32[8,64,128]{2,1,0:T(8,128)S(1)} collective-permute-done((f32[8,64,128]{2,1,0:T(8,128)S(1)}, f32[8,64,128]{2,1,0:T(8,128)S(1)}, u32[]{:S(2)}, u32[]{:S(2)}) %collective-permute-start) | collective-permute-done | bytes 262176 | tf_op jit(solution)/shard_map/while/body/eval_jaxpr/ppermute | solution.py:32
  574.4 16.1 %collective-permute-done = f32[8,64,128]{2,1,0:T(8,128)S(1)} collective-permute-done((f32[8,64,128]{2,1,0:T(8,128)S(1)}, f32[8,64,128]{2,1,0:T(8,128)S(1)}, u32[]{:S(2)}, u32[]{:S(2)}) %collective-permute-start) | collective-permute-done | bytes 262176 | tf_op jit(solution)/shard_map/while/body/eval_jaxpr/ppermute | solution.py:32
  593.1 18.6 %collective-permute-done = f32[8,64,128]{2,1,0:T(8,128)S(1)} collective-permute-done((f32[8,64,128]{2,1,0:T(8,128)S(1)}, f32[8,64,128]{2,1,0:T(8,128)S(1)}, u32[]{:S(2)}, u32[]{:S(2)}) %collective-permute-start) | collective-permute-done | bytes 262176 | tf_op jit(solution)/shard_map/while/body/eval_jaxpr/ppermute | solution.py:32
  614.4 15.7 %collective-permute-done = f32[8,64,128]{2,1,0:T(8,128)S(1)} collective-permute-done((f32[8,64,128]{2,1,0:T(8,128)S(1)}, f32[8,64,128]{2,1,0:T(8,128)S(1)}, u32[]{:S(2)}, u32[]{:S(2)}) %collective-permute-start) | collective-permute-done | bytes 262176 | tf_op jit(solution)/shard_map/while/body/eval_jaxpr/ppermute | solution.py:32
  632.7 14.6 %collective-permute-done = f32[8,64,128]{2,1,0:T(8,128)S(1)} collective-permute-done((f32[8,64,128]{2,1,0:T(8,128)S(1)}, f32[8,64,128]{2,1,0:T(8,128)S(1)}, u32[]{:S(2)}, u32[]{:S(2)}) %collective-permute-start) | collective-permute-done | bytes 262176 | tf_op jit(solution)/shard_map/while/body/eval_jaxpr/ppermute | solution.py:32
  649.9 16.4 %collective-permute-done = f32[8,64,128]{2,1,0:T(8,128)S(1)} collective-permute-done((f32[8,64,128]{2,1,0:T(8,128)S(1)}, f32[8,64,128]{2,1,0:T(8,128)S(1)}, u32[]{:S(2)}, u32[]{:S(2)}) %collective-permute-start) | collective-permute-done | bytes 262176 | tf_op jit(solution)/shard_map/while/body/eval_jaxpr/ppermute | solution.py:32
  669.0 15.5 %collective-permute-done = f32[8,64,128]{2,1,0:T(8,128)S(1)} collective-permute-done((f32[8,64,128]{2,1,0:T(8,128)S(1)}, f32[8,64,128]{2,1,0:T(8,128)S(1)}, u32[]{:S(2)}, u32[]{:S(2)}) %collective-permute-start) | collective-permute-done | bytes 262176 | tf_op jit(solution)/shard_map/while/body/eval_jaxpr/ppermute | solution.py:32
  717.9 14.0 %collective-permute-done = f32[8,64,128]{2,1,0:T(8,128)S(1)} collective-permute-done((f32[8,64,128]{2,1,0:T(8,128)S(1)}, f32[8,64,128]{2,1,0:T(8,128)S(1)}, u32[]{:S(2)}, u32[]{:S(2)}) %collective-permute-start) | collective-permute-done | bytes 262176 | tf_op jit(solution)/shard_map/while/body/eval_jaxpr/ppermute | solution.py:32
  734.6 14.4 %collective-permute-done = f32[8,64,128]{2,1,0:T(8,128)S(1)} collective-permute-done((f32[8,64,128]{2,1,0:T(8,128)S(1)}, f32[8,64,128]{2,1,0:T(8,128)S(1)}, u32[]{:S(2)}, u32[]{:S(2)}) %collective-permute-start) | collective-permute-done | bytes 262176 | tf_op jit(solution)/shard_map/while/body/eval_jaxpr/ppermute | solution.py:32
  751.7 13.9 %collective-permute-done = f32[8,64,128]{2,1,0:T(8,128)S(1)} collective-permute-done((f32[8,64,128]{2,1,0:T(8,128)S(1)}, f32[8,64,128]{2,1,0:T(8,128)S(1)}, u32[]{:S(2)}, u32[]{:S(2)}) %collective-permute-start) | collective-permute-done | bytes 262176 | tf_op jit(solution)/shard_map/while/body/eval_jaxpr/ppermute | solution.py:32
  845.5 13.3 %collective-permute-done = f32[8,64,128]{2,1,0:T(8,128)S(1)} collective-permute-done((f32[8,64,128]{2,1,0:T(8,128)S(1)}, f32[8,64,128]{2,1,0:T(8,128)S(1)}, u32[]{:S(2)}, u32[]{:S(2)}) %collective-permute-start) | collective-permute-done | bytes 262176 | tf_op jit(solution)/shard_map/while/body/eval_jaxpr/ppermute | solution.py:32
  861.4 15.0 %collective-permute-done = f32[8,64,128]{2,1,0:T(8,128)S(1)} collective-permute-done((f32[8,64,128]{2,1,0:T(8,128)S(1)}, f32[8,64,128]{2,1,0:T(8,128)S(1)}, u32[]{:S(2)}, u32[]{:S(2)}) %collective-permute-start) | collective-permute-done | bytes 262176 | tf_op jit(solution)/shard_map/while/body/eval_jaxpr/ppermute | solution.py:32
  879.0 15.4 %collective-permute-done = f32[8,64,128]{2,1,0:T(8,128)S(1)} collective-permute-done((f32[8,64,128]{2,1,0:T(8,128)S(1)}, f32[8,64,128]{2,1,0:T(8,128)S(1)}, u32[]{:S(2)}, u32[]{:S(2)}) %collective-permute-start) | collective-permute-done | bytes 262176 | tf_op jit(solution)/shard_map/while/body/eval_jaxpr/ppermute | solution.py:32
  897.1 17.2 %collective-permute-done = f32[8,64,128]{2,1,0:T(8,128)S(1)} collective-permute-done((f32[8,64,128]{2,1,0:T(8,128)S(1)}, f32[8,64,128]{2,1,0:T(8,128)S(1)}, u32[]{:S(2)}, u32[]{:S(2)}) %collective-permute-start) | collective-permute-done | bytes 262176 | tf_op jit(solution)/shard_map/while/body/eval_jaxpr/ppermute | solution.py:32
  917.0 17.2 %collective-permute-done = f32[8,64,128]{2,1,0:T(8,128)S(1)} collective-permute-done((f32[8,64,128]{2,1,0:T(8,128)S(1)}, f32[8,64,128]{2,1,0:T(8,128)S(1)}, u32[]{:S(2)}, u32[]{:S(2)}) %collective-permute-start) | collective-permute-done | bytes 262176 | tf_op jit(solution)/shard_map/while/body/eval_jaxpr/ppermute | solution.py:32
  936.9 17.5 %collective-permute-done = f32[8,64,128]{2,1,0:T(8,128)S(1)} collective-permute-done((f32[8,64,128]{2,1,0:T(8,128)S(1)}, f32[8,64,128]{2,1,0:T(8,128)S(1)}, u32[]{:S(2)}, u32[]{:S(2)}) %collective-permute-start) | collective-permute-done | bytes 262176 | tf_op jit(solution)/shard_map/while/body/eval_jaxpr/ppermute | solution.py:32
  957.0 16.1 %collective-permute-done = f32[8,64,128]{2,1,0:T(8,128)S(1)} collective-permute-done((f32[8,64,128]{2,1,0:T(8,128)S(1)}, f32[8,64,128]{2,1,0:T(8,128)S(1)}, u32[]{:S(2)}, u32[]{:S(2)}) %collective-permute-start) | collective-permute-done | bytes 262176 | tf_op jit(solution)/shard_map/while/body/eval_jaxpr/ppermute | solution.py:32
  975.9 14.6 %collective-permute-done = f32[8,64,128]{2,1,0:T(8,128)S(1)} collective-permute-done((f32[8,64,128]{2,1,0:T(8,128)S(1)}, f32[8,64,128]{2,1,0:T(8,128)S(1)}, u32[]{:S(2)}, u32[]{:S(2)}) %collective-permute-start) | collective-permute-done | bytes 262176 | tf_op jit(solution)/shard_map/while/body/eval_jaxpr/ppermute | solution.py:32
  993.1 14.2 %collective-permute-done = f32[8,64,128]{2,1,0:T(8,128)S(1)} collective-permute-done((f32[8,64,128]{2,1,0:T(8,128)S(1)}, f32[8,64,128]{2,1,0:T(8,128)S(1)}, u32[]{:S(2)}, u32[]{:S(2)}) %collective-permute-start) | collective-permute-done | bytes 262176 | tf_op jit(solution)/shard_map/while/body/eval_jaxpr/ppermute | solution.py:32
  1009.9 15.7 %collective-permute-done = f32[8,64,128]{2,1,0:T(8,128)S(1)} collective-permute-done((f32[8,64,128]{2,1,0:T(8,128)S(1)}, f32[8,64,128]{2,1,0:T(8,128)S(1)}, u32[]{:S(2)}, u32[]{:S(2)}) %collective-permute-start) | collective-permute-done | bytes 262176 | tf_op jit(solution)/shard_map/while/body/eval_jaxpr/ppermute | solution.py:32
  1028.2 14.9 %collective-permute-done = f32[8,64,128]{2,1,0:T(8,128)S(1)} collective-permute-done((f32[8,64,128]{2,1,0:T(8,128)S(1)}, f32[8,64,128]{2,1,0:T(8,128)S(1)}, u32[]{:S(2)}, u32[]{:S(2)}) %collective-permute-start) | collective-permute-done | bytes 262176 | tf_op jit(solution)/shard_map/while/body/eval_jaxpr/ppermute | solution.py:32
  1045.7 13.9 %collective-permute-done = f32[8,64,128]{2,1,0:T(8,128)S(1)} collective-permute-done((f32[8,64,128]{2,1,0:T(8,128)S(1)}, f32[8,64,128]{2,1,0:T(8,128)S(1)}, u32[]{:S(2)}, u32[]{:S(2)}) %collective-permute-start) | collective-permute-done | bytes 262176 | tf_op jit(solution)/shard_map/while/body/eval_jaxpr/ppermute | solution.py:32
  1194.2 27.8 %collective-permute-done.5 = f32[5,1,128,128]{3,2,1,0:T(8,128)S(1)} collective-permute-done((f32[5,1,128,128]{3,2,1,0:T(8,128)S(1)}, f32[5,1,128,128]{3,2,1,0:T(8,128)S(1)}, u32[]{:S(2)}, u32[]{:S(2)}) %collective-permute-start.5) | collective-permute-done | bytes 327712 | tf_op jit(solution)/shard_map/ppermute | solution.py:21
  (654 shorter events, 540.4 us)
Async XLA Ops:
  2.0 31.5 %collective-permute-start.1 = (f32[8,128,128]{2,1,0:T(8,128)}, f32[8,128,128]{2,1,0:T(8,128)}, u32[]{:S(2)}, u32[]{:S(2)}) collective-permute-start(f32[8,128,128]{2,1,0:T(8,128)} %get-tuple-element.158), channel_id=1, source_target_pairs={{0,4},{4,8},{8,12},{12,16},{16,20},{20,24},{24,28},{28,32},{32,36}... | collective-permute-start | bytes 1572872 | tf_op jit(solution)/shard_map/ppermute | solution.py:32
  68.0 22.4 %collective-permute-start = (f32[8,64,128]{2,1,0:T(8,128)S(1)}, f32[8,64,128]{2,1,0:T(8,128)S(1)}, u32[]{:S(2)}, u32[]{:S(2)}) collective-permute-start(f32[8,64,128]{2,1,0:T(8,128)S(1)} %get-tuple-element.293), channel_id=1, source_target_pairs={{0,4},{4,8},{8,12},{12,16},{16,20},{20,24},{24,28},{28,32},{32,36}... | collective-permute-start | bytes 786440 | tf_op jit(solution)/shard_map/while/body/eval_jaxpr/ppermute | solution.py:32
  91.1 19.7 %collective-permute-start = (f32[8,64,128]{2,1,0:T(8,128)S(1)}, f32[8,64,128]{2,1,0:T(8,128)S(1)}, u32[]{:S(2)}, u32[]{:S(2)}) collective-permute-start(f32[8,64,128]{2,1,0:T(8,128)S(1)} %get-tuple-element.293), channel_id=1, source_target_pairs={{0,4},{4,8},{8,12},{12,16},{16,20},{20,24},{24,28},{28,32},{32,36}... | collective-permute-start | bytes 786440 | tf_op jit(solution)/shard_map/while/body/eval_jaxpr/ppermute | solution.py:32
  111.6 17.0 %collective-permute-start = (f32[8,64,128]{2,1,0:T(8,128)S(1)}, f32[8,64,128]{2,1,0:T(8,128)S(1)}, u32[]{:S(2)}, u32[]{:S(2)}) collective-permute-start(f32[8,64,128]{2,1,0:T(8,128)S(1)} %get-tuple-element.293), channel_id=1, source_target_pairs={{0,4},{4,8},{8,12},{12,16},{16,20},{20,24},{24,28},{28,32},{32,36}... | collective-permute-start | bytes 786440 | tf_op jit(solution)/shard_map/while/body/eval_jaxpr/ppermute | solution.py:32
  129.4 18.3 %collective-permute-start = (f32[8,64,128]{2,1,0:T(8,128)S(1)}, f32[8,64,128]{2,1,0:T(8,128)S(1)}, u32[]{:S(2)}, u32[]{:S(2)}) collective-permute-start(f32[8,64,128]{2,1,0:T(8,128)S(1)} %get-tuple-element.293), channel_id=1, source_target_pairs={{0,4},{4,8},{8,12},{12,16},{16,20},{20,24},{24,28},{28,32},{32,36}... | collective-permute-start | bytes 786440 | tf_op jit(solution)/shard_map/while/body/eval_jaxpr/ppermute | solution.py:32
  148.4 20.9 %collective-permute-start = (f32[8,64,128]{2,1,0:T(8,128)S(1)}, f32[8,64,128]{2,1,0:T(8,128)S(1)}, u32[]{:S(2)}, u32[]{:S(2)}) collective-permute-start(f32[8,64,128]{2,1,0:T(8,128)S(1)} %get-tuple-element.293), channel_id=1, source_target_pairs={{0,4},{4,8},{8,12},{12,16},{16,20},{20,24},{24,28},{28,32},{32,36}... | collective-permute-start | bytes 786440 | tf_op jit(solution)/shard_map/while/body/eval_jaxpr/ppermute | solution.py:32
  170.0 19.0 %collective-permute-start = (f32[8,64,128]{2,1,0:T(8,128)S(1)}, f32[8,64,128]{2,1,0:T(8,128)S(1)}, u32[]{:S(2)}, u32[]{:S(2)}) collective-permute-start(f32[8,64,128]{2,1,0:T(8,128)S(1)} %get-tuple-element.293), channel_id=1, source_target_pairs={{0,4},{4,8},{8,12},{12,16},{16,20},{20,24},{24,28},{28,32},{32,36}... | collective-permute-start | bytes 786440 | tf_op jit(solution)/shard_map/while/body/eval_jaxpr/ppermute | solution.py:32
  189.7 19.3 %collective-permute-start = (f32[8,64,128]{2,1,0:T(8,128)S(1)}, f32[8,64,128]{2,1,0:T(8,128)S(1)}, u32[]{:S(2)}, u32[]{:S(2)}) collective-permute-start(f32[8,64,128]{2,1,0:T(8,128)S(1)} %get-tuple-element.293), channel_id=1, source_target_pairs={{0,4},{4,8},{8,12},{12,16},{16,20},{20,24},{24,28},{28,32},{32,36}... | collective-permute-start | bytes 786440 | tf_op jit(solution)/shard_map/while/body/eval_jaxpr/ppermute | solution.py:32
  209.7 19.0 %collective-permute-start = (f32[8,64,128]{2,1,0:T(8,128)S(1)}, f32[8,64,128]{2,1,0:T(8,128)S(1)}, u32[]{:S(2)}, u32[]{:S(2)}) collective-permute-start(f32[8,64,128]{2,1,0:T(8,128)S(1)} %get-tuple-element.293), channel_id=1, source_target_pairs={{0,4},{4,8},{8,12},{12,16},{16,20},{20,24},{24,28},{28,32},{32,36}... | collective-permute-start | bytes 786440 | tf_op jit(solution)/shard_map/while/body/eval_jaxpr/ppermute | solution.py:32
  229.5 15.8 %collective-permute-start = (f32[8,64,128]{2,1,0:T(8,128)S(1)}, f32[8,64,128]{2,1,0:T(8,128)S(1)}, u32[]{:S(2)}, u32[]{:S(2)}) collective-permute-start(f32[8,64,128]{2,1,0:T(8,128)S(1)} %get-tuple-element.293), channel_id=1, source_target_pairs={{0,4},{4,8},{8,12},{12,16},{16,20},{20,24},{24,28},{28,32},{32,36}... | collective-permute-start | bytes 786440 | tf_op jit(solution)/shard_map/while/body/eval_jaxpr/ppermute | solution.py:32
  246.0 15.6 %collective-permute-start = (f32[8,64,128]{2,1,0:T(8,128)S(1)}, f32[8,64,128]{2,1,0:T(8,128)S(1)}, u32[]{:S(2)}, u32[]{:S(2)}) collective-permute-start(f32[8,64,128]{2,1,0:T(8,128)S(1)} %get-tuple-element.293), channel_id=1, source_target_pairs={{0,4},{4,8},{8,12},{12,16},{16,20},{20,24},{24,28},{28,32},{32,36}... | collective-permute-start | bytes 786440 | tf_op jit(solution)/shard_map/while/body/eval_jaxpr/ppermute | solution.py:32
  308.3 16.5 %collective-permute-start = (f32[8,64,128]{2,1,0:T(8,128)S(1)}, f32[8,64,128]{2,1,0:T(8,128)S(1)}, u32[]{:S(2)}, u32[]{:S(2)}) collective-permute-start(f32[8,64,128]{2,1,0:T(8,128)S(1)} %get-tuple-element.293), channel_id=1, source_target_pairs={{0,4},{4,8},{8,12},{12,16},{16,20},{20,24},{24,28},{28,32},{32,36}... | collective-permute-start | bytes 786440 | tf_op jit(solution)/shard_map/while/body/eval_jaxpr/ppermute | solution.py:32
  325.5 18.1 %collective-permute-start = (f32[8,64,128]{2,1,0:T(8,128)S(1)}, f32[8,64,128]{2,1,0:T(8,128)S(1)}, u32[]{:S(2)}, u32[]{:S(2)}) collective-permute-start(f32[8,64,128]{2,1,0:T(8,128)S(1)} %get-tuple-element.293), channel_id=1, source_target_pairs={{0,4},{4,8},{8,12},{12,16},{16,20},{20,24},{24,28},{28,32},{32,36}... | collective-permute-start | bytes 786440 | tf_op jit(solution)/shard_map/while/body/eval_jaxpr/ppermute | solution.py:32
  344.4 20.5 %collective-permute-start = (f32[8,64,128]{2,1,0:T(8,128)S(1)}, f32[8,64,128]{2,1,0:T(8,128)S(1)}, u32[]{:S(2)}, u32[]{:S(2)}) collective-permute-start(f32[8,64,128]{2,1,0:T(8,128)S(1)} %get-tuple-element.293), channel_id=1, source_target_pairs={{0,4},{4,8},{8,12},{12,16},{16,20},{20,24},{24,28},{28,32},{32,36}... | collective-permute-start | bytes 786440 | tf_op jit(solution)/shard_map/while/body/eval_jaxpr/ppermute | solution.py:32
  365.6 17.0 %collective-permute-start = (f32[8,64,128]{2,1,0:T(8,128)S(1)}, f32[8,64,128]{2,1,0:T(8,128)S(1)}, u32[]{:S(2)}, u32[]{:S(2)}) collective-permute-start(f32[8,64,128]{2,1,0:T(8,128)S(1)} %get-tuple-element.293), channel_id=1, source_target_pairs={{0,4},{4,8},{8,12},{12,16},{16,20},{20,24},{24,28},{28,32},{32,36}... | collective-permute-start | bytes 786440 | tf_op jit(solution)/shard_map/while/body/eval_jaxpr/ppermute | solution.py:32
  383.4 20.3 %collective-permute-start = (f32[8,64,128]{2,1,0:T(8,128)S(1)}, f32[8,64,128]{2,1,0:T(8,128)S(1)}, u32[]{:S(2)}, u32[]{:S(2)}) collective-permute-start(f32[8,64,128]{2,1,0:T(8,128)S(1)} %get-tuple-element.293), channel_id=1, source_target_pairs={{0,4},{4,8},{8,12},{12,16},{16,20},{20,24},{24,28},{28,32},{32,36}... | collective-permute-start | bytes 786440 | tf_op jit(solution)/shard_map/while/body/eval_jaxpr/ppermute | solution.py:32
  404.4 17.7 %collective-permute-start = (f32[8,64,128]{2,1,0:T(8,128)S(1)}, f32[8,64,128]{2,1,0:T(8,128)S(1)}, u32[]{:S(2)}, u32[]{:S(2)}) collective-permute-start(f32[8,64,128]{2,1,0:T(8,128)S(1)} %get-tuple-element.293), channel_id=1, source_target_pairs={{0,4},{4,8},{8,12},{12,16},{16,20},{20,24},{24,28},{28,32},{32,36}... | collective-permute-start | bytes 786440 | tf_op jit(solution)/shard_map/while/body/eval_jaxpr/ppermute | solution.py:32
  422.8 16.5 %collective-permute-start = (f32[8,64,128]{2,1,0:T(8,128)S(1)}, f32[8,64,128]{2,1,0:T(8,128)S(1)}, u32[]{:S(2)}, u32[]{:S(2)}) collective-permute-start(f32[8,64,128]{2,1,0:T(8,128)S(1)} %get-tuple-element.293), channel_id=1, source_target_pairs={{0,4},{4,8},{8,12},{12,16},{16,20},{20,24},{24,28},{28,32},{32,36}... | collective-permute-start | bytes 786440 | tf_op jit(solution)/shard_map/while/body/eval_jaxpr/ppermute | solution.py:32
  440.0 15.4 %collective-permute-start = (f32[8,64,128]{2,1,0:T(8,128)S(1)}, f32[8,64,128]{2,1,0:T(8,128)S(1)}, u32[]{:S(2)}, u32[]{:S(2)}) collective-permute-start(f32[8,64,128]{2,1,0:T(8,128)S(1)} %get-tuple-element.293), channel_id=1, source_target_pairs={{0,4},{4,8},{8,12},{12,16},{16,20},{20,24},{24,28},{28,32},{32,36}... | collective-permute-start | bytes 786440 | tf_op jit(solution)/shard_map/while/body/eval_jaxpr/ppermute | solution.py:32
  456.2 15.0 %collective-permute-start = (f32[8,64,128]{2,1,0:T(8,128)S(1)}, f32[8,64,128]{2,1,0:T(8,128)S(1)}, u32[]{:S(2)}, u32[]{:S(2)}) collective-permute-start(f32[8,64,128]{2,1,0:T(8,128)S(1)} %get-tuple-element.293), channel_id=1, source_target_pairs={{0,4},{4,8},{8,12},{12,16},{16,20},{20,24},{24,28},{28,32},{32,36}... | collective-permute-start | bytes 786440 | tf_op jit(solution)/shard_map/while/body/eval_jaxpr/ppermute | solution.py:32
  472.0 17.8 %collective-permute-start = (f32[8,64,128]{2,1,0:T(8,128)S(1)}, f32[8,64,128]{2,1,0:T(8,128)S(1)}, u32[]{:S(2)}, u32[]{:S(2)}) collective-permute-start(f32[8,64,128]{2,1,0:T(8,128)S(1)} %get-tuple-element.293), channel_id=1, source_target_pairs={{0,4},{4,8},{8,12},{12,16},{16,20},{20,24},{24,28},{28,32},{32,36}... | collective-permute-start | bytes 786440 | tf_op jit(solution)/shard_map/while/body/eval_jaxpr/ppermute | solution.py:32
  490.5 17.4 %collective-permute-start = (f32[8,64,128]{2,1,0:T(8,128)S(1)}, f32[8,64,128]{2,1,0:T(8,128)S(1)}, u32[]{:S(2)}, u32[]{:S(2)}) collective-permute-start(f32[8,64,128]{2,1,0:T(8,128)S(1)} %get-tuple-element.293), channel_id=1, source_target_pairs={{0,4},{4,8},{8,12},{12,16},{16,20},{20,24},{24,28},{28,32},{32,36}... | collective-permute-start | bytes 786440 | tf_op jit(solution)/shard_map/while/body/eval_jaxpr/ppermute | solution.py:32
  508.6 19.2 %collective-permute-start = (f32[8,64,128]{2,1,0:T(8,128)S(1)}, f32[8,64,128]{2,1,0:T(8,128)S(1)}, u32[]{:S(2)}, u32[]{:S(2)}) collective-permute-start(f32[8,64,128]{2,1,0:T(8,128)S(1)} %get-tuple-element.293), channel_id=1, source_target_pairs={{0,4},{4,8},{8,12},{12,16},{16,20},{20,24},{24,28},{28,32},{32,36}... | collective-permute-start | bytes 786440 | tf_op jit(solution)/shard_map/while/body/eval_jaxpr/ppermute | solution.py:32
  528.6 21.1 %collective-permute-start = (f32[8,64,128]{2,1,0:T(8,128)S(1)}, f32[8,64,128]{2,1,0:T(8,128)S(1)}, u32[]{:S(2)}, u32[]{:S(2)}) collective-permute-start(f32[8,64,128]{2,1,0:T(8,128)S(1)} %get-tuple-element.293), channel_id=1, source_target_pairs={{0,4},{4,8},{8,12},{12,16},{16,20},{20,24},{24,28},{28,32},{32,36}... | collective-permute-start | bytes 786440 | tf_op jit(solution)/shard_map/while/body/eval_jaxpr/ppermute | solution.py:32
  550.4 21.3 %collective-permute-start = (f32[8,64,128]{2,1,0:T(8,128)S(1)}, f32[8,64,128]{2,1,0:T(8,128)S(1)}, u32[]{:S(2)}, u32[]{:S(2)}) collective-permute-start(f32[8,64,128]{2,1,0:T(8,128)S(1)} %get-tuple-element.293), channel_id=1, source_target_pairs={{0,4},{4,8},{8,12},{12,16},{16,20},{20,24},{24,28},{28,32},{32,36}... | collective-permute-start | bytes 786440 | tf_op jit(solution)/shard_map/while/body/eval_jaxpr/ppermute | solution.py:32
  572.5 18.0 %collective-permute-start = (f32[8,64,128]{2,1,0:T(8,128)S(1)}, f32[8,64,128]{2,1,0:T(8,128)S(1)}, u32[]{:S(2)}, u32[]{:S(2)}) collective-permute-start(f32[8,64,128]{2,1,0:T(8,128)S(1)} %get-tuple-element.293), channel_id=1, source_target_pairs={{0,4},{4,8},{8,12},{12,16},{16,20},{20,24},{24,28},{28,32},{32,36}... | collective-permute-start | bytes 786440 | tf_op jit(solution)/shard_map/while/body/eval_jaxpr/ppermute | solution.py:32
  591.2 20.5 %collective-permute-start = (f32[8,64,128]{2,1,0:T(8,128)S(1)}, f32[8,64,128]{2,1,0:T(8,128)S(1)}, u32[]{:S(2)}, u32[]{:S(2)}) collective-permute-start(f32[8,64,128]{2,1,0:T(8,128)S(1)} %get-tuple-element.293), channel_id=1, source_target_pairs={{0,4},{4,8},{8,12},{12,16},{16,20},{20,24},{24,28},{28,32},{32,36}... | collective-permute-start | bytes 786440 | tf_op jit(solution)/shard_map/while/body/eval_jaxpr/ppermute | solution.py:32
  612.5 17.6 %collective-permute-start = (f32[8,64,128]{2,1,0:T(8,128)S(1)}, f32[8,64,128]{2,1,0:T(8,128)S(1)}, u32[]{:S(2)}, u32[]{:S(2)}) collective-permute-start(f32[8,64,128]{2,1,0:T(8,128)S(1)} %get-tuple-element.293), channel_id=1, source_target_pairs={{0,4},{4,8},{8,12},{12,16},{16,20},{20,24},{24,28},{28,32},{32,36}... | collective-permute-start | bytes 786440 | tf_op jit(solution)/shard_map/while/body/eval_jaxpr/ppermute | solution.py:32
  630.8 16.5 %collective-permute-start = (f32[8,64,128]{2,1,0:T(8,128)S(1)}, f32[8,64,128]{2,1,0:T(8,128)S(1)}, u32[]{:S(2)}, u32[]{:S(2)}) collective-permute-start(f32[8,64,128]{2,1,0:T(8,128)S(1)} %get-tuple-element.293), channel_id=1, source_target_pairs={{0,4},{4,8},{8,12},{12,16},{16,20},{20,24},{24,28},{28,32},{32,36}... | collective-permute-start | bytes 786440 | tf_op jit(solution)/shard_map/while/body/eval_jaxpr/ppermute | solution.py:32
  648.0 18.4 %collective-permute-start = (f32[8,64,128]{2,1,0:T(8,128)S(1)}, f32[8,64,128]{2,1,0:T(8,128)S(1)}, u32[]{:S(2)}, u32[]{:S(2)}) collective-permute-start(f32[8,64,128]{2,1,0:T(8,128)S(1)} %get-tuple-element.293), channel_id=1, source_target_pairs={{0,4},{4,8},{8,12},{12,16},{16,20},{20,24},{24,28},{28,32},{32,36}... | collective-permute-start | bytes 786440 | tf_op jit(solution)/shard_map/while/body/eval_jaxpr/ppermute | solution.py:32
  667.1 17.4 %collective-permute-start = (f32[8,64,128]{2,1,0:T(8,128)S(1)}, f32[8,64,128]{2,1,0:T(8,128)S(1)}, u32[]{:S(2)}, u32[]{:S(2)}) collective-permute-start(f32[8,64,128]{2,1,0:T(8,128)S(1)} %get-tuple-element.293), channel_id=1, source_target_pairs={{0,4},{4,8},{8,12},{12,16},{16,20},{20,24},{24,28},{28,32},{32,36}... | collective-permute-start | bytes 786440 | tf_op jit(solution)/shard_map/while/body/eval_jaxpr/ppermute | solution.py:32
  716.0 16.0 %collective-permute-start = (f32[8,64,128]{2,1,0:T(8,128)S(1)}, f32[8,64,128]{2,1,0:T(8,128)S(1)}, u32[]{:S(2)}, u32[]{:S(2)}) collective-permute-start(f32[8,64,128]{2,1,0:T(8,128)S(1)} %get-tuple-element.293), channel_id=1, source_target_pairs={{0,4},{4,8},{8,12},{12,16},{16,20},{20,24},{24,28},{28,32},{32,36}... | collective-permute-start | bytes 786440 | tf_op jit(solution)/shard_map/while/body/eval_jaxpr/ppermute | solution.py:32
  732.7 16.4 %collective-permute-start = (f32[8,64,128]{2,1,0:T(8,128)S(1)}, f32[8,64,128]{2,1,0:T(8,128)S(1)}, u32[]{:S(2)}, u32[]{:S(2)}) collective-permute-start(f32[8,64,128]{2,1,0:T(8,128)S(1)} %get-tuple-element.293), channel_id=1, source_target_pairs={{0,4},{4,8},{8,12},{12,16},{16,20},{20,24},{24,28},{28,32},{32,36}... | collective-permute-start | bytes 786440 | tf_op jit(solution)/shard_map/while/body/eval_jaxpr/ppermute | solution.py:32
  749.8 15.8 %collective-permute-start = (f32[8,64,128]{2,1,0:T(8,128)S(1)}, f32[8,64,128]{2,1,0:T(8,128)S(1)}, u32[]{:S(2)}, u32[]{:S(2)}) collective-permute-start(f32[8,64,128]{2,1,0:T(8,128)S(1)} %get-tuple-element.293), channel_id=1, source_target_pairs={{0,4},{4,8},{8,12},{12,16},{16,20},{20,24},{24,28},{28,32},{32,36}... | collective-permute-start | bytes 786440 | tf_op jit(solution)/shard_map/while/body/eval_jaxpr/ppermute | solution.py:32
  843.5 15.2 %collective-permute-start = (f32[8,64,128]{2,1,0:T(8,128)S(1)}, f32[8,64,128]{2,1,0:T(8,128)S(1)}, u32[]{:S(2)}, u32[]{:S(2)}) collective-permute-start(f32[8,64,128]{2,1,0:T(8,128)S(1)} %get-tuple-element.293), channel_id=1, source_target_pairs={{0,4},{4,8},{8,12},{12,16},{16,20},{20,24},{24,28},{28,32},{32,36}... | collective-permute-start | bytes 786440 | tf_op jit(solution)/shard_map/while/body/eval_jaxpr/ppermute | solution.py:32
  859.5 16.9 %collective-permute-start = (f32[8,64,128]{2,1,0:T(8,128)S(1)}, f32[8,64,128]{2,1,0:T(8,128)S(1)}, u32[]{:S(2)}, u32[]{:S(2)}) collective-permute-start(f32[8,64,128]{2,1,0:T(8,128)S(1)} %get-tuple-element.293), channel_id=1, source_target_pairs={{0,4},{4,8},{8,12},{12,16},{16,20},{20,24},{24,28},{28,32},{32,36}... | collective-permute-start | bytes 786440 | tf_op jit(solution)/shard_map/while/body/eval_jaxpr/ppermute | solution.py:32
  877.1 17.4 %collective-permute-start = (f32[8,64,128]{2,1,0:T(8,128)S(1)}, f32[8,64,128]{2,1,0:T(8,128)S(1)}, u32[]{:S(2)}, u32[]{:S(2)}) collective-permute-start(f32[8,64,128]{2,1,0:T(8,128)S(1)} %get-tuple-element.293), channel_id=1, source_target_pairs={{0,4},{4,8},{8,12},{12,16},{16,20},{20,24},{24,28},{28,32},{32,36}... | collective-permute-start | bytes 786440 | tf_op jit(solution)/shard_map/while/body/eval_jaxpr/ppermute | solution.py:32
  895.2 19.1 %collective-permute-start = (f32[8,64,128]{2,1,0:T(8,128)S(1)}, f32[8,64,128]{2,1,0:T(8,128)S(1)}, u32[]{:S(2)}, u32[]{:S(2)}) collective-permute-start(f32[8,64,128]{2,1,0:T(8,128)S(1)} %get-tuple-element.293), channel_id=1, source_target_pairs={{0,4},{4,8},{8,12},{12,16},{16,20},{20,24},{24,28},{28,32},{32,36}... | collective-permute-start | bytes 786440 | tf_op jit(solution)/shard_map/while/body/eval_jaxpr/ppermute | solution.py:32
  915.0 19.1 %collective-permute-start = (f32[8,64,128]{2,1,0:T(8,128)S(1)}, f32[8,64,128]{2,1,0:T(8,128)S(1)}, u32[]{:S(2)}, u32[]{:S(2)}) collective-permute-start(f32[8,64,128]{2,1,0:T(8,128)S(1)} %get-tuple-element.293), channel_id=1, source_target_pairs={{0,4},{4,8},{8,12},{12,16},{16,20},{20,24},{24,28},{28,32},{32,36}... | collective-permute-start | bytes 786440 | tf_op jit(solution)/shard_map/while/body/eval_jaxpr/ppermute | solution.py:32
  934.9 19.5 %collective-permute-start = (f32[8,64,128]{2,1,0:T(8,128)S(1)}, f32[8,64,128]{2,1,0:T(8,128)S(1)}, u32[]{:S(2)}, u32[]{:S(2)}) collective-permute-start(f32[8,64,128]{2,1,0:T(8,128)S(1)} %get-tuple-element.293), channel_id=1, source_target_pairs={{0,4},{4,8},{8,12},{12,16},{16,20},{20,24},{24,28},{28,32},{32,36}... | collective-permute-start | bytes 786440 | tf_op jit(solution)/shard_map/while/body/eval_jaxpr/ppermute | solution.py:32
  955.1 18.1 %collective-permute-start = (f32[8,64,128]{2,1,0:T(8,128)S(1)}, f32[8,64,128]{2,1,0:T(8,128)S(1)}, u32[]{:S(2)}, u32[]{:S(2)}) collective-permute-start(f32[8,64,128]{2,1,0:T(8,128)S(1)} %get-tuple-element.293), channel_id=1, source_target_pairs={{0,4},{4,8},{8,12},{12,16},{16,20},{20,24},{24,28},{28,32},{32,36}... | collective-permute-start | bytes 786440 | tf_op jit(solution)/shard_map/while/body/eval_jaxpr/ppermute | solution.py:32
  973.9 16.5 %collective-permute-start = (f32[8,64,128]{2,1,0:T(8,128)S(1)}, f32[8,64,128]{2,1,0:T(8,128)S(1)}, u32[]{:S(2)}, u32[]{:S(2)}) collective-permute-start(f32[8,64,128]{2,1,0:T(8,128)S(1)} %get-tuple-element.293), channel_id=1, source_target_pairs={{0,4},{4,8},{8,12},{12,16},{16,20},{20,24},{24,28},{28,32},{32,36}... | collective-permute-start | bytes 786440 | tf_op jit(solution)/shard_map/while/body/eval_jaxpr/ppermute | solution.py:32
  991.1 16.1 %collective-permute-start = (f32[8,64,128]{2,1,0:T(8,128)S(1)}, f32[8,64,128]{2,1,0:T(8,128)S(1)}, u32[]{:S(2)}, u32[]{:S(2)}) collective-permute-start(f32[8,64,128]{2,1,0:T(8,128)S(1)} %get-tuple-element.293), channel_id=1, source_target_pairs={{0,4},{4,8},{8,12},{12,16},{16,20},{20,24},{24,28},{28,32},{32,36}... | collective-permute-start | bytes 786440 | tf_op jit(solution)/shard_map/while/body/eval_jaxpr/ppermute | solution.py:32
  1008.0 17.6 %collective-permute-start = (f32[8,64,128]{2,1,0:T(8,128)S(1)}, f32[8,64,128]{2,1,0:T(8,128)S(1)}, u32[]{:S(2)}, u32[]{:S(2)}) collective-permute-start(f32[8,64,128]{2,1,0:T(8,128)S(1)} %get-tuple-element.293), channel_id=1, source_target_pairs={{0,4},{4,8},{8,12},{12,16},{16,20},{20,24},{24,28},{28,32},{32,36}... | collective-permute-start | bytes 786440 | tf_op jit(solution)/shard_map/while/body/eval_jaxpr/ppermute | solution.py:32
  1026.3 16.8 %collective-permute-start = (f32[8,64,128]{2,1,0:T(8,128)S(1)}, f32[8,64,128]{2,1,0:T(8,128)S(1)}, u32[]{:S(2)}, u32[]{:S(2)}) collective-permute-start(f32[8,64,128]{2,1,0:T(8,128)S(1)} %get-tuple-element.293), channel_id=1, source_target_pairs={{0,4},{4,8},{8,12},{12,16},{16,20},{20,24},{24,28},{28,32},{32,36}... | collective-permute-start | bytes 786440 | tf_op jit(solution)/shard_map/while/body/eval_jaxpr/ppermute | solution.py:32
  1043.8 15.8 %collective-permute-start = (f32[8,64,128]{2,1,0:T(8,128)S(1)}, f32[8,64,128]{2,1,0:T(8,128)S(1)}, u32[]{:S(2)}, u32[]{:S(2)}) collective-permute-start(f32[8,64,128]{2,1,0:T(8,128)S(1)} %get-tuple-element.293), channel_id=1, source_target_pairs={{0,4},{4,8},{8,12},{12,16},{16,20},{20,24},{24,28},{28,32},{32,36}... | collective-permute-start | bytes 786440 | tf_op jit(solution)/shard_map/while/body/eval_jaxpr/ppermute | solution.py:32
  1060.3 14.9 %collective-permute-start = (f32[8,64,128]{2,1,0:T(8,128)S(1)}, f32[8,64,128]{2,1,0:T(8,128)S(1)}, u32[]{:S(2)}, u32[]{:S(2)}) collective-permute-start(f32[8,64,128]{2,1,0:T(8,128)S(1)} %get-tuple-element.293), channel_id=1, source_target_pairs={{0,4},{4,8},{8,12},{12,16},{16,20},{20,24},{24,28},{28,32},{32,36}... | collective-permute-start | bytes 786440 | tf_op jit(solution)/shard_map/while/body/eval_jaxpr/ppermute | solution.py:32
  1189.6 32.3 %collective-permute-start.5 = (f32[5,1,128,128]{3,2,1,0:T(8,128)S(1)}, f32[5,1,128,128]{3,2,1,0:T(8,128)S(1)}, u32[]{:S(2)}, u32[]{:S(2)}) collective-permute-start(f32[5,1,128,128]{3,2,1,0:T(8,128)S(1)} %get-tuple-element.150), channel_id=1, source_target_pairs={{0,1},{1,2},{2,3},{4,5},{5,6},{6,7},{8,9},{9,10},{10,11},{12,13},{... | collective-permute-start | bytes 983048 | tf_op jit(solution)/shard_map/ppermute | solution.py:21
  (106 other events, 475.2 us)
where the time goes:
time: 1310 us; the launch traced here: 1300 us
  waiting for transfers between devices  1020 us (78%)
  starting transfers between devices  164 us (13%)
  other arithmetic  61.1 us (5%)
  local copies, waits for them, and re-layouts  37.3 us (3%)
  blocking collectives  19.4 us (1%)
    ppermute x64, waiting for transfers between devices, from_behind(): return lax.ppermute(value, axis, pairs)  962 us
    ppermute x64, starting transfers between devices, from_behind(): return lax.ppermute(value, axis, pairs)  124 us
    ppermute x9, waiting for transfers between devices, with_halo(): lax.ppermute(lax.slice_in_dim(block, block.shape[dim] - width, None, axis...  53.3 us
  transfers between devices with their start and end apart: 82, of which 75 were waited for; matrix products, arithmetic and copies ran while one was open for 1% of the time, Pallas kernels for 0%

commit v1 on v0

v1 whole, which is shorter than its diff:
```python
import functools
import math

import jax
import jax.numpy as jnp
import numpy as np
from jax import lax
from jax.experimental import pallas as pl
from jax.experimental.pallas import tpu as pltpu
from jax.sharding import Mesh
from jax.sharding import PartitionSpec as P

NODES = 5
STEPS = NODES - 1
F32 = jnp.float32
TM = ("zh", "y", "x")
MIB = 1 << 20


def node_tables():
    radius = math.sqrt(3.0 / 7.0)
    points = [0.0, (1.0 - radius) / 2.0, 0.5, (1.0 + radius) / 2.0, 1.0]
    integrals = np.zeros((4, 5))
    for column in range(5):
        coeffs = [1.0]
        divisor = 1.0
        for other in range(5):
            if other != column:
                anchor = points[other]
                product = [0.0] * (len(coeffs) + 1)
                for degree in range(len(coeffs)):
                    product[degree + 1] = product[degree + 1] + coeffs[degree]
                    product[degree] = product[degree] - anchor * coeffs[degree]
                coeffs = product
                divisor = divisor * (points[column] - anchor)
        for row in range(4):
            bottom = points[row]
            summit = points[row + 1]
            amount = 0.0
            for degree in range(len(coeffs)):
                amount = amount + coeffs[degree] / (degree + 1) * (
                    summit ** (degree + 1) - bottom ** (degree + 1)
                )
            integrals[row, column] = amount / divisor
    return (np.array(points), integrals)


TAU, Q = node_tables()
WEIGHTS = Q.sum(axis=0)
DT = TAU[1:] - TAU[:-1]


def kappa_of(labels, table):
    value = jnp.where(labels == 3, table[3], 0.0)
    for region in range(3):
        value = jnp.where(labels == region, table[region], value)
    return value


def rate(below, mid, above, kappa, advect):
    rows, cols = mid.shape
    lane = lax.broadcasted_iota(jnp.int32, (1, cols), 1)
    behind = pltpu.roll(mid, 1, 0)
    ahead = pltpu.roll(mid, rows - 1, 0)
    left = jnp.where(lane == 0, 0.0, pltpu.roll(mid, 1, 1))
    right = jnp.where(lane == cols - 1, 0.0, pltpu.roll(mid, cols - 1, 1))
    total = ((below + above) + (behind + ahead)) + (left + right)
    return kappa * (total - 6.0 * mid) - advect * (mid - behind)


def sums_kernel(info, nodes, sums, weighted):
    first = (info[0] == 0).astype(F32)
    for z in range(nodes.shape[2]):
        u = [nodes[0, j, z] for j in range(1, NODES)]
        for m in range(STEPS):
            coef = [float(Q[m, j]) for j in range(1, NODES)]
            if m > 0:
                coef[m - 1] -= float(DT[m])
            total = coef[0] * u[0]
            for j in range(1, STEPS):
                total = total + coef[j] * u[j]
            sums[m, z] = total
        total = float(WEIGHTS[1]) * u[0]
        for j in range(1, STEPS):
            total = total + float(WEIGHTS[j + 1]) * u[j]
        weighted[z] = total + (first * float(WEIGHTS[0])) * nodes[0, 0, z]


def node_sums(info, node_fields):
    _, _, nz, nx, ny = node_fields.shape
    cut = 2
    return pl.pallas_call(
        sums_kernel,
        grid_spec=pltpu.PrefetchScalarGridSpec(
            num_scalar_prefetch=1,
            grid=(nz // cut,),
            in_specs=[pl.BlockSpec((1, NODES, cut, nx, ny), lambda i, *_: (0, 0, i, 0, 0))],
            out_specs=[
                pl.BlockSpec((STEPS, cut, nx, ny), lambda i, *_: (0, i, 0, 0)),
                pl.BlockSpec((cut, nx, ny), lambda i, *_: (i, 0, 0)),
            ],
        ),
        out_shape=[
            jax.ShapeDtypeStruct((STEPS, nz, nx, ny), F32),
            jax.ShapeDtypeStruct((nz, nx, ny), F32),
        ],
        compiler_params=pltpu.CompilerParams(vmem_limit_bytes=16 * MIB),
        cost_estimate=pl.CostEstimate(flops=10_000_000, bytes_accessed=6_000_000, transcendentals=0),
        name="node_sums",
    )(info, node_fields)


def residual_kernel(
    info, table, weighted, arrived, u0, u4, labels, shift, w_low, w_high, s_low, s_high,
    coarse, start, wide, block,
):
    nz, nx, ny = weighted.shape
    first = info[0] == 0
    advect = shift[...].astype(F32)
    w0 = float(WEIGHTS[0])
    for z in range(nz):
        wide[z + 1] = weighted[z] + w0 * arrived[z]
    wide[0] = w_low[0] + w0 * s_low[0]
    wide[nz + 1] = w_high[0] + w0 * s_high[0]
    for zb in range(nz // 4):
        total = None
        ksum = None
        for k in range(4):
            z = 4 * zb + k
            kappa = kappa_of(labels[z], table)
            begin = jnp.where(first, u0[0, 0, z], arrived[z])
            start[z] = begin
            value = begin - u4[0, 0, z] + rate(wide[z], wide[z + 1], wide[z + 2], kappa, advect)
            total = value if total is None else total + value
            ksum = kappa if ksum is None else ksum + kappa
        block[0] = total
        block[1] = ksum
        for f in range(2):
            even = block[f, pl.ds(0, nx // 2, stride=2), :]
            odd = block[f, pl.ds(1, nx // 2, stride=2), :]
            coarse[f, zb] = (even + odd) * 0.125


def residual(info, table, weighted, arrived, node_fields, labels, shift, w_low, w_high, s_low, s_high):
    nz, nx, ny = weighted.shape
    full = pl.BlockSpec(memory_space=pltpu.VMEM)
    smem = pl.BlockSpec(memory_space=pltpu.SMEM)

    def node(j):
        return pl.BlockSpec((1, 1, nz, nx, ny), lambda i: (0, j, 0, 0, 0))

    def whole(shape):
        return pl.BlockSpec(shape, lambda i: (0,) * len(shape))

    return pl.pallas_call(
        residual_kernel,
        grid=(1,),
        in_specs=[
            smem, smem, whole((nz, nx, ny)), whole((nz, nx, ny)), node(0), node(NODES - 1),
            whole((nz, nx, ny)), whole((1, ny)),
            whole((1, nx, ny)), whole((1, nx, ny)), whole((1, nx, ny)), whole((1, nx, ny)),
        ],
        out_specs=[whole((2, nz // 4, nx // 2, ny)), whole((nz, nx, ny))],
        out_shape=[
            jax.ShapeDtypeStruct((2, nz // 4, nx // 2, ny), F32),
            jax.ShapeDtypeStruct((nz, nx, ny), F32),
        ],
        scratch_shapes=[pltpu.VMEM((nz + 2, nx, ny), F32), pltpu.VMEM((2, nx, ny), F32)],
        compiler_params=pltpu.CompilerParams(vmem_limit_bytes=16 * MIB),
        cost_estimate=pl.CostEstimate(flops=4_000_000, bytes_accessed=4_000_000, transcendentals=0),
        name="residual",
    )(info, table, weighted, arrived, node_fields, node_fields, labels, shift, w_low, w_high, s_low, s_high)


def coarse_step(src, dst, kappa, half):
    nx, nz, ny = kappa.shape
    lane = lax.broadcasted_iota(jnp.int32, (nz, ny), 1)
    sub = lax.broadcasted_iota(jnp.int32, (nz, ny), 0)
    past, mid = src[nx - 1], src[0]
    for x in range(nx):
        ahead = src[(x + 1) % nx]
        below = jnp.where(sub == 0, 0.0, pltpu.roll(mid, 1, 0))
        above = jnp.where(sub == nz - 1, 0.0, pltpu.roll(mid, nz - 1, 0))
        left = jnp.where(lane == 0, 0.0, pltpu.roll(mid, 1, 1))
        right = jnp.where(lane == ny - 1, 0.0, pltpu.roll(mid, ny - 1, 1))
        total = (below + above) * 0.0625 + (past + ahead) * 0.25 + ((left + right) - 2.625 * mid)
        dst[x] = mid + kappa[x] * total - half * (mid - past)
        past, mid = mid, ahead


def entry_kernel(info, gathered, shift, field, kappa, packet):
    ns, _, nzs, nx, ny = gathered.shape
    rows = nx // 2
    for z in range(ns * nzs):
        field[:, z, :] = gathered[z // nzs, 0, z % nzs]
        kappa[:, z, :] = gathered[z // nzs, 1, z % nzs]
    core = info[4] % 2
    packet[pl.ds(0, rows)] = field[pl.ds(core * rows, rows)]
    packet[rows] = jnp.broadcast_to(shift[...].astype(F32) * 0.5, packet.shape[1:])


def chain_entry(info, gathered, shift):
    ns, _, nzs, nx, ny = gathered.shape
    nz = ns * nzs
    vmem = pl.BlockSpec(memory_space=pltpu.VMEM)
    return pl.pallas_call(
        entry_kernel,
        in_specs=[pl.BlockSpec(memory_space=pltpu.SMEM), vmem, vmem],
        out_specs=[vmem] * 3,
        out_shape=[
            jax.ShapeDtypeStruct((nx, nz, ny), F32),
            jax.ShapeDtypeStruct((nx, nz, ny), F32),
            jax.ShapeDtypeStruct((nx // 2 + 1, nz, ny), F32),
        ],
        compiler_params=pltpu.CompilerParams(vmem_limit_bytes=8 * MIB),
        name="chain_entry",
    )(info, gathered, shift)


def place(members, slot, core, mine, theirs, rows):
    members[slot, pl.ds(core * rows, rows)] = mine[pl.ds(0, rows)]
    members[slot, pl.ds((1 - core) * rows, rows)] = theirs[pl.ds(0, rows)]


def level_kernel(length, axis, info, own, own_tail, before, kappa, *refs):
    packets, (packet, after, members, halves, work, saved) = refs[:6], refs[6:]
    nx, nz, ny = kappa.shape
    rows = nx // 2
    core, position = info[4] % 2, info[axis]
    inner = info[3] if length > 1 else 0
    members[position] = own[...]
    for j in range(length):
        halves[position * length + j] = jnp.broadcast_to(own_tail[j : j + 1], (nz, ny))
    for k in range(1, 4):
        slot = (position + (4 - k)) % 4
        mine, theirs = packets[2 * (k - 1)], packets[2 * (k - 1) + 1]
        place(members, slot, core, mine, theirs, rows)
        for j in range(length):
            halves[slot * length + j] = jnp.broadcast_to(mine[rows, j : j + 1], (nz, ny))
    work[0] = members[0]
    saved[...] = jnp.zeros(saved.shape, F32)

    def turn(t, _):
        group, inside = t // length, t % length
        here, there = (t - length) % 2, (t - length + 1) % 2

        @pl.when((group == position) & (inside == inner))
        def _():
            saved[...] = work[here]

        coarse_step(work.at[here], work.at[there], kappa, halves[t])

        @pl.when(inside == length - 1)
        def _():
            work[there] = work[there] + members[group]

        return 0

    lax.fori_loop(length, 4 * length, turn, 0)
    last = (3 * length) % 2
    after[...] = saved[...] + before[...] if length > 1 else saved[...]
    if length > 1:
        packet[pl.ds(0, rows)] = work[last, pl.ds(core * rows, rows)]
        for j in range(4 * length):
            packet[rows + j // 8, j % 8 : j % 8 + 1] = halves[j, 0:1]
    else:
        packet[pl.ds(0, nx)] = work[last]
        for j in range(4):
            packet[nx, j : j + 1] = halves[j, 0:1]


def chain_level(length, axis, info, own, own_tail, before, kappa, packets):
    nx, nz, ny = kappa.shape
    rows = nx // 2
    vmem = pl.BlockSpec(memory_space=pltpu.VMEM)
    size = rows + 2 if length > 1 else nx + 1
    return pl.pallas_call(
        functools.partial(level_kernel, length, axis),
        in_specs=[pl.BlockSpec(memory_space=pltpu.SMEM)] + [vmem] * (4 + len(packets)),
        out_specs=[vmem] * 2,
        out_shape=[
            jax.ShapeDtypeStruct((size, nz, ny), F32),
            jax.ShapeDtypeStruct((nx, nz, ny), F32),
        ],
        scratch_shapes=[
            pltpu.VMEM((4, nx, nz, ny), F32),
            pltpu.VMEM((4 * length, nz, ny), F32),
            pltpu.VMEM((2, nx, nz, ny), F32),
            pltpu.VMEM((nx, nz, ny), F32),
        ],
        compiler_params=pltpu.CompilerParams(vmem_limit_bytes=12 * MIB),
        name=f"chain_level_{length}",
    )(info, own, own_tail, before, kappa, *packets)


def final_kernel(info, field, before, kappa, tail, *refs):
    packets, (coarse, members, halves, work) = refs[:6], refs[6:]
    nx, nz, ny = kappa.shape
    rows = nx // 2
    core, zh = info[4] % 2, info[1]
    inside = info[2] * 4 + info[3]
    for j in range(16):
        halves[zh * 16 + j] = jnp.broadcast_to(tail[j // 8, j % 8 : j % 8 + 1], (nz, ny))
    for k in range(1, 4):
        slot = (zh + (4 - k)) % 4
        mine, theirs = packets[2 * (k - 1)], packets[2 * (k - 1) + 1]
        place(members, slot, core, mine, theirs, rows)
        for j in range(16):
            halves[slot * 16 + j] = jnp.broadcast_to(mine[rows + j // 8, j % 8 : j % 8 + 1], (nz, ny))
    begin = zh * 16
    work[0] = jnp.where(zh > 0, members[0], 0.0)
    low = jnp.where(zh > 0, 16, 0)
    high = jnp.where(zh > 0, begin + inside, 0)

    def turn(t, _):
        here, there = t % 2, (t + 1) % 2
        coarse_step(work.at[here], work.at[there], kappa, halves[t])

        @pl.when((t % 16 == 15) & (t < begin))
        def _():
            work[there] = work[there] + members[t // 16]

        return 0

    lax.fori_loop(low, high, turn, 0)
    here, there = high % 2, (high + 1) % 2
    work[here] = work[here] + before[...]
    coarse_step(work.at[here], work.at[there], kappa, halves[begin + inside])
    members[0] = work[here]
    members[1] = work[there] + field[...] - work[here]
    blank = jnp.zeros((nx, ny), F32)
    for f in range(2):
        for edge in range(2):
            coarse[f, edge] = blank
            coarse[f, nz + 2 + edge] = blank
        for z in range(nz):
            coarse[f, z + 2] = members[f, :, z, :]


def chain_final(info, field, before, kappa, tail, packets):
    nx, nz, ny = kappa.shape
    vmem = pl.BlockSpec(memory_space=pltpu.VMEM)
    return pl.pallas_call(
        final_kernel,
        in_specs=[pl.BlockSpec(memory_space=pltpu.SMEM)] + [vmem] * (4 + len(packets)),
        out_specs=vmem,
        out_shape=jax.ShapeDtypeStruct((2, nz + 4, nx, ny), F32),
        scratch_shapes=[
            pltpu.VMEM((4, nx, nz, ny), F32),
            pltpu.VMEM((64, nz, ny), F32),
            pltpu.VMEM((2, nx, nz, ny), F32),
        ],
        compiler_params=pltpu.CompilerParams(vmem_limit_bytes=12 * MIB),
        name="chain_final",
    )(info, field, before, kappa, tail, *packets)


def sweeps_kernel(
    info, table, coarse, sums, sums_low, sums_high, start, start_low, start_high,
    labels, labels_low, labels_high, shift, out,
    lift, kappa, first, fields, second, mixed,
):
    nz, nx, ny = start.shape
    wide = 3 * nz
    space = info[4]
    advect = shift[...].astype(F32)
    for f in range(2):
        for k in range(wide // 4):
            value = coarse[f, space * (nz // 4) + k]
            lift[f, k, pl.ds(0, nx // 2, stride=2), :] = value
            lift[f, k, pl.ds(1, nx // 2, stride=2), :] = value

    def parts(body, low, high):
        lax.fori_loop(low, high, lambda z, _: (body(z), 0)[1], 0)

    inside_low, inside_high = space > 0, space < 3
    for base, ref, keep in (
        (0, labels_low, inside_low), (nz, labels, None), (2 * nz, labels_high, inside_high),
    ):
        def fill(z, base=base, ref=ref, keep=keep):
            value = kappa_of(ref[z], table)
            kappa[base + z] = value if keep is None else jnp.where(keep, value, 0.0)
        parts(fill, 0, nz)

    q00 = float(Q[0, 0])
    for base, ref, src in (
        (0, start_low, sums_low), (nz, start, sums), (2 * nz, start_high, sums_high),
    ):
        def opening(z, base=base, ref=ref, src=src):
            at = (base + z) // 4
            begin, grow = lift[0, at], lift[1, at]
            own = ref[z]
            first[base + z] = own + begin
            mixed[base + z] = (
                src[0, z] + q00 * own + float(DT[0]) * begin + float(0.5 * DT[0] ** 2) * grow
            )
        parts(opening, 0, nz)

    def advance(source, target, low, high):
        def body(z):
            target[z] = source[z] + rate(mixed[z - 1], mixed[z], mixed[z + 1], kappa[z], advect)
        parts(body, low, high)

    advance(first, fields.at[0], 1, wide - 1)
    for m in range(1, STEPS):
        for base, ref, src in (
            (0, start_low, sums_low), (nz, start, sums), (2 * nz, start_high, sums_high),
        ):
            def mixing(z, base=base, ref=ref, src=src, m=m):
                at = (base + z) // 4
                mixed[base + z] = (
                    float(DT[m]) * fields[m - 1, base + z]
                    + src[m, z]
                    + float(Q[m, 0]) * ref[z]
                    + float(0.5 * DT[m] ** 2) * lift[1, at]
                )
            parts(mixing, m if base == 0 else 0, nz - m if base == 2 * nz else nz)
        advance(fields.at[m - 1], fields.at[m], m + 1, wide - 1 - m)

    for m in range(STEPS):
        edge = STEPS + m

        def mixing(z, m=m):
            total = float(Q[m, 0] - (DT[0] if m == 0 else 0.0)) * first[z]
            for j in range(1, NODES):
                total = total + float(Q[m, j] - (DT[m] if m == j else 0.0)) * fields[j - 1, z]
            before = first[z] if m == 0 else second[m - 1, z]
            mixed[z] = total + float(DT[m]) * before

        parts(mixing, edge, wide - edge)
        advance(first if m == 0 else second.at[m - 1], second.at[m], edge + 1, wide - edge - 1)

    def emit(z):
        out[0, 0, z] = first[nz + z]
        for m in range(STEPS):
            out[0, m + 1, z] = second[m, nz + z]
    parts(emit, 0, nz)


def fine_sweeps(info, table, coarse, sums, sums_low, sums_high, start, start_low, start_high,
                labels, labels_low, labels_high, shift):
    nz, nx, ny = start.shape
    vmem = pl.BlockSpec(memory_space=pltpu.VMEM)
    smem = pl.BlockSpec(memory_space=pltpu.SMEM)
    wide = 3 * nz
    return pl.pallas_call(
        sweeps_kernel,
        in_specs=[smem, smem] + [vmem] * 11,
        out_specs=vmem,
        out_shape=jax.ShapeDtypeStruct((1, NODES, nz, nx, ny), F32),
        scratch_shapes=[
            pltpu.VMEM((2, wide // 4, nx, ny), F32),
            pltpu.VMEM((wide, nx, ny), F32),
            pltpu.VMEM((wide, nx, ny), F32),
            pltpu.VMEM((STEPS, wide, nx, ny), F32),
            pltpu.VMEM((STEPS, wide, nx, ny), F32),
            pltpu.VMEM((wide, nx, ny), F32),
        ],
        compiler_params=pltpu.CompilerParams(vmem_limit_bytes=48 * MIB),
        name="fine_sweeps",
    )(info, table, coarse, sums, sums_low, sums_high, start, start_low, start_high,
      labels, labels_low, labels_high, shift)


def to_space(value, by):
    return lax.ppermute(value, "space", [(i, i + by) for i in range(4) if 0 <= i + by < 4])


def to_next(value, by):
    axes = TM + ("space",)
    pairs = [
        (4 * n + s, 4 * (n + 1) + s + by) for n in range(63) for s in range(4) if 0 <= s + by < 4
    ]
    return lax.ppermute(value, axes, pairs)


def swap_core(value):
    return lax.ppermute(value, "space", [(0, 1), (1, 0), (2, 3), (3, 2)])


def gather_axis(packet, axis):
    packets = []
    for k in range(1, 4):
        got = lax.ppermute(packet, axis, [(i, (i + k) % 4) for i in range(4)])
        packets += [got, swap_core(got)]
    return packets


def shards(node_fields, region_label, sheet_shift, diffusivity):
    zh, y, x = (lax.axis_index(a) for a in TM)
    space = lax.axis_index("space")
    info = jnp.stack([zh * 16 + y * 4 + x, zh, y, x, space]).astype(jnp.int32)
    nz = region_label.shape[0]
    last = node_fields[0, NODES - 1]
    arrived = to_next(last, 0)
    s_low = to_next(last[nz - 1 :], 1)
    s_high = to_next(last[:1], -1)
    sums, weighted = node_sums(info, node_fields)
    w_low = to_space(weighted[nz - 1 :], 1)
    w_high = to_space(weighted[:1], -1)
    coarse, start = residual(
        info, diffusivity, weighted, arrived, node_fields, region_label, sheet_shift,
        w_low, w_high, s_low, s_high,
    )
    sums_low, sums_high = to_space(sums, 1), to_space(sums, -1)
    labels_low, labels_high = to_space(region_label, 1), to_space(region_label, -1)
    start_low, start_high = to_space(start, 1), to_space(start, -1)

    gathered = lax.all_gather(coarse, "space", axis=0, tiled=False)
    field, kappa, packet = chain_entry(info, gathered, sheet_shift)
    rows = field.shape[0] // 2
    packets = gather_axis(packet, "x")
    one, prefix = chain_level(1, 3, info, field, packet[rows], field, kappa, packets)
    own = one[: 2 * rows]
    half = lax.dynamic_slice_in_dim(own, (space % 2) * rows, rows, 0)
    packet = jnp.concatenate([half, one[2 * rows :]], 0)
    packets = gather_axis(packet, "y")
    two, prefix = chain_level(4, 2, info, own, one[2 * rows], prefix, kappa, packets)
    packets = gather_axis(two, "zh")
    correction = chain_final(info, field, prefix, kappa, two[rows:], packets)
    return fine_sweeps(
        info, diffusivity, correction, sums, sums_low, sums_high, start, start_low, start_high,
        region_label, labels_low, labels_high, sheet_shift,
    )


def solution(mesh):
    grid = Mesh(mesh.devices.reshape(4, 4, 4, 4), TM + ("space",))
    in_specs = (P(TM, None, "space", None, None), P("space", None, None), P(TM, None), P())
    out_specs = P(TM, None, "space", None, None)
    return jax.shard_map(shards, mesh=grid, in_specs=in_specs, out_specs=out_specs, check_vma=False)
```

time: 1310 us -> 165 us (0.13)
  the two profiles are of different devices: /device:TPU:160 before, /device:TPU:217 now
where the time goes in v1:
time: 165 us; the launch traced here: 164 us
  starting transfers between devices  66.3 us (40%)
  Pallas kernels  47.3 us (29%)
  blocking collectives  24.7 us (15%)
  waiting for transfers between devices  20 us (12%)
  local copies, waits for them, and re-layouts  5.4 us (3%)
    ppermute x8, starting transfers between devices, to_space(): lax.ppermute(value, 'space', [(i, i + by) for i in range(4) if 0 <= i + b...  28.9 us
    all_gather x1, blocking collectives, shards(): gathered = lax.all_gather(coarse, 'space', axis=0, tiled=False)  24.7 us
    ppermute x9, starting transfers between devices, gather_axis(): got = lax.ppermute(packet, axis, [(i, (i + k) % 4) for i in range(4)])  23.8 us
    pallas_call x1, Pallas kernels, fine_sweeps(): pl.pallas_call(sweeps_kernel, in_specs=[smem, smem] + [vmem] * 11, out_sp...  21.3 us
    ppermute x9, waiting for transfers between devices, gather_axis(): got = lax.ppermute(packet, axis, [(i, (i + k) % 4) for i in range(4)])  18.3 us
    pallas_call x1, Pallas kernels, chain_final(): pl.pallas_call(final_kernel, in_specs=[pl.BlockSpec(memory_space=pltpu.SM...  15.3 us
    ppermute x3, starting transfers between devices, to_next(): return lax.ppermute(value, axes, pairs)  10.2 us
    pallas_call x2, Pallas kernels, chain_level(): pl.pallas_call(functools.partial(level_kernel, length, axis), in_specs=[p...  6.35 us
  transfers between devices with their start and end apart: 29, of which 12 were waited for; matrix products, arithmetic and copies ran while one was open for 1% of the time, Pallas kernels for 16%

profile of v1, /device:TPU:217, one launch (start us, length us, event | category | flops | bytes accessed | tf_op | source)
XLA Modules:
  0.0 164.2 jit_solution(13851563188111852226)
XLA Ops:
  0.0 1.9 %slice_bitcast_fusion = f32[8,128,128]{2,1,0:T(8,128)} fusion(f32[1,5,8,128,128]{4,3,2,1,0:T(8,128)} %u4_.1), kind=kLoop, calls=%fused_computation | loop fusion | bytes 1048576 | tf_op jit(solution)/shard_map/squeeze | solution.py:494
  1.9 3.1 %collective-permute-start = (f32[8,128,128]{2,1,0:T(8,128)}, f32[8,128,128]{2,1,0:T(8,128)S(1)}, u32[]{:S(2)}, u32[]{:S(2)}) collective-permute-start(f32[8,128,128]{2,1,0:T(8,128)} %slice_bitcast_fusion), channel_id=1, source_target_pairs={{0,4},{1,5},{2,6},{3,7},{4,8},{5,9},{6,10},{7,11},{8,12},{9,13},{1... | collective-permute-start | bytes 1572872 | tf_op jit(solution)/shard_map/ppermute | solution.py:474
  5.1 0.9 slice_bitcast_fusion.1
  5.9 4.0 %collective-permute-start.4 = (f32[1,128,128]{2,1,0:T(8,128)S(1)}, f32[1,128,128]{2,1,0:T(8,128)S(1)}, u32[]{:S(2)}, u32[]{:S(2)}) collective-permute-start(f32[1,128,128]{2,1,0:T(8,128)S(1)} %get-tuple-element.27), channel_id=1, source_target_pairs={{1,4},{2,5},{3,6},{5,8},{6,9},{7,10},{9,12},{10,13},{11,14},{13,16... | collective-permute-start | bytes 196616 | tf_op jit(solution)/shard_map/ppermute | solution.py:474
  9.9 3.2 %collective-permute-start.3 = (f32[1,128,128]{2,1,0:T(8,128)S(1)}, f32[1,128,128]{2,1,0:T(8,128)S(1)}, u32[]{:S(2)}, u32[]{:S(2)}) collective-permute-start(f32[1,128,128]{2,1,0:T(8,128)S(1)} %get-tuple-element.28), channel_id=1, source_target_pairs={{0,5},{1,6},{2,7},{4,9},{5,10},{6,11},{8,13},{9,14},{10,15},{12,17... | collective-permute-start | bytes 196616 | tf_op jit(solution)/shard_map/ppermute | solution.py:474
  13.1 0.1 stack.23.info
  13.2 1.7 %copy-done = f32[1,5,8,128,128]{4,3,2,1,0:T(8,128)S(1)} copy-done((f32[1,5,8,128,128]{4,3,2,1,0:T(8,128)S(1)}, f32[1,5,8,128,128]{4,3,2,1,0:T(8,128)}, u32[]{:S(2)}) %copy-start) | copy-done | bytes 2621464
  14.9 1.7 %node_sums.1 = (f32[4,8,128,128]{3,2,1,0:T(8,128)S(1)}, f32[8,128,128]{2,1,0:T(8,128)S(1)}) custom-call(s32[5]{0:T(128)S(1)} %stack.23.info, f32[1,5,8,128,128]{4,3,2,1,0:T(8,128)S(1)} %copy-done), custom_call_target="tpu_custom_call" | custom-call | flops 10000000 | bytes 6000000 | tf_op jit(solution)/shard_map/node_sums/pallas_call | solution.py:92
  16.6 2.0 %collective-permute-start.2 = (f32[1,128,128]{2,1,0:T(8,128)S(1)}, f32[1,128,128]{2,1,0:T(8,128)S(1)}, u32[]{:S(2)}, u32[]{:S(2)}) collective-permute-start(f32[1,128,128]{2,1,0:T(8,128)S(1)} %get-tuple-element.29), channel_id=1, source_target_pairs={{1,0},{2,1},{3,2},{5,4},{6,5},{7,6},{9,8},{10,9},{11,10},{13,12},{... | collective-permute-start | bytes 196616 | tf_op jit(solution)/shard_map/ppermute | solution.py:466
  18.6 3.6 %collective-permute-start.1 = (f32[1,128,128]{2,1,0:T(8,128)S(1)}, f32[1,128,128]{2,1,0:T(8,128)S(1)}, u32[]{:S(2)}, u32[]{:S(2)}) collective-permute-start(f32[1,128,128]{2,1,0:T(8,128)S(1)} %get-tuple-element.30), channel_id=1, source_target_pairs={{0,1},{1,2},{2,3},{4,5},{5,6},{6,7},{8,9},{9,10},{10,11},{12,13},{... | collective-permute-start | bytes 196616 | tf_op jit(solution)/shard_map/ppermute | solution.py:466
  22.2 1.9 %collective-permute-start.24 = (f32[4,8,128,128]{3,2,1,0:T(8,128)S(1)}, f32[4,8,128,128]{3,2,1,0:T(8,128)}, u32[]{:S(2)}, u32[]{:S(2)}) collective-permute-start(f32[4,8,128,128]{3,2,1,0:T(8,128)S(1)} %get-tuple-element.25.sums), channel_id=1, source_target_pairs={{1,0},{2,1},{3,2},{5,4},{6,5},{7,6},{9,8},{10,9},{11,10},{13,12},{... | collective-permute-start | bytes 6291464 | tf_op jit(solution)/shard_map/ppermute | solution.py:466
  24.2 3.6 %collective-permute-start.23 = (f32[4,8,128,128]{3,2,1,0:T(8,128)S(1)}, f32[4,8,128,128]{3,2,1,0:T(8,128)}, u32[]{:S(2)}, u32[]{:S(2)}) collective-permute-start(f32[4,8,128,128]{3,2,1,0:T(8,128)S(1)} %get-tuple-element.25.sums), channel_id=1, source_target_pairs={{0,1},{1,2},{2,3},{4,5},{5,6},{6,7},{8,9},{9,10},{10,11},{12,13},{... | collective-permute-start | bytes 6291464 | tf_op jit(solution)/shard_map/ppermute | solution.py:466
  27.9 1.2 residual.1
  29.1 24.7 %all-gather = f32[8,2,64,128]{3,2,1,0:T(8,128)S(1)} all-gather(f32[2,2,64,128]{3,2,1,0:T(8,128)S(1)} %get-tuple-element.17), channel_id=2, replica_groups=mesh['zh'=4,'y'=4,'x'=4,'space'=4] {'space'}, dimensions={0}, use_global_device_ids=true | all-gather | bytes 655360 | tf_op jit(solution)/shard_map/all_gather | solution.py:509
  53.8 1.5 chain_entry.1
  55.3 5.0 %collective-permute-start.9 = (f32[33,8,128]{2,1,0:T(8,128)}, f32[33,8,128]{2,1,0:T(8,128)S(1)}, u32[]{:S(2)}, u32[]{:S(2)}) collective-permute-start(f32[33,8,128]{2,1,0:T(8,128)} %get-tuple-element.19), channel_id=1, source_target_pairs={{0,12},{4,0},{8,4},{12,8},{1,13},{5,1},{9,5},{13,9},{2,14},{6,2},{... | collective-permute-start | bytes 405512 | tf_op jit(solution)/shard_map/ppermute | solution.py:484
  60.3 0.6 collective-permute-start.5
  60.8 3.7 %collective-permute-done.9.refs_4_ = f32[33,8,128]{2,1,0:T(8,128)S(1)} collective-permute-done((f32[33,8,128]{2,1,0:T(8,128)}, f32[33,8,128]{2,1,0:T(8,128)S(1)}, u32[]{:S(2)}, u32[]{:S(2)}) %collective-permute-start.9) | collective-permute-done | bytes 135200 | tf_op jit(solution)/shard_map/ppermute | solution.py:484
  64.5 1.4 collective-permute-done.7.refs_2_
  66.0 1.0 collective-permute-done.5.refs_0_
  67.0 0.7 slice_bitcast_fusion.3.own_tail
  67.7 8.1 %collective-permute-start.27 = (s32[8,128,128]{2,1,0:T(8,128)S(1)}, s32[8,128,128]{2,1,0:T(8,128)S(1)}, u32[]{:S(2)}, u32[]{:S(2)}) collective-permute-start(s32[8,128,128]{2,1,0:T(8,128)S(1)} %copy-done.1), channel_id=1, source_target_pairs={{0,1},{1,2},{2,3},{4,5},{5,6},{6,7},{8,9},{9,10},{10,11},{12,13},{... | collective-permute-start | bytes 1572872 | tf_op jit(solution)/shard_map/ppermute | solution.py:466
  75.8 1.6 chain_level_1.1
  77.6 0.1 collective-permute-start.15
  77.6 10.9 %collective-permute-start.13 = (f32[33,8,128]{2,1,0:T(8,128)S(1)}, f32[33,8,128]{2,1,0:T(8,128)S(1)}, u32[]{:S(2)}, u32[]{:S(2)}) collective-permute-start(f32[33,8,128]{2,1,0:T(8,128)S(1)} %pad_maximum_fusion), channel_id=1, source_target_pairs={{0,32},{16,48},{32,0},{48,16},{1,33},{17,49},{33,1},{49,17},{2,34}... | collective-permute-start | bytes 405512 | tf_op jit(solution)/shard_map/ppermute | solution.py:484
  88.5 1.9 %collective-permute-done.15.refs_4_ = f32[33,8,128]{2,1,0:T(8,128)S(1)} collective-permute-done((f32[33,8,128]{2,1,0:T(8,128)S(1)}, f32[33,8,128]{2,1,0:T(8,128)S(1)}, u32[]{:S(2)}, u32[]{:S(2)}) %collective-permute-start.15) | collective-permute-done | bytes 135200 | tf_op jit(solution)/shard_map/ppermute | solution.py:484
  90.4 2.2 %collective-permute-start.11 = (f32[33,8,128]{2,1,0:T(8,128)S(1)}, f32[33,8,128]{2,1,0:T(8,128)S(1)}, u32[]{:S(2)}, u32[]{:S(2)}) collective-permute-start(f32[33,8,128]{2,1,0:T(8,128)S(1)} %pad_maximum_fusion), channel_id=1, source_target_pairs={{0,16},{16,32},{32,48},{48,0},{1,17},{17,33},{33,49},{49,1},{2,18}... | collective-permute-start | bytes 405512 | tf_op jit(solution)/shard_map/ppermute | solution.py:484
  92.6 1.2 collective-permute-done.13.refs_2_
  93.8 0.8 collective-permute-done.11.refs_0_
  94.6 0.5 collective-permute-done.16.refs_5_
  95.2 0.1 collective-permute-start.12
  95.3 0.7 collective-permute-done.14.refs_3_
  96.0 0.5 collective-permute-done.12.refs_1_
  96.5 4.8 %chain_level_4.1 = (f32[34,8,128]{2,1,0:T(8,128)S(1)}, f32[64,8,128]{2,1,0:T(8,128)S(1)}) custom-call(s32[5]{0:T(128)S(1)} %stack.23.info, f32[64,8,128]{2,1,0:T(8,128)S(1)} %slice.44.own, f32[8,128]{1,0:T(8,128)S(1)} %get-tuple-element.32.own_tail, f32[64,8,128]{2,1,0:T(8,128)S(1)} %get-tuple-element.22.before, f32[64,8,128]{2,1,0:T(8,128)S(1)} %get-tuple-element.20.kappa, ...), custom_call_target="tpu_custom_call" | custom-call | tf_op jit(solution)/shard_map/chain_level_4/pallas_call | solution.py:277
  101.3 1.5 collective-permute-start.21
  102.8 2.6 %collective-permute-start.19 = (f32[34,8,128]{2,1,0:T(8,128)S(1)}, f32[34,8,128]{2,1,0:T(8,128)S(1)}, u32[]{:S(2)}, u32[]{:S(2)}) collective-permute-start(f32[34,8,128]{2,1,0:T(8,128)S(1)} %get-tuple-element.24), channel_id=1, source_target_pairs={{0,128},{64,192},{128,0},{192,64},{1,129},{65,193},{129,1},{193,65... | collective-permute-start | bytes 417800 | tf_op jit(solution)/shard_map/ppermute | solution.py:484
  105.4 1.0 collective-permute-start.17
  106.4 2.3 %collective-permute-done.21.refs_4_ = f32[34,8,128]{2,1,0:T(8,128)S(1)} collective-permute-done((f32[34,8,128]{2,1,0:T(8,128)S(1)}, f32[34,8,128]{2,1,0:T(8,128)S(1)}, u32[]{:S(2)}, u32[]{:S(2)}) %collective-permute-start.21) | collective-permute-done | bytes 139296 | tf_op jit(solution)/shard_map/ppermute | solution.py:484
  108.7 1.3 collective-permute-start.22
  110.0 5.4 %collective-permute-done.19.refs_2_ = f32[34,8,128]{2,1,0:T(8,128)S(1)} collective-permute-done((f32[34,8,128]{2,1,0:T(8,128)S(1)}, f32[34,8,128]{2,1,0:T(8,128)S(1)}, u32[]{:S(2)}, u32[]{:S(2)}) %collective-permute-start.19) | collective-permute-done | bytes 139296 | tf_op jit(solution)/shard_map/ppermute | solution.py:484
  115.4 0.6 collective-permute-start.20
  116.0 0.6 collective-permute-done.17.refs_0_
  116.5 1.3 collective-permute-start.18
  117.8 1.9 %collective-permute-start.28 = (s32[8,128,128]{2,1,0:T(8,128)S(1)}, s32[8,128,128]{2,1,0:T(8,128)S(1)}, u32[]{:S(2)}, u32[]{:S(2)}) collective-permute-start(s32[8,128,128]{2,1,0:T(8,128)S(1)} %copy-done.1), channel_id=1, source_target_pairs={{1,0},{2,1},{3,2},{5,4},{6,5},{7,6},{9,8},{10,9},{11,10},{13,12},{... | collective-permute-start | bytes 1572872 | tf_op jit(solution)/shard_map/ppermute | solution.py:466
  119.7 1.9 %collective-permute-start.26 = (f32[8,128,128]{2,1,0:T(8,128)S(1)}, f32[8,128,128]{2,1,0:T(8,128)S(1)}, u32[]{:S(2)}, u32[]{:S(2)}) collective-permute-start(f32[8,128,128]{2,1,0:T(8,128)S(1)} %copy-done.3), channel_id=1, source_target_pairs={{1,0},{2,1},{3,2},{5,4},{6,5},{7,6},{9,8},{10,9},{11,10},{13,12},{... | collective-permute-start | bytes 1572872 | tf_op jit(solution)/shard_map/ppermute | solution.py:466
  121.7 5.8 %collective-permute-start.25 = (f32[8,128,128]{2,1,0:T(8,128)S(1)}, f32[8,128,128]{2,1,0:T(8,128)S(1)}, u32[]{:S(2)}, u32[]{:S(2)}) collective-permute-start(f32[8,128,128]{2,1,0:T(8,128)S(1)} %copy-done.3), channel_id=1, source_target_pairs={{0,1},{1,2},{2,3},{4,5},{5,6},{6,7},{8,9},{9,10},{10,11},{12,13},{... | collective-permute-start | bytes 1572872 | tf_op jit(solution)/shard_map/ppermute | solution.py:466
  127.5 15.3 %chain_final.1.coarse = f32[2,12,64,128]{3,2,1,0:T(8,128)S(1)} custom-call(s32[5]{0:T(128)S(1)} %stack.23.info, f32[64,8,128]{2,1,0:T(8,128)S(1)} %get-tuple-element.18.own.before.field, f32[64,8,128]{2,1,0:T(8,128)S(1)} %get-tuple-element.23.before, f32[64,8,128]{2,1,0:T(8,128)S(1)} %get-tuple-element.20.kappa, f32[2,8,128]{2,1,0:T(8,128)S(1)} %slice.46.tail, ...), custom_call_target="tpu_custom_call" | custom-call | tf_op jit(solution)/shard_map/chain_final/pallas_call | solution.py:343
  142.9 21.3 %fine_sweeps.1 = f32[1,5,8,128,128]{4,3,2,1,0:T(8,128)} custom-call(s32[5]{0:T(128)S(1)} %stack.23.info, f32[4]{0:T(128)S(1)} %copy-done.7, f32[2,12,64,128]{3,2,1,0:T(8,128)S(1)} %chain_final.1.coarse, f32[4,8,128,128]{3,2,1,0:T(8,128)S(1)} %get-tuple-element.25.sums, f32[4,8,128,128]{3,2,1,0:T(8,128)} %collective-permute-done.23.sums_low, ...), custom_call_target="tpu_custom_call" | custom-call | tf_op jit(solution)/shard_map/fine_sweeps/pallas_call | solution.py:446
  (44 shorter events, 0.2 us)
Async XLA Ops:
  0.0 27.8 %copy-start.1 = (s32[8,128,128]{2,1,0:T(8,128)S(1)}, s32[8,128,128]{2,1,0:T(8,128)}, u32[]{:S(2)}) copy-start(s32[8,128,128]{2,1,0:T(8,128)} %labels.3) | copy-start | bytes 1572868
  0.0 27.8 %copy-start.4 = (s32[1,128]{1,0:T(1,128)S(1)}, s32[1,128]{1,0:T(1,128)}, u32[]{:S(2)}) copy-start(s32[1,128]{1,0:T(1,128)} %shift.5) | copy-start | bytes 1540
  0.0 27.9 %copy-start.6 = (f32[4]{0:T(128)S(1)}, f32[4]{0:T(128)}, u32[]{:S(2)}) copy-start(f32[4]{0:T(128)} %table.3) | copy-start | bytes 52
  1.9 25.9 %collective-permute-start = (f32[8,128,128]{2,1,0:T(8,128)}, f32[8,128,128]{2,1,0:T(8,128)S(1)}, u32[]{:S(2)}, u32[]{:S(2)}) collective-permute-start(f32[8,128,128]{2,1,0:T(8,128)} %slice_bitcast_fusion), channel_id=1, source_target_pairs={{0,4},{1,5},{2,6},{3,7},{4,8},{5,9},{6,10},{7,11},{8,12},{9,13},{1... | collective-permute-start | bytes 1572872 | tf_op jit(solution)/shard_map/ppermute | solution.py:474
  5.9 16.3 %collective-permute-start.4 = (f32[1,128,128]{2,1,0:T(8,128)S(1)}, f32[1,128,128]{2,1,0:T(8,128)S(1)}, u32[]{:S(2)}, u32[]{:S(2)}) collective-permute-start(f32[1,128,128]{2,1,0:T(8,128)S(1)} %get-tuple-element.27), channel_id=1, source_target_pairs={{1,4},{2,5},{3,6},{5,8},{6,9},{7,10},{9,12},{10,13},{11,14},{13,16... | collective-permute-start | bytes 196616 | tf_op jit(solution)/shard_map/ppermute | solution.py:474
  9.9 14.2 %collective-permute-start.3 = (f32[1,128,128]{2,1,0:T(8,128)S(1)}, f32[1,128,128]{2,1,0:T(8,128)S(1)}, u32[]{:S(2)}, u32[]{:S(2)}) collective-permute-start(f32[1,128,128]{2,1,0:T(8,128)S(1)} %get-tuple-element.28), channel_id=1, source_target_pairs={{0,5},{1,6},{2,7},{4,9},{5,10},{6,11},{8,13},{9,14},{10,15},{12,17... | collective-permute-start | bytes 196616 | tf_op jit(solution)/shard_map/ppermute | solution.py:474
  13.2 1.7 %copy-start = (f32[1,5,8,128,128]{4,3,2,1,0:T(8,128)S(1)}, f32[1,5,8,128,128]{4,3,2,1,0:T(8,128)}, u32[]{:S(2)}) copy-start(f32[1,5,8,128,128]{4,3,2,1,0:T(8,128)} %u4_.1) | copy-start | bytes 7864324
  16.6 11.2 %collective-permute-start.2 = (f32[1,128,128]{2,1,0:T(8,128)S(1)}, f32[1,128,128]{2,1,0:T(8,128)S(1)}, u32[]{:S(2)}, u32[]{:S(2)}) collective-permute-start(f32[1,128,128]{2,1,0:T(8,128)S(1)} %get-tuple-element.29), channel_id=1, source_target_pairs={{1,0},{2,1},{3,2},{5,4},{6,5},{7,6},{9,8},{10,9},{11,10},{13,12},{... | collective-permute-start | bytes 196616 | tf_op jit(solution)/shard_map/ppermute | solution.py:466
  18.6 9.2 %collective-permute-start.1 = (f32[1,128,128]{2,1,0:T(8,128)S(1)}, f32[1,128,128]{2,1,0:T(8,128)S(1)}, u32[]{:S(2)}, u32[]{:S(2)}) collective-permute-start(f32[1,128,128]{2,1,0:T(8,128)S(1)} %get-tuple-element.30), channel_id=1, source_target_pairs={{0,1},{1,2},{2,3},{4,5},{5,6},{6,7},{8,9},{9,10},{10,11},{12,13},{... | collective-permute-start | bytes 196616 | tf_op jit(solution)/shard_map/ppermute | solution.py:466
  22.2 120.7 %collective-permute-start.24 = (f32[4,8,128,128]{3,2,1,0:T(8,128)S(1)}, f32[4,8,128,128]{3,2,1,0:T(8,128)}, u32[]{:S(2)}, u32[]{:S(2)}) collective-permute-start(f32[4,8,128,128]{3,2,1,0:T(8,128)S(1)} %get-tuple-element.25.sums), channel_id=1, source_target_pairs={{1,0},{2,1},{3,2},{5,4},{6,5},{7,6},{9,8},{10,9},{11,10},{13,12},{... | collective-permute-start | bytes 6291464 | tf_op jit(solution)/shard_map/ppermute | solution.py:466
  24.2 118.7 %collective-permute-start.23 = (f32[4,8,128,128]{3,2,1,0:T(8,128)S(1)}, f32[4,8,128,128]{3,2,1,0:T(8,128)}, u32[]{:S(2)}, u32[]{:S(2)}) collective-permute-start(f32[4,8,128,128]{3,2,1,0:T(8,128)S(1)} %get-tuple-element.25.sums), channel_id=1, source_target_pairs={{0,1},{1,2},{2,3},{4,5},{5,6},{6,7},{8,9},{9,10},{10,11},{12,13},{... | collective-permute-start | bytes 6291464 | tf_op jit(solution)/shard_map/ppermute | solution.py:466
  29.1 26.2 %copy-start.2 = (f32[8,128,128]{2,1,0:T(8,128)}, f32[8,128,128]{2,1,0:T(8,128)S(1)}, u32[]{:S(2)}) copy-start(f32[8,128,128]{2,1,0:T(8,128)S(1)} %get-tuple-element.26.start) | copy-start | bytes 1572868
  55.3 9.2 %collective-permute-start.9 = (f32[33,8,128]{2,1,0:T(8,128)}, f32[33,8,128]{2,1,0:T(8,128)S(1)}, u32[]{:S(2)}, u32[]{:S(2)}) collective-permute-start(f32[33,8,128]{2,1,0:T(8,128)} %get-tuple-element.19), channel_id=1, source_target_pairs={{0,12},{4,0},{8,4},{12,8},{1,13},{5,1},{9,5},{13,9},{2,14},{6,2},{... | collective-permute-start | bytes 405512 | tf_op jit(solution)/shard_map/ppermute | solution.py:484
  60.3 5.7 %collective-permute-start.7 = (f32[33,8,128]{2,1,0:T(8,128)}, f32[33,8,128]{2,1,0:T(8,128)S(1)}, u32[]{:S(2)}, u32[]{:S(2)}) collective-permute-start(f32[33,8,128]{2,1,0:T(8,128)} %get-tuple-element.19), channel_id=1, source_target_pairs={{0,8},{4,12},{8,0},{12,4},{1,9},{5,13},{9,1},{13,5},{2,10},{6,14},... | collective-permute-start | bytes 405512 | tf_op jit(solution)/shard_map/ppermute | solution.py:484
  60.3 6.7 %collective-permute-start.5 = (f32[33,8,128]{2,1,0:T(8,128)}, f32[33,8,128]{2,1,0:T(8,128)S(1)}, u32[]{:S(2)}, u32[]{:S(2)}) collective-permute-start(f32[33,8,128]{2,1,0:T(8,128)} %get-tuple-element.19), channel_id=1, source_target_pairs={{0,4},{4,8},{8,12},{12,0},{1,5},{5,9},{9,13},{13,1},{2,6},{6,10},{... | collective-permute-start | bytes 405512 | tf_op jit(solution)/shard_map/ppermute | solution.py:484
  60.8 58.9 %copy-start.3 = (f32[8,128,128]{2,1,0:T(8,128)S(1)}, f32[8,128,128]{2,1,0:T(8,128)}, u32[]{:S(2)}) copy-start(f32[8,128,128]{2,1,0:T(8,128)} %copy-done.2) | copy-start | bytes 1572868
  64.5 3.1 %collective-permute-start.10 = (f32[33,8,128]{2,1,0:T(8,128)S(1)}, f32[33,8,128]{2,1,0:T(8,128)S(1)}, u32[]{:S(2)}, u32[]{:S(2)}) collective-permute-start(f32[33,8,128]{2,1,0:T(8,128)S(1)} %collective-permute-done.9.refs_4_), channel_id=1, source_target_pairs={{0,1},{1,0},{2,3},{3,2},{4,5},{5,4},{6,7},{7,6},{8,9},{9,8},{10,11... | collective-permute-start | bytes 405512 | tf_op jit(solution)/shard_map/ppermute | solution.py:478
  65.9 9.9 %collective-permute-start.8 = (f32[33,8,128]{2,1,0:T(8,128)S(1)}, f32[33,8,128]{2,1,0:T(8,128)S(1)}, u32[]{:S(2)}, u32[]{:S(2)}) collective-permute-start(f32[33,8,128]{2,1,0:T(8,128)S(1)} %collective-permute-done.7.refs_2_), channel_id=1, source_target_pairs={{0,1},{1,0},{2,3},{3,2},{4,5},{5,4},{6,7},{7,6},{8,9},{9,8},{10,11... | collective-permute-start | bytes 405512 | tf_op jit(solution)/shard_map/ppermute | solution.py:478
  67.0 8.8 %collective-permute-start.6 = (f32[33,8,128]{2,1,0:T(8,128)S(1)}, f32[33,8,128]{2,1,0:T(8,128)S(1)}, u32[]{:S(2)}, u32[]{:S(2)}) collective-permute-start(f32[33,8,128]{2,1,0:T(8,128)S(1)} %collective-permute-done.5.refs_0_), channel_id=1, source_target_pairs={{0,1},{1,0},{2,3},{3,2},{4,5},{5,4},{6,7},{7,6},{8,9},{9,8},{10,11... | collective-permute-start | bytes 405512 | tf_op jit(solution)/shard_map/ppermute | solution.py:478
  67.7 37.7 %collective-permute-start.27 = (s32[8,128,128]{2,1,0:T(8,128)S(1)}, s32[8,128,128]{2,1,0:T(8,128)S(1)}, u32[]{:S(2)}, u32[]{:S(2)}) collective-permute-start(s32[8,128,128]{2,1,0:T(8,128)S(1)} %copy-done.1), channel_id=1, source_target_pairs={{0,1},{1,2},{2,3},{4,5},{5,6},{6,7},{8,9},{9,10},{10,11},{12,13},{... | collective-permute-start | bytes 1572872 | tf_op jit(solution)/shard_map/ppermute | solution.py:466
  77.5 65.5 %copy-start.5 = (s32[1,128]{1,0:T(1,128)S(1)}, s32[1,128]{1,0:T(1,128)}, u32[]{:S(2)}) copy-start(s32[1,128]{1,0:T(1,128)} %shift.5) | copy-start | bytes 1540
  77.5 65.5 %copy-start.7 = (f32[4]{0:T(128)S(1)}, f32[4]{0:T(128)}, u32[]{:S(2)}) copy-start(f32[4]{0:T(128)} %table.3) | copy-start | bytes 52
  77.6 12.9 %collective-permute-start.15 = (f32[33,8,128]{2,1,0:T(8,128)S(1)}, f32[33,8,128]{2,1,0:T(8,128)S(1)}, u32[]{:S(2)}, u32[]{:S(2)}) collective-permute-start(f32[33,8,128]{2,1,0:T(8,128)S(1)} %pad_maximum_fusion), channel_id=1, source_target_pairs={{0,48},{16,0},{32,16},{48,32},{1,49},{17,1},{33,17},{49,33},{2,50}... | collective-permute-start | bytes 405512 | tf_op jit(solution)/shard_map/ppermute | solution.py:484
  77.6 16.2 %collective-permute-start.13 = (f32[33,8,128]{2,1,0:T(8,128)S(1)}, f32[33,8,128]{2,1,0:T(8,128)S(1)}, u32[]{:S(2)}, u32[]{:S(2)}) collective-permute-start(f32[33,8,128]{2,1,0:T(8,128)S(1)} %pad_maximum_fusion), channel_id=1, source_target_pairs={{0,32},{16,48},{32,0},{48,16},{1,33},{17,49},{33,1},{49,17},{2,34}... | collective-permute-start | bytes 405512 | tf_op jit(solution)/shard_map/ppermute | solution.py:484
  90.4 4.2 %collective-permute-start.11 = (f32[33,8,128]{2,1,0:T(8,128)S(1)}, f32[33,8,128]{2,1,0:T(8,128)S(1)}, u32[]{:S(2)}, u32[]{:S(2)}) collective-permute-start(f32[33,8,128]{2,1,0:T(8,128)S(1)} %pad_maximum_fusion), channel_id=1, source_target_pairs={{0,16},{16,32},{32,48},{48,0},{1,17},{17,33},{33,49},{49,1},{2,18}... | collective-permute-start | bytes 405512 | tf_op jit(solution)/shard_map/ppermute | solution.py:484
  93.8 1.4 collective-permute-start.16
  94.6 1.4 collective-permute-start.14
  95.2 1.4 collective-permute-start.12
  101.3 7.4 %collective-permute-start.21 = (f32[34,8,128]{2,1,0:T(8,128)S(1)}, f32[34,8,128]{2,1,0:T(8,128)S(1)}, u32[]{:S(2)}, u32[]{:S(2)}) collective-permute-start(f32[34,8,128]{2,1,0:T(8,128)S(1)} %get-tuple-element.24), channel_id=1, source_target_pairs={{0,192},{64,0},{128,64},{192,128},{1,193},{65,1},{129,65},{193,129... | collective-permute-start | bytes 417800 | tf_op jit(solution)/shard_map/ppermute | solution.py:484
  102.8 12.6 %collective-permute-start.19 = (f32[34,8,128]{2,1,0:T(8,128)S(1)}, f32[34,8,128]{2,1,0:T(8,128)S(1)}, u32[]{:S(2)}, u32[]{:S(2)}) collective-permute-start(f32[34,8,128]{2,1,0:T(8,128)S(1)} %get-tuple-element.24), channel_id=1, source_target_pairs={{0,128},{64,192},{128,0},{192,64},{1,129},{65,193},{129,1},{193,65... | collective-permute-start | bytes 417800 | tf_op jit(solution)/shard_map/ppermute | solution.py:484
  105.4 11.1 %collective-permute-start.17 = (f32[34,8,128]{2,1,0:T(8,128)S(1)}, f32[34,8,128]{2,1,0:T(8,128)S(1)}, u32[]{:S(2)}, u32[]{:S(2)}) collective-permute-start(f32[34,8,128]{2,1,0:T(8,128)S(1)} %get-tuple-element.24), channel_id=1, source_target_pairs={{0,64},{64,128},{128,192},{192,0},{1,65},{65,129},{129,193},{193,1... | collective-permute-start | bytes 417800 | tf_op jit(solution)/shard_map/ppermute | solution.py:484
  108.7 9.1 %collective-permute-start.22 = (f32[34,8,128]{2,1,0:T(8,128)S(1)}, f32[34,8,128]{2,1,0:T(8,128)S(1)}, u32[]{:S(2)}, u32[]{:S(2)}) collective-permute-start(f32[34,8,128]{2,1,0:T(8,128)S(1)} %collective-permute-done.21.refs_4_), channel_id=1, source_target_pairs={{0,1},{1,0},{2,3},{3,2},{4,5},{5,4},{6,7},{7,6},{8,9},{9,8},{10,11... | collective-permute-start | bytes 417800 | tf_op jit(solution)/shard_map/ppermute | solution.py:478
  115.4 4.4 %collective-permute-start.20 = (f32[34,8,128]{2,1,0:T(8,128)S(1)}, f32[34,8,128]{2,1,0:T(8,128)S(1)}, u32[]{:S(2)}, u32[]{:S(2)}) collective-permute-start(f32[34,8,128]{2,1,0:T(8,128)S(1)} %collective-permute-done.19.refs_2_), channel_id=1, source_target_pairs={{0,1},{1,0},{2,3},{3,2},{4,5},{5,4},{6,7},{7,6},{8,9},{9,8},{10,11... | collective-permute-start | bytes 417800 | tf_op jit(solution)/shard_map/ppermute | solution.py:478
  116.5 5.2 %collective-permute-start.18 = (f32[34,8,128]{2,1,0:T(8,128)S(1)}, f32[34,8,128]{2,1,0:T(8,128)S(1)}, u32[]{:S(2)}, u32[]{:S(2)}) collective-permute-start(f32[34,8,128]{2,1,0:T(8,128)S(1)} %collective-permute-done.17.refs_0_), channel_id=1, source_target_pairs={{0,1},{1,0},{2,3},{3,2},{4,5},{5,4},{6,7},{7,6},{8,9},{9,8},{10,11... | collective-permute-start | bytes 417800 | tf_op jit(solution)/shard_map/ppermute | solution.py:478
  117.8 25.1 %collective-permute-start.28 = (s32[8,128,128]{2,1,0:T(8,128)S(1)}, s32[8,128,128]{2,1,0:T(8,128)S(1)}, u32[]{:S(2)}, u32[]{:S(2)}) collective-permute-start(s32[8,128,128]{2,1,0:T(8,128)S(1)} %copy-done.1), channel_id=1, source_target_pairs={{1,0},{2,1},{3,2},{5,4},{6,5},{7,6},{9,8},{10,9},{11,10},{13,12},{... | collective-permute-start | bytes 1572872 | tf_op jit(solution)/shard_map/ppermute | solution.py:466
  119.7 23.1 %collective-permute-start.26 = (f32[8,128,128]{2,1,0:T(8,128)S(1)}, f32[8,128,128]{2,1,0:T(8,128)S(1)}, u32[]{:S(2)}, u32[]{:S(2)}) collective-permute-start(f32[8,128,128]{2,1,0:T(8,128)S(1)} %copy-done.3), channel_id=1, source_target_pairs={{1,0},{2,1},{3,2},{5,4},{6,5},{7,6},{9,8},{10,9},{11,10},{13,12},{... | collective-permute-start | bytes 1572872 | tf_op jit(solution)/shard_map/ppermute | solution.py:466
  121.7 21.2 %collective-permute-start.25 = (f32[8,128,128]{2,1,0:T(8,128)S(1)}, f32[8,128,128]{2,1,0:T(8,128)S(1)}, u32[]{:S(2)}, u32[]{:S(2)}) collective-permute-start(f32[8,128,128]{2,1,0:T(8,128)S(1)} %copy-done.3), channel_id=1, source_target_pairs={{0,1},{1,2},{2,3},{4,5},{5,6},{6,7},{8,9},{9,10},{10,11},{12,13},{... | collective-permute-start | bytes 1572872 | tf_op jit(solution)/shard_map/ppermute | solution.py:466

commit v2 on v0

v2 whole, which is shorter than its diff:
```python
import functools
import math

import jax
import jax.numpy as jnp
import numpy as np
from jax import lax
from jax.experimental import pallas as pl
from jax.experimental.pallas import tpu as pltpu
from jax.sharding import Mesh
from jax.sharding import PartitionSpec as P

NODES = 5
STEPS = NODES - 1
F32 = jnp.float32
TM = ("zh", "y", "x")
MIB = 1 << 20


def node_tables():
    radius = math.sqrt(3.0 / 7.0)
    points = [0.0, (1.0 - radius) / 2.0, 0.5, (1.0 + radius) / 2.0, 1.0]
    integrals = np.zeros((4, 5))
    for column in range(5):
        coeffs = [1.0]
        divisor = 1.0
        for other in range(5):
            if other != column:
                anchor = points[other]
                product = [0.0] * (len(coeffs) + 1)
                for degree in range(len(coeffs)):
                    product[degree + 1] = product[degree + 1] + coeffs[degree]
                    product[degree] = product[degree] - anchor * coeffs[degree]
                coeffs = product
                divisor = divisor * (points[column] - anchor)
        for row in range(4):
            bottom = points[row]
            summit = points[row + 1]
            amount = 0.0
            for degree in range(len(coeffs)):
                amount = amount + coeffs[degree] / (degree + 1) * (
                    summit ** (degree + 1) - bottom ** (degree + 1)
                )
            integrals[row, column] = amount / divisor
    return (np.array(points), integrals)


TAU, Q = node_tables()
WEIGHTS = Q.sum(axis=0)
DT = TAU[1:] - TAU[:-1]


def kappa_of(labels, table):
    value = jnp.where(labels == 3, table[3], 0.0)
    for region in range(3):
        value = jnp.where(labels == region, table[region], value)
    return value


def rate(below, mid, above, behind, ahead, kappa, advect):
    cols = mid.shape[1]
    lane = lax.broadcasted_iota(jnp.int32, mid.shape, 1)
    left = jnp.where(lane == 0, 0.0, pltpu.roll(mid, 1, 1))
    right = jnp.where(lane == cols - 1, 0.0, pltpu.roll(mid, cols - 1, 1))
    total = ((below + above) + (behind + ahead)) + (left + right)
    return kappa * (total - 6.0 * mid) - advect * (mid - behind)


def put_ring(ref, z, value):
    nx = value.shape[0]
    ref[z, pl.ds(8, nx)] = value
    ref[z, 7:8] = value[nx - 1 : nx]
    ref[z, 8 + nx : 9 + nx] = value[0:1]


def pair_mean(block):
    nx = block.shape[0]
    return (block[pl.ds(0, nx // 2, stride=2), :] + block[pl.ds(1, nx // 2, stride=2), :]) * 0.125


def whole(shape):
    return pl.BlockSpec(shape, lambda i, *_: (0,) * len(shape))


def node_block(j, nz, nx, ny):
    return pl.BlockSpec((1, 1, nz, nx, ny), lambda i, *_: (0, j, 0, 0, 0))


SMEM = pl.BlockSpec(memory_space=pltpu.SMEM)
VMEM = pl.BlockSpec(memory_space=pltpu.VMEM)
ANY = pl.BlockSpec(memory_space=pl.ANY)


def weigh_kernel(info, table, nodes, labels, weighted, kappa, block):
    first = (info[0] == 0).astype(F32)
    total = None
    for z in range(nodes.shape[2]):
        value = float(WEIGHTS[1]) * nodes[0, 1, z]
        for j in range(2, NODES):
            value = value + float(WEIGHTS[j]) * nodes[0, j, z]
        weighted[z] = value + (first * float(WEIGHTS[0])) * nodes[0, 0, z]
        cells = kappa_of(labels[z], table)
        total = cells if z == 0 else total + cells
    block[...] = total
    kappa[0] = pair_mean(block)


def weigh(info, table, node_fields, labels):
    _, _, nz, nx, ny = node_fields.shape
    cut = 4
    return pl.pallas_call(
        weigh_kernel,
        grid=(nz // cut,),
        in_specs=[
            SMEM, SMEM,
            pl.BlockSpec((1, NODES, cut, nx, ny), lambda i: (0, 0, i, 0, 0)),
            pl.BlockSpec((cut, nx, ny), lambda i: (i, 0, 0)),
        ],
        out_specs=[
            pl.BlockSpec((cut, nx, ny), lambda i: (i, 0, 0)),
            pl.BlockSpec((1, nx // 2, ny), lambda i: (i, 0, 0)),
        ],
        out_shape=[
            jax.ShapeDtypeStruct((nz, nx, ny), F32),
            jax.ShapeDtypeStruct((nz // 4, nx // 2, ny), F32),
        ],
        scratch_shapes=[pltpu.VMEM((nx, ny), F32)],
        compiler_params=pltpu.CompilerParams(vmem_limit_bytes=16 * MIB),
        name="weigh",
    )(info, table, node_fields, labels)


def residual_kernel(
    info, table, weighted, arrived, u0, u4, labels, label_low, label_high, shift,
    coarse, start, wide, block,
):
    nz, nx, ny = weighted.shape
    first = info[0] == 0
    advect = shift[...].astype(F32)
    w0 = float(WEIGHTS[0])
    blank = jnp.zeros((nx, ny), F32)
    wide[0, pl.ds(8, nx)] = blank
    wide[nz + 1, pl.ds(8, nx)] = blank
    for z in range(nz):
        put_ring(wide, z + 1, weighted[z] + w0 * arrived[z])
    for zb in range(nz // 4):
        total = None
        for k in range(4):
            z = 4 * zb + k
            begin = jnp.where(first, u0[0, 0, z], arrived[z])
            start[z] = begin
            value = begin - u4[0, 0, z] + rate(
                wide[z, pl.ds(8, nx)], wide[z + 1, pl.ds(8, nx)], wide[z + 2, pl.ds(8, nx)],
                wide[z + 1, pl.ds(7, nx)], wide[z + 1, pl.ds(9, nx)],
                kappa_of(labels[z], table), advect,
            )
            total = value if total is None else total + value
        block[...] = total
        coarse[zb] = pair_mean(block)
    block[...] = kappa_of(label_low[nz - 1], table) * wide[1, pl.ds(8, nx)]
    coarse[nz // 4] = pair_mean(block)
    block[...] = kappa_of(label_high[0], table) * wide[nz, pl.ds(8, nx)]
    coarse[nz // 4 + 1] = pair_mean(block)


def residual(info, table, weighted, arrived, node_fields, labels, label_low, label_high, shift):
    nz, nx, ny = weighted.shape
    slab = whole((nz, nx, ny))
    return pl.pallas_call(
        residual_kernel,
        grid=(1,),
        in_specs=[
            SMEM, SMEM, slab, slab, node_block(0, nz, nx, ny), node_block(NODES - 1, nz, nx, ny),
            slab, slab, slab, whole((1, ny)),
        ],
        out_specs=[whole((nz // 4 + 2, nx // 2, ny)), slab],
        out_shape=[
            jax.ShapeDtypeStruct((nz // 4 + 2, nx // 2, ny), F32),
            jax.ShapeDtypeStruct((nz, nx, ny), F32),
        ],
        scratch_shapes=[pltpu.VMEM((nz + 2, nx + 16, ny), F32), pltpu.VMEM((nx, ny), F32)],
        compiler_params=pltpu.CompilerParams(vmem_limit_bytes=20 * MIB),
        name="residual",
    )(info, table, weighted, arrived, node_fields, node_fields, labels, label_low, label_high, shift)


def pack_kernel(nodes, start, packed):
    for z in range(nodes.shape[2]):
        u = [start[z]] + [nodes[0, j, z] for j in range(1, NODES)]
        for m in range(STEPS):
            coef = [float(Q[m, j]) for j in range(NODES)]
            if m > 0:
                coef[m] -= float(DT[m])
            total = coef[0] * u[0]
            for j in range(1, NODES):
                total = total + coef[j] * u[j]
            packed[m, z] = total
        packed[STEPS, z] = u[0]


def pack(node_fields, start):
    _, _, nz, nx, ny = node_fields.shape
    cut = 2
    return pl.pallas_call(
        pack_kernel,
        grid=(nz // cut,),
        in_specs=[
            pl.BlockSpec((1, NODES, cut, nx, ny), lambda i: (0, 0, i, 0, 0)),
            pl.BlockSpec((cut, nx, ny), lambda i: (i, 0, 0)),
        ],
        out_specs=pl.BlockSpec((NODES, cut, nx, ny), lambda i: (0, i, 0, 0)),
        out_shape=jax.ShapeDtypeStruct((NODES, nz, nx, ny), F32),
        compiler_params=pltpu.CompilerParams(vmem_limit_bytes=16 * MIB),
        name="pack",
    )(node_fields, start)


def coarse_step(src, dst, kappa, half):
    nz, nx, ny = kappa.shape
    lane = lax.broadcasted_iota(jnp.int32, (8, ny), 1)
    for x in range(0, nx, 8):
        rows = pl.ds(8 + x, 8)
        below, mid = src[0, rows], src[1, rows]
        for z in range(nz):
            above = src[z + 2, rows]
            past = src[z + 1, pl.ds(7 + x, 8)]
            ahead = src[z + 1, pl.ds(9 + x, 8)]
            left = jnp.where(lane == 0, 0.0, pltpu.roll(mid, 1, 1))
            right = jnp.where(lane == ny - 1, 0.0, pltpu.roll(mid, ny - 1, 1))
            total = (below + above) * 0.0625 + (past + ahead) * 0.25 + ((left + right) - 2.625 * mid)
            value = mid + kappa[z, pl.ds(x, 8)] * total - half * (mid - past)
            dst[z + 1, rows] = value
            if x == 0:
                dst[z + 1, 8 + nx : 9 + nx] = value[0:1]
            if x == nx - 8:
                dst[z + 1, 7:8] = value[7:8]
            below, mid = mid, above


def clear_edges(*buffers):
    for ref in buffers:
        nz, nx = ref.shape[0] - 2, ref.shape[1] - 16
        blank = jnp.zeros((nx, ref.shape[2]), F32)
        ref[0, pl.ds(8, nx)] = blank
        ref[nz + 1, pl.ds(8, nx)] = blank


def get_layer(state, z):
    return state[z + 1, pl.ds(8, state.shape[1] - 16)]


def add_layers(state, member, nz):
    for z in range(nz):
        put_ring(state, z + 1, get_layer(state, z) + member[z])


def entry_kernel(info, gathered, shift, field, packet):
    ns, parts, nx, ny = gathered.shape
    for s in range(ns):
        low = gathered[s, 0]
        high = gathered[s, 1]
        if s > 0:
            low = low + gathered[s - 1, 3]
        if s < ns - 1:
            high = high + gathered[s + 1, 2]
        field[2 * s] = low
        field[2 * s + 1] = high
    core = info[4] % 2
    for k in range(ns):
        packet[pl.ds(k * nx, nx)] = field[core * ns + k]
    packet[pl.ds(ns * nx, 8)] = jnp.broadcast_to(shift[...].astype(F32) * 0.5, (8, ny))


def chain_entry(info, gathered, shift):
    ns, _, nx, ny = gathered.shape
    return pl.pallas_call(
        entry_kernel,
        in_specs=[SMEM, VMEM, VMEM],
        out_specs=[VMEM] * 2,
        out_shape=[
            jax.ShapeDtypeStruct((2 * ns, nx, ny), F32),
            jax.ShapeDtypeStruct((ns * nx + 8, ny), F32),
        ],
        compiler_params=pltpu.CompilerParams(vmem_limit_bytes=8 * MIB),
        name="chain_entry",
    )(info, gathered, shift)


def place(members, slot, core, mine, theirs):
    _, nz, nx, _ = members.shape
    half = nz // 2
    for k in range(half):
        members[slot, core * half + k] = mine[pl.ds(k * nx, nx)]
        members[slot, (1 - core) * half + k] = theirs[pl.ds(k * nx, nx)]


def halves_of(halves, base, ref, row, count):
    for j in range(count):
        halves[base + j] = jnp.broadcast_to(ref[row + j : row + j + 1], halves.shape[1:])


def level_kernel(length, axis, info, own, tail, before, kappa, *refs):
    packets, (packet, full, after, members, halves, ping, pong, saved) = refs[:6], refs[6:]
    nz, nx, ny = kappa.shape
    core, position = info[4] % 2, info[axis]
    inner = info[3] if length > 1 else 0
    base = nz // 2 * nx
    for z in range(nz):
        members[position, z] = own[z]
    halves_of(halves, position * length, tail, base, length)
    for k in range(1, 4):
        slot = (position + (4 - k)) % 4
        mine, theirs = packets[2 * (k - 1)], packets[2 * (k - 1) + 1]
        place(members, slot, core, mine, theirs)
        halves_of(halves, slot * length, mine, base, length)
    clear_edges(ping, pong)
    for z in range(nz):
        put_ring(ping, z + 1, members[0, z])
    saved[...] = jnp.zeros(saved.shape, F32)

    def member(group, here, there):
        for j in range(length):
            @pl.when((group == position) & (j == inner))
            def _(here=here):
                for z in range(nz):
                    saved[z] = get_layer(here, z)

            coarse_step(here, there, kappa, halves[group * length + j])
            here, there = there, here
        add_layers(here, members.at[group], nz)
        return here

    if length % 2:
        last, other = ping, pong
        for group in range(1, 4):
            last, other = member(group, last, other), last
    else:
        lax.fori_loop(1, 4, lambda group, _: (member(group, ping, pong), 0)[1], 0)
        last = ping
    after[...] = saved[...] + before[...] if length > 1 else saved[...]
    for z in range(nz):
        full[z] = get_layer(last, z)
    for k in range(nz // 2):
        packet[pl.ds(k * nx, nx)] = full[core * (nz // 2) + k]
    for j in range(4 * length):
        packet[base + j : base + j + 1] = halves[j, 0:1]
    if length == 1:
        packet[base + 4 : base + 8] = halves[0, 0:4]


def chain_level(length, axis, info, own, tail, before, kappa, packets):
    nz, nx, ny = kappa.shape
    return pl.pallas_call(
        functools.partial(level_kernel, length, axis),
        in_specs=[SMEM] + [VMEM] * (4 + len(packets)),
        out_specs=[VMEM] * 3,
        out_shape=[
            jax.ShapeDtypeStruct((nz // 2 * nx + max(8, 4 * length), ny), F32),
            jax.ShapeDtypeStruct((nz, nx, ny), F32),
            jax.ShapeDtypeStruct((nz, nx, ny), F32),
        ],
        scratch_shapes=[
            pltpu.VMEM((4, nz, nx, ny), F32),
            pltpu.VMEM((4 * length, 8, ny), F32),
            pltpu.VMEM((nz + 2, nx + 16, ny), F32),
            pltpu.VMEM((nz + 2, nx + 16, ny), F32),
            pltpu.VMEM((nz, nx, ny), F32),
        ],
        compiler_params=pltpu.CompilerParams(vmem_limit_bytes=12 * MIB),
        name=f"chain_level_{length}",
    )(info, own, tail, before, kappa, *packets)


def final_kernel(info, field, tail, before, kappa, *refs):
    packets, (coarse, members, halves, ping, pong) = refs[:6], refs[6:]
    nz, nx, ny = kappa.shape
    core, zh = info[4] % 2, info[1]
    inside = info[2] * 4 + info[3]
    base = nz // 2 * nx
    halves_of(halves, zh * 16, tail, base, 16)
    for k in range(1, 4):
        slot = (zh + (4 - k)) % 4
        mine, theirs = packets[2 * (k - 1)], packets[2 * (k - 1) + 1]
        place(members, slot, core, mine, theirs)
        halves_of(halves, slot * 16, mine, base, 16)
    begin = zh * 16
    clear_edges(ping, pong)
    for z in range(nz):
        put_ring(ping, z + 1, jnp.where(zh > 0, members[0, z], 0.0))

    def pair(t, _):
        coarse_step(ping, pong, kappa, halves[2 * t])
        coarse_step(pong, ping, kappa, halves[2 * t + 1])
        return 0

    def group(g, _):
        lax.fori_loop(8 * g, 8 * g + 8, pair, 0)
        add_layers(ping, members.at[g], nz)
        return 0

    lax.fori_loop(1, zh, group, 0)

    @pl.when(zh > 0)
    def _():
        lax.fori_loop(8 * zh, 8 * zh + inside // 2, pair, 0)

        @pl.when(inside % 2 == 1)
        def _():
            coarse_step(ping, pong, kappa, halves[begin + inside - 1])
            for z in range(nz):
                put_ring(ping, z + 1, get_layer(pong, z))

    add_layers(ping, before, nz)
    coarse_step(ping, pong, kappa, halves[begin + inside])
    blank = jnp.zeros((nx, ny), F32)
    for f in range(2):
        for edge in range(2):
            coarse[f, edge] = blank
            coarse[f, nz + 2 + edge] = blank
    for z in range(nz):
        value = get_layer(ping, z)
        coarse[0, z + 2] = value
        coarse[1, z + 2] = get_layer(pong, z) + field[z] - value


def chain_final(info, field, tail, before, kappa, packets):
    nz, nx, ny = kappa.shape
    return pl.pallas_call(
        final_kernel,
        in_specs=[SMEM] + [VMEM] * (4 + len(packets)),
        out_specs=VMEM,
        out_shape=jax.ShapeDtypeStruct((2, nz + 4, nx, ny), F32),
        scratch_shapes=[
            pltpu.VMEM((4, nz, nx, ny), F32),
            pltpu.VMEM((64, 8, ny), F32),
            pltpu.VMEM((nz + 2, nx + 16, ny), F32),
            pltpu.VMEM((nz + 2, nx + 16, ny), F32),
        ],
        compiler_params=pltpu.CompilerParams(vmem_limit_bytes=12 * MIB),
        name="chain_final",
    )(info, field, tail, before, kappa, *packets)


CHUNK = 32


def sweeps_kernel(
    info, table, coarse, own, low, high, labels, labels_low, labels_high, shift, out,
    held, marks, lift, kappa, first, mixed_a, mixed_b, *rest,
):
    fields, second, (sems, out_sems) = rest[:STEPS], rest[STEPS : 2 * STEPS], rest[2 * STEPS :]
    mixed = (mixed_a, mixed_b)
    nz, nx, ny = labels.shape
    wide = 3 * nz
    space = info[4]
    copies = []
    for k, (src, mark) in enumerate(((low, labels_low), (own, labels), (high, labels_high))):
        copies.append(
            pltpu.make_async_copy(mark, marks.at[pl.ds(k * nz, nz)], sems.at[2 * k])
        )
        copies.append(
            pltpu.make_async_copy(src, held.at[:, pl.ds(k * nz, nz)], sems.at[2 * k + 1])
        )
    for copy in copies:
        copy.start()
    advect = jnp.broadcast_to(shift[...].astype(F32), (CHUNK, ny))
    for f in range(2):
        for k in range(wide // 4):
            value = coarse[f, space * (nz // 4) + k]
            lift[f, k, pl.ds(0, nx // 2, stride=2), :] = value
            lift[f, k, pl.ds(1, nx // 2, stride=2), :] = value
    for copy in copies:
        copy.wait()

    def layers(low, high, body):
        lax.fori_loop(low, high, lambda z, _: (body(z), 0)[1], 0, unroll=True)

    def mix(slot, z, c, value):
        ref = mixed[slot]
        ref[z, pl.ds(8 + c, CHUNK)] = value
        if c == 0:
            ref[z, 8 + nx : 9 + nx] = value[0:1]
        if c == nx - CHUNK:
            ref[z, 7:8] = value[CHUNK - 1 : CHUNK]

    def opening(z):
        inside = ((z >= nz) | (space > 0)) & ((z < 2 * nz) | (space < 3))
        at = z // 4
        for c in range(0, nx, CHUNK):
            rows = pl.ds(c, CHUNK)
            kappa[z, rows] = jnp.where(inside, kappa_of(marks[z, rows], table), 0.0)
            begin, grow = lift[0, at, rows], lift[1, at, rows]
            first[z, rows] = held[STEPS, z, rows] + begin
            value = held[0, z, rows] + float(DT[0]) * begin + float(0.5 * DT[0] ** 2) * grow
            mix(0, z, c, value)

    layers(0, wide, opening)

    def later_sum(m, z, rows, newest):
        total = None
        for j in range(NODES):
            coef = float(Q[m, j] - (DT[m] if m == j else 0.0))
            node = first[z, rows] if j == 0 else fields[j - 1][z, rows]
            if j == NODES - 1 and newest is not None:
                node = newest
            total = coef * node if total is None else total + coef * node
        return total

    outs = [pltpu.make_async_copy(first.at[pl.ds(nz, nz)], out.at[0, 0], out_sems.at[0])]
    outs[0].start()
    for turn in range(2 * STEPS):
        sweep, m = turn // STEPS, turn % STEPS
        past = first if m == 0 else (fields if sweep == 0 else second)[m - 1]
        target = (fields if sweep == 0 else second)[m]
        now, later = turn % 2, (turn + 1) % 2

        def stage(z, turn=turn, sweep=sweep, m=m, past=past, target=target, now=now, later=later):
            source = mixed[now]
            for c in range(0, nx, CHUNK):
                rows, inner = pl.ds(c, CHUNK), pl.ds(8 + c, CHUNK)
                value = past[z, rows] + rate(
                    source[z - 1, inner], source[z, inner], source[z + 1, inner],
                    source[z, pl.ds(7 + c, CHUNK)], source[z, pl.ds(9 + c, CHUNK)],
                    kappa[z, rows], advect,
                )
                target[z, rows] = value
                if turn == 2 * STEPS - 1:
                    continue
                if turn < STEPS - 1:
                    blend = (
                        float(DT[m + 1]) * value
                        + held[m + 1, z, rows]
                        + float(0.5 * DT[m + 1] ** 2) * lift[1, z // 4, rows]
                    )
                elif turn == STEPS - 1:
                    blend = later_sum(0, z, rows, value) + float(DT[0]) * first[z, rows]
                else:
                    blend = later_sum(m + 1, z, rows, None) + float(DT[m + 1]) * value
                mix(later, z, c, blend)

        layers(turn + 1, wide - 1 - turn, stage)
        if sweep == 1:
            copy = pltpu.make_async_copy(
                target.at[pl.ds(nz, nz)], out.at[0, m + 1], out_sems.at[m + 1]
            )
            copy.start()
            outs.append(copy)
    for copy in outs:
        copy.wait()


def fine_sweeps(info, table, coarse, own, low, high, labels, labels_low, labels_high, shift):
    nz, nx, ny = labels.shape
    wide = 3 * nz
    return pl.pallas_call(
        sweeps_kernel,
        in_specs=[SMEM, SMEM, VMEM] + [ANY] * 6 + [VMEM],
        out_specs=ANY,
        out_shape=jax.ShapeDtypeStruct((1, NODES, nz, nx, ny), F32),
        scratch_shapes=[
            pltpu.VMEM((NODES, wide, nx, ny), F32),
            pltpu.VMEM((wide, nx, ny), jnp.int32),
            pltpu.VMEM((2, wide // 4, nx, ny), F32),
            pltpu.VMEM((wide, nx, ny), F32),
            pltpu.VMEM((wide, nx, ny), F32),
            pltpu.VMEM((wide, nx + 16, ny), F32),
            pltpu.VMEM((wide, nx + 16, ny), F32),
        ]
        + [pltpu.VMEM((wide, nx, ny), F32)] * (2 * STEPS)
        + [
            pltpu.SemaphoreType.DMA((6,)),
            pltpu.SemaphoreType.DMA((NODES,)),
        ],
        compiler_params=pltpu.CompilerParams(vmem_limit_bytes=36 * MIB),
        name="fine_sweeps",
    )(info, table, coarse, own, low, high, labels, labels_low, labels_high, shift)


def to_space(value, by):
    return lax.ppermute(value, "space", [(i, i + by) for i in range(4) if 0 <= i + by < 4])


def to_next(value, by):
    axes = TM + ("space",)
    pairs = [
        (4 * n + s, 4 * (n + 1) + s + by) for n in range(63) for s in range(4) if 0 <= s + by < 4
    ]
    return lax.ppermute(value, axes, pairs)


def swap_core(value):
    return lax.ppermute(value, "space", [(0, 1), (1, 0), (2, 3), (3, 2)])


def gather_axis(packet, axis):
    packets = []
    for k in range(1, 4):
        got = lax.ppermute(packet, axis, [(i, (i + k) % 4) for i in range(4)])
        packets += [got, swap_core(got)]
    return packets


def shards(node_fields, region_label, sheet_shift, diffusivity):
    zh, y, x = (lax.axis_index(a) for a in TM)
    space = lax.axis_index("space")
    info = jnp.stack([zh * 16 + y * 4 + x, zh, y, x, space]).astype(jnp.int32)
    arrived = to_next(node_fields[0, NODES - 1], 0)
    labels_low, labels_high = to_space(region_label, 1), to_space(region_label, -1)
    weighted, kappa = weigh(info, diffusivity, node_fields, region_label)
    kappa = lax.all_gather(kappa, "space", axis=0, tiled=True)
    weighted, kappa = lax.optimization_barrier((weighted, kappa))
    coarse, start = residual(
        info, diffusivity, weighted, arrived, node_fields, region_label, labels_low, labels_high,
        sheet_shift,
    )
    gathered = lax.all_gather(coarse, "space", axis=0, tiled=False)
    field, packet = chain_entry(info, gathered, sheet_shift)
    packets = gather_axis(packet, "x")
    start, _ = lax.optimization_barrier((start, packet))
    packed = pack(node_fields, start)
    packed, packets[4] = lax.optimization_barrier((packed, packets[4]))
    packed_low, packed_high = to_space(packed, 1), to_space(packed, -1)
    packet, field4, prefix = chain_level(1, 3, info, field, packet, field, kappa, packets)
    packets = gather_axis(packet, "y")
    packet, _, prefix = chain_level(4, 2, info, field4, packet, prefix, kappa, packets)
    packets = gather_axis(packet, "zh")
    correction = chain_final(info, field, packet, prefix, kappa, packets)
    return fine_sweeps(
        info, diffusivity, correction, packed, packed_low, packed_high,
        region_label, labels_low, labels_high, sheet_shift,
    )


def solution(mesh):
    grid = Mesh(mesh.devices.reshape(4, 4, 4, 4), TM + ("space",))
    in_specs = (P(TM, None, "space", None, None), P("space", None, None), P(TM, None), P())
    out_specs = P(TM, None, "space", None, None)
    return jax.shard_map(shards, mesh=grid, in_specs=in_specs, out_specs=out_specs, check_vma=False)
```

time: 1310 us -> 122 us (0.09)
  the two profiles are of different devices: /device:TPU:160 before, /device:TPU:217 now
where the time goes in v2:
time: 122 us
  starting transfers between devices  54.1 us (44%)
  Pallas kernels  27.5 us (23%)
  waiting for transfers between devices  21.8 us (18%)
  blocking collectives  13.2 us (11%)
  local copies, waits for them, and re-layouts  4.67 us (4%)
    ppermute x9, starting transfers between devices, gather_axis(): got = lax.ppermute(packet, axis, [(i, (i + k) % 4) for i in range(4)])  31.3 us
    ppermute x9, waiting for transfers between devices, gather_axis(): got = lax.ppermute(packet, axis, [(i, (i + k) % 4) for i in range(4)])  17.8 us
    ppermute x4, starting transfers between devices, to_space(): lax.ppermute(value, 'space', [(i, i + by) for i in range(4) if 0 <= i + b...  13.9 us
    pallas_call x1, Pallas kernels, chain_final(): pl.pallas_call(final_kernel, in_specs=[SMEM] + [VMEM] * (4 + len(packets)...  9.16 us
    pallas_call x1, Pallas kernels, fine_sweeps(): pl.pallas_call(sweeps_kernel, in_specs=[SMEM, SMEM, VMEM] + [ANY] * 6 + [...  8.88 us
    all_gather x1, blocking collectives, shards(): gathered = lax.all_gather(coarse, 'space', axis=0, tiled=False)  7.29 us
    all_gather x1, blocking collectives, shards(): kappa = lax.all_gather(kappa, 'space', axis=0, tiled=True)  5.86 us
    ppermute x9, starting transfers between devices, swap_core(): return lax.ppermute(value, 'space', [(0, 1), (1, 0), (2, 3), (3, 2)])  5.75 us
  transfers between devices with their start and end apart: 23, of which 11 were waited for; matrix products, arithmetic and copies ran while one was open for 0% of the time, Pallas kernels for 14%

profile of v2, /device:TPU:217, one launch (start us, length us, event | category | flops | bytes accessed | tf_op | source)
XLA Modules:
  0.0 121.6 jit_solution(14732885770951880018)
XLA Ops:
  0.0 1.1 slice_bitcast_fusion
  1.2 3.1 %collective-permute-start = (f32[8,128,128]{2,1,0:T(8,128)S(1)}, f32[8,128,128]{2,1,0:T(8,128)S(1)}, u32[]{:S(2)}, u32[]{:S(2)}) collective-permute-start(f32[8,128,128]{2,1,0:T(8,128)S(1)} %slice_bitcast_fusion), channel_id=1, source_target_pairs={{0,4},{1,5},{2,6},{3,7},{4,8},{5,9},{6,10},{7,11},{8,12},{9,13},{1... | collective-permute-start | bytes 1572872 | tf_op jit(solution)/shard_map/ppermute | solution.py:588
  4.3 2.9 %collective-permute-start.2 = (s32[8,128,128]{2,1,0:T(8,128)}, s32[8,128,128]{2,1,0:T(8,128)S(1)}, u32[]{:S(2)}, u32[]{:S(2)}) collective-permute-start(s32[8,128,128]{2,1,0:T(8,128)} %labels.5), channel_id=1, source_target_pairs={{1,0},{2,1},{3,2},{5,4},{6,5},{7,6},{9,8},{10,9},{11,10},{13,12},{... | collective-permute-start | bytes 1572872 | tf_op jit(solution)/shard_map/ppermute | solution.py:580
  7.2 2.7 %collective-permute-start.1 = (s32[8,128,128]{2,1,0:T(8,128)}, s32[8,128,128]{2,1,0:T(8,128)S(1)}, u32[]{:S(2)}, u32[]{:S(2)}) collective-permute-start(s32[8,128,128]{2,1,0:T(8,128)} %labels.5), channel_id=1, source_target_pairs={{0,1},{1,2},{2,3},{4,5},{5,6},{6,7},{8,9},{9,10},{10,11},{12,13},{... | collective-permute-start | bytes 1572872 | tf_op jit(solution)/shard_map/ppermute | solution.py:580
  9.9 0.1 stack.23.info
  10.0 1.7 %copy-done = f32[1,5,8,128,128]{4,3,2,1,0:T(8,128)S(1)} copy-done((f32[1,5,8,128,128]{4,3,2,1,0:T(8,128)S(1)}, f32[1,5,8,128,128]{4,3,2,1,0:T(8,128)}, u32[]{:S(2)}) %copy-start) | copy-done | bytes 2621464
  11.7 1.0 copy-done.2
  12.7 0.7 copy-done.4
  13.4 1.0 weigh.1
  14.4 5.9 %all_gather.9.kappa = f32[8,64,128]{2,1,0:T(8,128)S(1)} all-gather(f32[2,64,128]{2,1,0:T(8,128)S(1)} %get-tuple-element.22), channel_id=1, replica_groups=mesh['zh'=4,'y'=4,'x'=4,'space'=4] {'space'}, dimensions={0}, use_global_device_ids=true | all-gather | bytes 327680 | tf_op jit(solution)/shard_map/all_gather | solution.py:610
  20.3 0.0 collective-permute-done.arrived
  20.3 0.0 collective-permute-done.2.label_high.labels_high
  20.3 0.0 collective-permute-done.1.label_low.labels_low
  20.4 1.2 residual.1
  21.6 7.3 %all-gather = f32[16,64,128]{2,1,0:T(8,128)S(1)} all-gather(f32[4,64,128]{2,1,0:T(8,128)S(1)} %get-tuple-element.24), channel_id=2, replica_groups=mesh['zh'=4,'y'=4,'x'=4,'space'=4] {'space'}, dimensions={0}, use_global_device_ids=true | all-gather | bytes 655360 | tf_op jit(solution)/shard_map/all_gather | solution.py:616
  28.9 0.6 chain_entry.1
  29.4 2.9 %collective-permute-start.7 = (f32[264,128]{1,0:T(8,128)S(1)}, f32[264,128]{1,0:T(8,128)S(1)}, u32[]{:S(2)}, u32[]{:S(2)}) collective-permute-start(f32[264,128]{1,0:T(8,128)S(1)} %get-tuple-element.26.tail), channel_id=1, source_target_pairs={{0,12},{4,0},{8,4},{12,8},{1,13},{5,1},{9,5},{13,9},{2,14},{6,2},{... | collective-permute-start | bytes 405512 | tf_op jit(solution)/shard_map/ppermute | solution.py:598
  32.4 1.2 pack.1.own
  33.6 1.3 %collective-permute-done.7.refs_4_ = f32[264,128]{1,0:T(8,128)S(1)} collective-permute-done((f32[264,128]{1,0:T(8,128)S(1)}, f32[264,128]{1,0:T(8,128)S(1)}, u32[]{:S(2)}, u32[]{:S(2)}) %collective-permute-start.7) | collective-permute-done | bytes 135200 | tf_op jit(solution)/shard_map/ppermute | solution.py:598
  34.9 3.2 %collective-permute-start.22 = (f32[5,8,128,128]{3,2,1,0:T(8,128)S(1)}, f32[5,8,128,128]{3,2,1,0:T(8,128)S(1)}, u32[]{:S(2)}, u32[]{:S(2)}) collective-permute-start(f32[5,8,128,128]{3,2,1,0:T(8,128)S(1)} %pack.1.own), channel_id=1, source_target_pairs={{1,0},{2,1},{3,2},{5,4},{6,5},{7,6},{9,8},{10,9},{11,10},{13,12},{... | collective-permute-start | bytes 7864328 | tf_op jit(solution)/shard_map/ppermute | solution.py:580
  38.1 5.2 %collective-permute-start.21 = (f32[5,8,128,128]{3,2,1,0:T(8,128)S(1)}, f32[5,8,128,128]{3,2,1,0:T(8,128)S(1)}, u32[]{:S(2)}, u32[]{:S(2)}) collective-permute-start(f32[5,8,128,128]{3,2,1,0:T(8,128)S(1)} %pack.1.own), channel_id=1, source_target_pairs={{0,1},{1,2},{2,3},{4,5},{5,6},{6,7},{8,9},{9,10},{10,11},{12,13},{... | collective-permute-start | bytes 7864328 | tf_op jit(solution)/shard_map/ppermute | solution.py:580
  43.2 2.0 %collective-permute-start.5 = (f32[264,128]{1,0:T(8,128)S(1)}, f32[264,128]{1,0:T(8,128)S(1)}, u32[]{:S(2)}, u32[]{:S(2)}) collective-permute-start(f32[264,128]{1,0:T(8,128)S(1)} %get-tuple-element.26.tail), channel_id=1, source_target_pairs={{0,8},{4,12},{8,0},{12,4},{1,9},{5,13},{9,1},{13,5},{2,10},{6,14},... | collective-permute-start | bytes 405512 | tf_op jit(solution)/shard_map/ppermute | solution.py:598
  45.3 2.1 %collective-permute-start.3 = (f32[264,128]{1,0:T(8,128)S(1)}, f32[264,128]{1,0:T(8,128)S(1)}, u32[]{:S(2)}, u32[]{:S(2)}) collective-permute-start(f32[264,128]{1,0:T(8,128)S(1)} %get-tuple-element.26.tail), channel_id=1, source_target_pairs={{0,4},{4,8},{8,12},{12,0},{1,5},{5,9},{9,13},{13,1},{2,6},{6,10},{... | collective-permute-start | bytes 405512 | tf_op jit(solution)/shard_map/ppermute | solution.py:598
  47.3 2.5 %collective-permute-done.5.refs_2_ = f32[264,128]{1,0:T(8,128)S(1)} collective-permute-done((f32[264,128]{1,0:T(8,128)S(1)}, f32[264,128]{1,0:T(8,128)S(1)}, u32[]{:S(2)}, u32[]{:S(2)}) %collective-permute-start.5) | collective-permute-done | bytes 135200 | tf_op jit(solution)/shard_map/ppermute | solution.py:598
  49.8 1.6 %collective-permute-done.3.refs_0_ = f32[264,128]{1,0:T(8,128)S(1)} collective-permute-done((f32[264,128]{1,0:T(8,128)S(1)}, f32[264,128]{1,0:T(8,128)S(1)}, u32[]{:S(2)}, u32[]{:S(2)}) %collective-permute-start.3) | collective-permute-done | bytes 135200 | tf_op jit(solution)/shard_map/ppermute | solution.py:598
  51.4 1.3 %collective-permute-done.4.refs_1_ = f32[264,128]{1,0:T(8,128)S(1)} collective-permute-done((f32[264,128]{1,0:T(8,128)S(1)}, f32[264,128]{1,0:T(8,128)S(1)}, u32[]{:S(2)}, u32[]{:S(2)}) %collective-permute-start.4) | collective-permute-done | bytes 135200 | tf_op jit(solution)/shard_map/ppermute | solution.py:592
  52.7 1.4 %chain_level_1.1 = (f32[264,128]{1,0:T(8,128)S(1)}, f32[8,64,128]{2,1,0:T(8,128)S(1)}, f32[8,64,128]{2,1,0:T(8,128)S(1)}) custom-call(s32[5]{0:T(128)S(1)} %stack.23.info, f32[8,64,128]{2,1,0:T(8,128)S(1)} %get-tuple-element.25.own.before.field, f32[264,128]{1,0:T(8,128)S(1)} %get-tuple-element.26.tail, ...), custom_call_target="tpu_custom_call" | custom-call | tf_op jit(solution)/shard_map/chain_level_1/pallas_call | solution.py:353
  54.1 0.1 collective-permute-start.13
  54.2 13.5 %collective-permute-start.11 = (f32[264,128]{1,0:T(8,128)S(1)}, f32[264,128]{1,0:T(8,128)S(1)}, u32[]{:S(2)}, u32[]{:S(2)}) collective-permute-start(f32[264,128]{1,0:T(8,128)S(1)} %get-tuple-element.32.tail), channel_id=1, source_target_pairs={{0,32},{16,48},{32,0},{48,16},{1,33},{17,49},{33,1},{49,17},{2,34}... | collective-permute-start | bytes 405512 | tf_op jit(solution)/shard_map/ppermute | solution.py:598
  67.7 2.5 %collective-permute-done.13.refs_4_ = f32[264,128]{1,0:T(8,128)S(1)} collective-permute-done((f32[264,128]{1,0:T(8,128)S(1)}, f32[264,128]{1,0:T(8,128)S(1)}, u32[]{:S(2)}, u32[]{:S(2)}) %collective-permute-start.13) | collective-permute-done | bytes 135200 | tf_op jit(solution)/shard_map/ppermute | solution.py:598
  70.2 0.9 collective-permute-start.14
  71.0 2.9 %collective-permute-done.11.refs_2_ = f32[264,128]{1,0:T(8,128)S(1)} collective-permute-done((f32[264,128]{1,0:T(8,128)S(1)}, f32[264,128]{1,0:T(8,128)S(1)}, u32[]{:S(2)}, u32[]{:S(2)}) %collective-permute-start.11) | collective-permute-done | bytes 135200 | tf_op jit(solution)/shard_map/ppermute | solution.py:598
  73.9 1.2 collective-permute-start.12
  75.1 0.0 collective-permute-start.10
  75.1 1.0 collective-permute-done.12.refs_3_
  76.1 0.4 collective-permute-done.10.refs_1_
  76.5 4.1 %chain_level_4.1 = (f32[272,128]{1,0:T(8,128)S(1)}, f32[8,64,128]{2,1,0:T(8,128)}, f32[8,64,128]{2,1,0:T(8,128)S(1)}) custom-call(s32[5]{0:T(128)S(1)} %stack.23.info, f32[8,64,128]{2,1,0:T(8,128)S(1)} %get-tuple-element.31.own, f32[264,128]{1,0:T(8,128)S(1)} %get-tuple-element.32.tail, f32[8,64,128]{2,1,0:T(8,128)S(1)} %get-tuple-element.33.before, ...), custom_call_target="tpu_custom_call" | custom-call | tf_op jit(solution)/shard_map/chain_level_4/pallas_call | solution.py:353
  80.5 5.2 %collective-permute-start.19 = (f32[272,128]{1,0:T(8,128)S(1)}, f32[272,128]{1,0:T(8,128)S(1)}, u32[]{:S(2)}, u32[]{:S(2)}) collective-permute-start(f32[272,128]{1,0:T(8,128)S(1)} %get-tuple-element.34.tail), channel_id=1, source_target_pairs={{0,192},{64,0},{128,64},{192,128},{1,193},{65,1},{129,65},{193,129... | collective-permute-start | bytes 417800 | tf_op jit(solution)/shard_map/ppermute | solution.py:598
  85.8 2.0 %collective-permute-start.17 = (f32[272,128]{1,0:T(8,128)S(1)}, f32[272,128]{1,0:T(8,128)S(1)}, u32[]{:S(2)}, u32[]{:S(2)}) collective-permute-start(f32[272,128]{1,0:T(8,128)S(1)} %get-tuple-element.34.tail), channel_id=1, source_target_pairs={{0,128},{64,192},{128,0},{192,64},{1,129},{65,193},{129,1},{193,65... | collective-permute-start | bytes 417800 | tf_op jit(solution)/shard_map/ppermute | solution.py:598
  87.7 3.6 %collective-permute-start.15 = (f32[272,128]{1,0:T(8,128)S(1)}, f32[272,128]{1,0:T(8,128)S(1)}, u32[]{:S(2)}, u32[]{:S(2)}) collective-permute-start(f32[272,128]{1,0:T(8,128)S(1)} %get-tuple-element.34.tail), channel_id=1, source_target_pairs={{0,64},{64,128},{128,192},{192,0},{1,65},{65,129},{129,193},{193,1... | collective-permute-start | bytes 417800 | tf_op jit(solution)/shard_map/ppermute | solution.py:598
  91.3 1.2 collective-permute-start.20
  92.5 7.0 %collective-permute-done.17.refs_2_ = f32[272,128]{1,0:T(8,128)S(1)} collective-permute-done((f32[272,128]{1,0:T(8,128)S(1)}, f32[272,128]{1,0:T(8,128)S(1)}, u32[]{:S(2)}, u32[]{:S(2)}) %collective-permute-start.17) | collective-permute-done | bytes 139296 | tf_op jit(solution)/shard_map/ppermute | solution.py:598
  99.5 2.5 %collective-permute-start.18 = (f32[272,128]{1,0:T(8,128)S(1)}, f32[272,128]{1,0:T(8,128)S(1)}, u32[]{:S(2)}, u32[]{:S(2)}) collective-permute-start(f32[272,128]{1,0:T(8,128)S(1)} %collective-permute-done.17.refs_2_), channel_id=1, source_target_pairs={{0,1},{1,0},{2,3},{3,2},{4,5},{5,4},{6,7},{7,6},{8,9},{9,8},{10,11... | collective-permute-start | bytes 417800 | tf_op jit(solution)/shard_map/ppermute | solution.py:592
  102.0 0.0 collective-permute-start.16
  102.0 1.0 collective-permute-done.18.refs_3_
  103.0 0.4 collective-permute-done.16.refs_1_
  103.4 9.2 %chain_final.1.coarse = f32[2,12,64,128]{3,2,1,0:T(8,128)S(1)} custom-call(s32[5]{0:T(128)S(1)} %stack.23.info, f32[8,64,128]{2,1,0:T(8,128)S(1)} %get-tuple-element.25.own.before.field, f32[272,128]{1,0:T(8,128)S(1)} %get-tuple-element.34.tail, f32[8,64,128]{2,1,0:T(8,128)S(1)} %get-tuple-element.35.before, f32[8,64,128]{2,1,0:T(8,128)S(1)} %all_gather.9.kappa, ...), custom_call_target="tpu_custom_call" | custom-call | tf_op jit(solution)/shard_map/chain_final/pallas_call | solution.py:428
  112.5 8.9 %fine_sweeps.1 = f32[1,5,8,128,128]{4,3,2,1,0:T(8,128)} custom-call(s32[5]{0:T(128)S(1)} %stack.23.info, f32[4]{0:T(128)S(1)} %copy-done.5, f32[2,12,64,128]{3,2,1,0:T(8,128)S(1)} %chain_final.1.coarse, f32[5,8,128,128]{3,2,1,0:T(8,128)S(1)} %pack.1.own, f32[5,8,128,128]{3,2,1,0:T(8,128)S(1)} %collective-permute-done.21.low, ...), custom_call_target="tpu_custom_call" | custom-call | tf_op jit(solution)/shard_map/fine_sweeps/pallas_call | solution.py:555
  (24 shorter events, 0.1 us)
Async XLA Ops:
  0.0 20.3 %copy-start.3 = (s32[8,128,128]{2,1,0:T(8,128)S(1)}, s32[8,128,128]{2,1,0:T(8,128)}, u32[]{:S(2)}) copy-start(s32[8,128,128]{2,1,0:T(8,128)} %labels.5) | copy-start | bytes 1572868
  0.0 20.3 %copy-start.5 = (f32[4]{0:T(128)S(1)}, f32[4]{0:T(128)}, u32[]{:S(2)}) copy-start(f32[4]{0:T(128)} %table.5) | copy-start | bytes 52
  0.0 20.3 %copy-start.6 = (s32[1,128]{1,0:T(1,128)S(1)}, s32[1,128]{1,0:T(1,128)}, u32[]{:S(2)}) copy-start(s32[1,128]{1,0:T(1,128)} %shift.5) | copy-start | bytes 1540
  1.2 19.2 %collective-permute-start = (f32[8,128,128]{2,1,0:T(8,128)S(1)}, f32[8,128,128]{2,1,0:T(8,128)S(1)}, u32[]{:S(2)}, u32[]{:S(2)}) collective-permute-start(f32[8,128,128]{2,1,0:T(8,128)S(1)} %slice_bitcast_fusion), channel_id=1, source_target_pairs={{0,4},{1,5},{2,6},{3,7},{4,8},{5,9},{6,10},{7,11},{8,12},{9,13},{1... | collective-permute-start | bytes 1572872 | tf_op jit(solution)/shard_map/ppermute | solution.py:588
  4.3 16.0 %collective-permute-start.2 = (s32[8,128,128]{2,1,0:T(8,128)}, s32[8,128,128]{2,1,0:T(8,128)S(1)}, u32[]{:S(2)}, u32[]{:S(2)}) collective-permute-start(s32[8,128,128]{2,1,0:T(8,128)} %labels.5), channel_id=1, source_target_pairs={{1,0},{2,1},{3,2},{5,4},{6,5},{7,6},{9,8},{10,9},{11,10},{13,12},{... | collective-permute-start | bytes 1572872 | tf_op jit(solution)/shard_map/ppermute | solution.py:580
  7.2 13.2 %collective-permute-start.1 = (s32[8,128,128]{2,1,0:T(8,128)}, s32[8,128,128]{2,1,0:T(8,128)S(1)}, u32[]{:S(2)}, u32[]{:S(2)}) collective-permute-start(s32[8,128,128]{2,1,0:T(8,128)} %labels.5), channel_id=1, source_target_pairs={{0,1},{1,2},{2,3},{4,5},{5,6},{6,7},{8,9},{9,10},{10,11},{12,13},{... | collective-permute-start | bytes 1572872 | tf_op jit(solution)/shard_map/ppermute | solution.py:580
  10.0 1.7 %copy-start = (f32[1,5,8,128,128]{4,3,2,1,0:T(8,128)S(1)}, f32[1,5,8,128,128]{4,3,2,1,0:T(8,128)}, u32[]{:S(2)}) copy-start(f32[1,5,8,128,128]{4,3,2,1,0:T(8,128)} %nodes.3) | copy-start | bytes 7864324
  11.7 1.0 copy-start.2
  12.7 0.7 copy-start.4
  13.4 7.0 %copy-start.1 = (f32[1,5,8,128,128]{4,3,2,1,0:T(8,128)S(1)}, f32[1,5,8,128,128]{4,3,2,1,0:T(8,128)}, u32[]{:S(2)}) copy-start(f32[1,5,8,128,128]{4,3,2,1,0:T(8,128)} %nodes.3) | copy-start | bytes 7864324
  29.4 5.4 %collective-permute-start.7 = (f32[264,128]{1,0:T(8,128)S(1)}, f32[264,128]{1,0:T(8,128)S(1)}, u32[]{:S(2)}, u32[]{:S(2)}) collective-permute-start(f32[264,128]{1,0:T(8,128)S(1)} %get-tuple-element.26.tail), channel_id=1, source_target_pairs={{0,12},{4,0},{8,4},{12,8},{1,13},{5,1},{9,5},{13,9},{2,14},{6,2},{... | collective-permute-start | bytes 405512 | tf_op jit(solution)/shard_map/ppermute | solution.py:598
  34.9 77.7 %collective-permute-start.22 = (f32[5,8,128,128]{3,2,1,0:T(8,128)S(1)}, f32[5,8,128,128]{3,2,1,0:T(8,128)S(1)}, u32[]{:S(2)}, u32[]{:S(2)}) collective-permute-start(f32[5,8,128,128]{3,2,1,0:T(8,128)S(1)} %pack.1.own), channel_id=1, source_target_pairs={{1,0},{2,1},{3,2},{5,4},{6,5},{7,6},{9,8},{10,9},{11,10},{13,12},{... | collective-permute-start | bytes 7864328 | tf_op jit(solution)/shard_map/ppermute | solution.py:580
  38.1 74.5 %collective-permute-start.21 = (f32[5,8,128,128]{3,2,1,0:T(8,128)S(1)}, f32[5,8,128,128]{3,2,1,0:T(8,128)S(1)}, u32[]{:S(2)}, u32[]{:S(2)}) collective-permute-start(f32[5,8,128,128]{3,2,1,0:T(8,128)S(1)} %pack.1.own), channel_id=1, source_target_pairs={{0,1},{1,2},{2,3},{4,5},{5,6},{6,7},{8,9},{9,10},{10,11},{12,13},{... | collective-permute-start | bytes 7864328 | tf_op jit(solution)/shard_map/ppermute | solution.py:580
  43.2 6.5 %collective-permute-start.5 = (f32[264,128]{1,0:T(8,128)S(1)}, f32[264,128]{1,0:T(8,128)S(1)}, u32[]{:S(2)}, u32[]{:S(2)}) collective-permute-start(f32[264,128]{1,0:T(8,128)S(1)} %get-tuple-element.26.tail), channel_id=1, source_target_pairs={{0,8},{4,12},{8,0},{12,4},{1,9},{5,13},{9,1},{13,5},{2,10},{6,14},... | collective-permute-start | bytes 405512 | tf_op jit(solution)/shard_map/ppermute | solution.py:598
  45.3 6.1 %collective-permute-start.3 = (f32[264,128]{1,0:T(8,128)S(1)}, f32[264,128]{1,0:T(8,128)S(1)}, u32[]{:S(2)}, u32[]{:S(2)}) collective-permute-start(f32[264,128]{1,0:T(8,128)S(1)} %get-tuple-element.26.tail), channel_id=1, source_target_pairs={{0,4},{4,8},{8,12},{12,0},{1,5},{5,9},{9,13},{13,1},{2,6},{6,10},{... | collective-permute-start | bytes 405512 | tf_op jit(solution)/shard_map/ppermute | solution.py:598
  47.3 4.1 %collective-permute-start.8 = (f32[264,128]{1,0:T(8,128)S(1)}, f32[264,128]{1,0:T(8,128)S(1)}, u32[]{:S(2)}, u32[]{:S(2)}) collective-permute-start(f32[264,128]{1,0:T(8,128)S(1)} %collective-permute-done.7.refs_4_), channel_id=1, source_target_pairs={{0,1},{1,0},{2,3},{3,2},{4,5},{5,4},{6,7},{7,6},{8,9},{9,8},{10,11... | collective-permute-start | bytes 405512 | tf_op jit(solution)/shard_map/ppermute | solution.py:592
  49.8 1.6 %collective-permute-start.6 = (f32[264,128]{1,0:T(8,128)S(1)}, f32[264,128]{1,0:T(8,128)S(1)}, u32[]{:S(2)}, u32[]{:S(2)}) collective-permute-start(f32[264,128]{1,0:T(8,128)S(1)} %collective-permute-done.5.refs_2_), channel_id=1, source_target_pairs={{0,1},{1,0},{2,3},{3,2},{4,5},{5,4},{6,7},{7,6},{8,9},{9,8},{10,11... | collective-permute-start | bytes 405512 | tf_op jit(solution)/shard_map/ppermute | solution.py:592
  51.4 1.4 %collective-permute-start.4 = (f32[264,128]{1,0:T(8,128)S(1)}, f32[264,128]{1,0:T(8,128)S(1)}, u32[]{:S(2)}, u32[]{:S(2)}) collective-permute-start(f32[264,128]{1,0:T(8,128)S(1)} %collective-permute-done.3.refs_0_), channel_id=1, source_target_pairs={{0,1},{1,0},{2,3},{3,2},{4,5},{5,4},{6,7},{7,6},{8,9},{9,8},{10,11... | collective-permute-start | bytes 405512 | tf_op jit(solution)/shard_map/ppermute | solution.py:592
  54.1 16.0 %collective-permute-start.13 = (f32[264,128]{1,0:T(8,128)S(1)}, f32[264,128]{1,0:T(8,128)S(1)}, u32[]{:S(2)}, u32[]{:S(2)}) collective-permute-start(f32[264,128]{1,0:T(8,128)S(1)} %get-tuple-element.32.tail), channel_id=1, source_target_pairs={{0,48},{16,0},{32,16},{48,32},{1,49},{17,1},{33,17},{49,33},{2,50}... | collective-permute-start | bytes 405512 | tf_op jit(solution)/shard_map/ppermute | solution.py:598
  54.2 19.7 %collective-permute-start.11 = (f32[264,128]{1,0:T(8,128)S(1)}, f32[264,128]{1,0:T(8,128)S(1)}, u32[]{:S(2)}, u32[]{:S(2)}) collective-permute-start(f32[264,128]{1,0:T(8,128)S(1)} %get-tuple-element.32.tail), channel_id=1, source_target_pairs={{0,32},{16,48},{32,0},{48,16},{1,33},{17,49},{33,1},{49,17},{2,34}... | collective-permute-start | bytes 405512 | tf_op jit(solution)/shard_map/ppermute | solution.py:598
  67.7 7.4 %collective-permute-start.9 = (f32[264,128]{1,0:T(8,128)S(1)}, f32[264,128]{1,0:T(8,128)S(1)}, u32[]{:S(2)}, u32[]{:S(2)}) collective-permute-start(f32[264,128]{1,0:T(8,128)S(1)} %get-tuple-element.32.tail), channel_id=1, source_target_pairs={{0,16},{16,32},{32,48},{48,0},{1,17},{17,33},{33,49},{49,1},{2,18}... | collective-permute-start | bytes 405512 | tf_op jit(solution)/shard_map/ppermute | solution.py:598
  70.2 5.0 %collective-permute-start.14 = (f32[264,128]{1,0:T(8,128)S(1)}, f32[264,128]{1,0:T(8,128)S(1)}, u32[]{:S(2)}, u32[]{:S(2)}) collective-permute-start(f32[264,128]{1,0:T(8,128)S(1)} %collective-permute-done.13.refs_4_), channel_id=1, source_target_pairs={{0,1},{1,0},{2,3},{3,2},{4,5},{5,4},{6,7},{7,6},{8,9},{9,8},{10,11... | collective-permute-start | bytes 405512 | tf_op jit(solution)/shard_map/ppermute | solution.py:592
  73.9 2.2 %collective-permute-start.12 = (f32[264,128]{1,0:T(8,128)S(1)}, f32[264,128]{1,0:T(8,128)S(1)}, u32[]{:S(2)}, u32[]{:S(2)}) collective-permute-start(f32[264,128]{1,0:T(8,128)S(1)} %collective-permute-done.11.refs_2_), channel_id=1, source_target_pairs={{0,1},{1,0},{2,3},{3,2},{4,5},{5,4},{6,7},{7,6},{8,9},{9,8},{10,11... | collective-permute-start | bytes 405512 | tf_op jit(solution)/shard_map/ppermute | solution.py:592
  75.1 1.4 %collective-permute-start.10 = (f32[264,128]{1,0:T(8,128)S(1)}, f32[264,128]{1,0:T(8,128)S(1)}, u32[]{:S(2)}, u32[]{:S(2)}) collective-permute-start(f32[264,128]{1,0:T(8,128)S(1)} %collective-permute-done.9.refs_0_), channel_id=1, source_target_pairs={{0,1},{1,0},{2,3},{3,2},{4,5},{5,4},{6,7},{7,6},{8,9},{9,8},{10,11... | collective-permute-start | bytes 405512 | tf_op jit(solution)/shard_map/ppermute | solution.py:592
  80.5 10.8 %collective-permute-start.19 = (f32[272,128]{1,0:T(8,128)S(1)}, f32[272,128]{1,0:T(8,128)S(1)}, u32[]{:S(2)}, u32[]{:S(2)}) collective-permute-start(f32[272,128]{1,0:T(8,128)S(1)} %get-tuple-element.34.tail), channel_id=1, source_target_pairs={{0,192},{64,0},{128,64},{192,128},{1,193},{65,1},{129,65},{193,129... | collective-permute-start | bytes 417800 | tf_op jit(solution)/shard_map/ppermute | solution.py:598
  85.8 13.7 %collective-permute-start.17 = (f32[272,128]{1,0:T(8,128)S(1)}, f32[272,128]{1,0:T(8,128)S(1)}, u32[]{:S(2)}, u32[]{:S(2)}) collective-permute-start(f32[272,128]{1,0:T(8,128)S(1)} %get-tuple-element.34.tail), channel_id=1, source_target_pairs={{0,128},{64,192},{128,0},{192,64},{1,129},{65,193},{129,1},{193,65... | collective-permute-start | bytes 417800 | tf_op jit(solution)/shard_map/ppermute | solution.py:598
  87.7 14.3 %collective-permute-start.15 = (f32[272,128]{1,0:T(8,128)S(1)}, f32[272,128]{1,0:T(8,128)S(1)}, u32[]{:S(2)}, u32[]{:S(2)}) collective-permute-start(f32[272,128]{1,0:T(8,128)S(1)} %get-tuple-element.34.tail), channel_id=1, source_target_pairs={{0,64},{64,128},{128,192},{192,0},{1,65},{65,129},{129,193},{193,1... | collective-permute-start | bytes 417800 | tf_op jit(solution)/shard_map/ppermute | solution.py:598
  91.3 10.7 %collective-permute-start.20 = (f32[272,128]{1,0:T(8,128)S(1)}, f32[272,128]{1,0:T(8,128)S(1)}, u32[]{:S(2)}, u32[]{:S(2)}) collective-permute-start(f32[272,128]{1,0:T(8,128)S(1)} %collective-permute-done.19.refs_4_), channel_id=1, source_target_pairs={{0,1},{1,0},{2,3},{3,2},{4,5},{5,4},{6,7},{7,6},{8,9},{9,8},{10,11... | collective-permute-start | bytes 417800 | tf_op jit(solution)/shard_map/ppermute | solution.py:592
  99.5 3.5 %collective-permute-start.18 = (f32[272,128]{1,0:T(8,128)S(1)}, f32[272,128]{1,0:T(8,128)S(1)}, u32[]{:S(2)}, u32[]{:S(2)}) collective-permute-start(f32[272,128]{1,0:T(8,128)S(1)} %collective-permute-done.17.refs_2_), channel_id=1, source_target_pairs={{0,1},{1,0},{2,3},{3,2},{4,5},{5,4},{6,7},{7,6},{8,9},{9,8},{10,11... | collective-permute-start | bytes 417800 | tf_op jit(solution)/shard_map/ppermute | solution.py:592
  102.0 1.4 %collective-permute-start.16 = (f32[272,128]{1,0:T(8,128)S(1)}, f32[272,128]{1,0:T(8,128)S(1)}, u32[]{:S(2)}, u32[]{:S(2)}) collective-permute-start(f32[272,128]{1,0:T(8,128)S(1)} %collective-permute-done.15.refs_0_), channel_id=1, source_target_pairs={{0,1},{1,0},{2,3},{3,2},{4,5},{5,4},{6,7},{7,6},{8,9},{9,8},{10,11... | collective-permute-start | bytes 417800 | tf_op jit(solution)/shard_map/ppermute | solution.py:592

commit v3 on v2

--- a/solution.py
+++ b/solution.py
@@ -131,7 +131,7 @@
 
 
 def residual_kernel(
-    info, table, weighted, arrived, u0, u4, labels, label_low, label_high, shift,
+    info, table, weighted, arrived, u0, u4, labels, label_low, label_high, shift, cells,
     coarse, start, wide, block,
 ):
     nz, nx, ny = weighted.shape
@@ -161,9 +161,13 @@
     coarse[nz // 4] = pair_mean(block)
     block[...] = kappa_of(label_high[0], table) * wide[nz, pl.ds(8, nx)]
     coarse[nz // 4 + 1] = pair_mean(block)
-
-
-def residual(info, table, weighted, arrived, node_fields, labels, label_low, label_high, shift):
+    coarse[nz // 4 + 2] = cells[0]
+    coarse[nz // 4 + 3] = cells[1]
+
+
+def residual(
+    info, table, weighted, arrived, node_fields, labels, label_low, label_high, shift, cells
+):
     nz, nx, ny = weighted.shape
     slab = whole((nz, nx, ny))
     return pl.pallas_call(
@@ -171,17 +175,20 @@
         grid=(1,),
         in_specs=[
             SMEM, SMEM, slab, slab, node_block(0, nz, nx, ny), node_block(NODES - 1, nz, nx, ny),
-            slab, slab, slab, whole((1, ny)),
-        ],
-        out_specs=[whole((nz // 4 + 2, nx // 2, ny)), slab],
+            slab, slab, slab, whole((1, ny)), whole(cells.shape),
+        ],
+        out_specs=[whole((nz // 4 + 4, nx // 2, ny)), slab],
         out_shape=[
-            jax.ShapeDtypeStruct((nz // 4 + 2, nx // 2, ny), F32),
+            jax.ShapeDtypeStruct((nz // 4 + 4, nx // 2, ny), F32),
             jax.ShapeDtypeStruct((nz, nx, ny), F32),
         ],
         scratch_shapes=[pltpu.VMEM((nz + 2, nx + 16, ny), F32), pltpu.VMEM((nx, ny), F32)],
         compiler_params=pltpu.CompilerParams(vmem_limit_bytes=20 * MIB),
         name="residual",
-    )(info, table, weighted, arrived, node_fields, node_fields, labels, label_low, label_high, shift)
+    )(
+        info, table, weighted, arrived, node_fields, node_fields, labels, label_low, label_high,
+        shift, cells,
+    )
 
 
 def pack_kernel(nodes, start, packed):
@@ -254,7 +261,7 @@
         put_ring(state, z + 1, get_layer(state, z) + member[z])
 
 
-def entry_kernel(info, gathered, shift, field, packet):
+def entry_kernel(info, gathered, shift, field, kappa, packet):
     ns, parts, nx, ny = gathered.shape
     for s in range(ns):
         low = gathered[s, 0]
@@ -265,6 +272,8 @@
             high = high + gathered[s + 1, 2]
         field[2 * s] = low
         field[2 * s + 1] = high
+        kappa[2 * s] = gathered[s, 4]
+        kappa[2 * s + 1] = gathered[s, 5]
     core = info[4] % 2
     for k in range(ns):
         packet[pl.ds(k * nx, nx)] = field[core * ns + k]
@@ -276,8 +285,9 @@
     return pl.pallas_call(
         entry_kernel,
         in_specs=[SMEM, VMEM, VMEM],
-        out_specs=[VMEM] * 2,
+        out_specs=[VMEM] * 3,
         out_shape=[
+            jax.ShapeDtypeStruct((2 * ns, nx, ny), F32),
             jax.ShapeDtypeStruct((2 * ns, nx, ny), F32),
             jax.ShapeDtypeStruct((ns * nx + 8, ny), F32),
         ],
@@ -371,8 +381,7 @@
     )(info, own, tail, before, kappa, *packets)
 
 
-def final_kernel(info, field, tail, before, kappa, *refs):
-    packets, (coarse, members, halves, ping, pong) = refs[:6], refs[6:]
+def finish_chain(info, field, tail, before, kappa, packets, coarse, members, halves, ping, pong):
     nz, nx, ny = kappa.shape
     core, zh = info[4] % 2, info[1]
     inside = info[2] * 4 + info[3]
@@ -423,30 +432,13 @@
         coarse[1, z + 2] = get_layer(pong, z) + field[z] - value
 
 
-def chain_final(info, field, tail, before, kappa, packets):
-    nz, nx, ny = kappa.shape
-    return pl.pallas_call(
-        final_kernel,
-        in_specs=[SMEM] + [VMEM] * (4 + len(packets)),
-        out_specs=VMEM,
-        out_shape=jax.ShapeDtypeStruct((2, nz + 4, nx, ny), F32),
-        scratch_shapes=[
-            pltpu.VMEM((4, nz, nx, ny), F32),
-            pltpu.VMEM((64, 8, ny), F32),
-            pltpu.VMEM((nz + 2, nx + 16, ny), F32),
-            pltpu.VMEM((nz + 2, nx + 16, ny), F32),
-        ],
-        compiler_params=pltpu.CompilerParams(vmem_limit_bytes=12 * MIB),
-        name="chain_final",
-    )(info, field, tail, before, kappa, *packets)
-
-
 CHUNK = 32
 
 
 def sweeps_kernel(
-    info, table, coarse, own, low, high, labels, labels_low, labels_high, shift, out,
-    held, marks, lift, kappa, first, mixed_a, mixed_b, *rest,
+    info, table, own, low, high, labels, labels_low, labels_high, shift,
+    field, tail, before, kappa_c, p0, p1, p2, p3, p4, p5, out,
+    coarse, members, halves, ping, pong, held, marks, lift, kappa, first, mixed_a, mixed_b, *rest,
 ):
     fields, second, (sems, out_sems) = rest[:STEPS], rest[STEPS : 2 * STEPS], rest[2 * STEPS :]
     mixed = (mixed_a, mixed_b)
@@ -463,6 +455,9 @@
         )
     for copy in copies:
         copy.start()
+    finish_chain(
+        info, field, tail, before, kappa_c, (p0, p1, p2, p3, p4, p5), coarse, members, halves, ping, pong
+    )
     advect = jnp.broadcast_to(shift[...].astype(F32), (CHUNK, ny))
     for f in range(2):
         for k in range(wide // 4):
@@ -549,15 +544,21 @@
         copy.wait()
 
 
-def fine_sweeps(info, table, coarse, own, low, high, labels, labels_low, labels_high, shift):
-    nz, nx, ny = labels.shape
+def fine_sweeps(info, table, fine, chain):
+    nz, nx, ny = fine[3].shape
+    nzc, nxc, _ = chain[3].shape
     wide = 3 * nz
     return pl.pallas_call(
         sweeps_kernel,
-        in_specs=[SMEM, SMEM, VMEM] + [ANY] * 6 + [VMEM],
+        in_specs=[SMEM, SMEM] + [ANY] * 6 + [VMEM] * 11,
         out_specs=ANY,
         out_shape=jax.ShapeDtypeStruct((1, NODES, nz, nx, ny), F32),
         scratch_shapes=[
+            pltpu.VMEM((2, nzc + 4, nxc, ny), F32),
+            pltpu.VMEM((4, nzc, nxc, ny), F32),
+            pltpu.VMEM((64, 8, ny), F32),
+            pltpu.VMEM((nzc + 2, nxc + 16, ny), F32),
+            pltpu.VMEM((nzc + 2, nxc + 16, ny), F32),
             pltpu.VMEM((NODES, wide, nx, ny), F32),
             pltpu.VMEM((wide, nx, ny), jnp.int32),
             pltpu.VMEM((2, wide // 4, nx, ny), F32),
@@ -571,9 +572,9 @@
             pltpu.SemaphoreType.DMA((6,)),
             pltpu.SemaphoreType.DMA((NODES,)),
         ],
-        compiler_params=pltpu.CompilerParams(vmem_limit_bytes=36 * MIB),
+        compiler_params=pltpu.CompilerParams(vmem_limit_bytes=40 * MIB),
         name="fine_sweeps",
-    )(info, table, coarse, own, low, high, labels, labels_low, labels_high, shift)
+    )(info, table, *fine, *chain)
 
 
 def to_space(value, by):
@@ -606,15 +607,13 @@
     info = jnp.stack([zh * 16 + y * 4 + x, zh, y, x, space]).astype(jnp.int32)
     arrived = to_next(node_fields[0, NODES - 1], 0)
     labels_low, labels_high = to_space(region_label, 1), to_space(region_label, -1)
-    weighted, kappa = weigh(info, diffusivity, node_fields, region_label)
-    kappa = lax.all_gather(kappa, "space", axis=0, tiled=True)
-    weighted, kappa = lax.optimization_barrier((weighted, kappa))
+    weighted, cells = weigh(info, diffusivity, node_fields, region_label)
     coarse, start = residual(
         info, diffusivity, weighted, arrived, node_fields, region_label, labels_low, labels_high,
-        sheet_shift,
+        sheet_shift, cells,
     )
     gathered = lax.all_gather(coarse, "space", axis=0, tiled=False)
-    field, packet = chain_entry(info, gathered, sheet_shift)
+    field, kappa, packet = chain_entry(info, gathered, sheet_shift)
     packets = gather_axis(packet, "x")
     start, _ = lax.optimization_barrier((start, packet))
     packed = pack(node_fields, start)
@@ -624,10 +623,11 @@
     packets = gather_axis(packet, "y")
     packet, _, prefix = chain_level(4, 2, info, field4, packet, prefix, kappa, packets)
     packets = gather_axis(packet, "zh")
-    correction = chain_final(info, field, packet, prefix, kappa, packets)
     return fine_sweeps(
-        info, diffusivity, correction, packed, packed_low, packed_high,
-        region_label, labels_low, labels_high, sheet_shift,
+        info,
+        diffusivity,
+        (packed, packed_low, packed_high, region_label, labels_low, labels_high, sheet_shift),
+        (field, packet, prefix, kappa, *packets),
     )
 
 

time: 122 us -> 120 us (0.984)
  waiting for transfers between devices: 21.8 us -> 26.3 us
  blocking collectives: 13.2 us -> 9.51 us
  starting transfers between devices: 54.1 us -> 52.1 us
    all_gather x1 -> x0, blocking collectives: 5.86 us -> none  [shards(): kappa = lax.all_gather(kappa, 'space', axis=0, tiled=True)]
    ppermute x1, waiting for transfers between devices: 0.01 us -> 3.5 us  [to_next(): return lax.ppermute(value, axes, pairs)]
    all_gather x1, blocking collectives: 7.29 us -> 9.51 us  [shards(): gathered = lax.all_gather(coarse, 'space', axis=0, tiled=False)]
    ppermute x9, waiting for transfers between devices: 17.8 us -> 19.4 us  [gather_axis(): got = lax.ppermute(packet, axis, [(i, (i + k) % 4) for i in range(4)])]
    ppermute x9, starting transfers between devices: 5.75 us -> 4.14 us  [swap_core(): return lax.ppermute(value, 'space', [(0, 1), (1, 0), (2, 3), (3, 2)])]
    pallas_call x2 -> x1, Pallas kernels: 18 us -> 17.5 us  [fine_sweeps(): pl.pallas_call(sweeps_kernel, in_specs=[SMEM, SMEM] + [ANY] * 6 + [VMEM]...]
  transfers between devices with their start and end apart: 23 -> 23, of which waited for: 11 -> 14; matrix products, arithmetic and copies ran while one was open for 0% -> 0% of each run, Pallas kernels for 14% -> 6%
where the time goes in v3:
time: 120 us
  starting transfers between devices  52.1 us (43%)
  Pallas kernels  26.9 us (22%)
  waiting for transfers between devices  26.3 us (22%)
  blocking collectives  9.51 us (8%)
  local copies, waits for them, and re-layouts  4.67 us (4%)
    ppermute x9, starting transfers between devices, gather_axis(): got = lax.ppermute(packet, axis, [(i, (i + k) % 4) for i in range(4)])  30.9 us
    ppermute x9, waiting for transfers between devices, gather_axis(): got = lax.ppermute(packet, axis, [(i, (i + k) % 4) for i in range(4)])  19.4 us
    pallas_call x1, Pallas kernels, fine_sweeps(): pl.pallas_call(sweeps_kernel, in_specs=[SMEM, SMEM] + [ANY] * 6 + [VMEM]...  17.5 us
    ppermute x4, starting transfers between devices, to_space(): lax.ppermute(value, 'space', [(i, i + by) for i in range(4) if 0 <= i + b...  14 us
    all_gather x1, blocking collectives, shards(): gathered = lax.all_gather(coarse, 'space', axis=0, tiled=False)  9.51 us
    pallas_call x2, Pallas kernels, chain_level(): pl.pallas_call(functools.partial(level_kernel, length, axis), in_specs=[S...  5.44 us
    ppermute x9, starting transfers between devices, swap_core(): return lax.ppermute(value, 'space', [(0, 1), (1, 0), (2, 3), (3, 2)])  4.14 us
    ppermute x1, waiting for transfers between devices, to_next(): return lax.ppermute(value, axes, pairs)  3.5 us
  transfers between devices with their start and end apart: 23, of which 14 were waited for; matrix products, arithmetic and copies ran while one was open for 0% of the time, Pallas kernels for 6%

profile of v3, /device:TPU:217, one launch (start us, length us, event | category | flops | bytes accessed | tf_op | source)
XLA Modules:
  0.0 119.9 jit_solution(10975117627598411893)
XLA Ops:
  0.0 1.1 slice_bitcast_fusion
  1.2 3.1 %collective-permute-start = (f32[8,128,128]{2,1,0:T(8,128)S(1)}, f32[8,128,128]{2,1,0:T(8,128)S(1)}, u32[]{:S(2)}, u32[]{:S(2)}) collective-permute-start(f32[8,128,128]{2,1,0:T(8,128)S(1)} %slice_bitcast_fusion), channel_id=1, source_target_pairs={{0,4},{1,5},{2,6},{3,7},{4,8},{5,9},{6,10},{7,11},{8,12},{9,13},{1... | collective-permute-start | bytes 1572872 | tf_op jit(solution)/shard_map/ppermute | solution.py:589
  4.3 2.9 %collective-permute-start.2 = (s32[8,128,128]{2,1,0:T(8,128)}, s32[8,128,128]{2,1,0:T(8,128)S(1)}, u32[]{:S(2)}, u32[]{:S(2)}) collective-permute-start(s32[8,128,128]{2,1,0:T(8,128)} %labels.5), channel_id=1, source_target_pairs={{1,0},{2,1},{3,2},{5,4},{6,5},{7,6},{9,8},{10,9},{11,10},{13,12},{... | collective-permute-start | bytes 1572872 | tf_op jit(solution)/shard_map/ppermute | solution.py:581
  7.2 2.7 %collective-permute-start.1 = (s32[8,128,128]{2,1,0:T(8,128)}, s32[8,128,128]{2,1,0:T(8,128)S(1)}, u32[]{:S(2)}, u32[]{:S(2)}) collective-permute-start(s32[8,128,128]{2,1,0:T(8,128)} %labels.5), channel_id=1, source_target_pairs={{0,1},{1,2},{2,3},{4,5},{5,6},{6,7},{8,9},{9,10},{10,11},{12,13},{... | collective-permute-start | bytes 1572872 | tf_op jit(solution)/shard_map/ppermute | solution.py:581
  9.9 0.1 stack.23.info
  10.0 1.7 %copy-done = f32[1,5,8,128,128]{4,3,2,1,0:T(8,128)S(1)} copy-done((f32[1,5,8,128,128]{4,3,2,1,0:T(8,128)S(1)}, f32[1,5,8,128,128]{4,3,2,1,0:T(8,128)}, u32[]{:S(2)}) %copy-start) | copy-done | bytes 2621464
  11.7 1.0 copy-done.2
  12.7 0.7 copy-done.4
  13.4 1.0 weigh.1
  14.4 3.5 %collective-permute-done.arrived = f32[8,128,128]{2,1,0:T(8,128)S(1)} collective-permute-done((f32[8,128,128]{2,1,0:T(8,128)S(1)}, f32[8,128,128]{2,1,0:T(8,128)S(1)}, u32[]{:S(2)}, u32[]{:S(2)}) %collective-permute-start) | collective-permute-done | bytes 524320 | tf_op jit(solution)/shard_map/ppermute | solution.py:589
  17.9 0.0 collective-permute-done.2.label_high.labels_high
  18.0 1.2 %residual.1 = (f32[6,64,128]{2,1,0:T(8,128)S(1)}, f32[8,128,128]{2,1,0:T(8,128)S(1)}) custom-call(s32[5]{0:T(128)S(1)} %stack.23.info, f32[4]{0:T(128)S(1)} %copy-done.5, f32[8,128,128]{2,1,0:T(8,128)S(1)} %get-tuple-element.20.weighted, f32[8,128,128]{2,1,0:T(8,128)S(1)} %collective-permute-done.arrived, f32[1,5,8,128,128]{4,3,2,1,0:T(8,128)S(1)} %copy-done.1, ...), custom_call_target="tpu_custom_call" | custom-call | tf_op jit(solution)/shard_map/residual/pallas_call | solution.py:173
  19.2 9.5 %all-gather = f32[24,64,128]{2,1,0:T(8,128)S(1)} all-gather(f32[6,64,128]{2,1,0:T(8,128)S(1)} %get-tuple-element.23), channel_id=2, replica_groups=mesh['zh'=4,'y'=4,'x'=4,'space'=4] {'space'}, dimensions={0}, use_global_device_ids=true | all-gather | bytes 983040 | tf_op jit(solution)/shard_map/all_gather | solution.py:615
  28.7 0.6 chain_entry.1
  29.3 4.5 %collective-permute-start.3 = (f32[264,128]{1,0:T(8,128)S(1)}, f32[264,128]{1,0:T(8,128)S(1)}, u32[]{:S(2)}, u32[]{:S(2)}) collective-permute-start(f32[264,128]{1,0:T(8,128)S(1)} %get-tuple-element.24.tail), channel_id=1, source_target_pairs={{0,12},{4,0},{8,4},{12,8},{1,13},{5,1},{9,5},{13,9},{2,14},{6,2},{... | collective-permute-start | bytes 405512 | tf_op jit(solution)/shard_map/ppermute | solution.py:599
  33.8 1.2 pack.1.own
  34.9 1.3 %collective-permute-done.3.refs_4_ = f32[264,128]{1,0:T(8,128)S(1)} collective-permute-done((f32[264,128]{1,0:T(8,128)S(1)}, f32[264,128]{1,0:T(8,128)S(1)}, u32[]{:S(2)}, u32[]{:S(2)}) %collective-permute-start.3) | collective-permute-done | bytes 135200 | tf_op jit(solution)/shard_map/ppermute | solution.py:599
  36.2 3.2 %collective-permute-start.5 = (f32[5,8,128,128]{3,2,1,0:T(8,128)S(1)}, f32[5,8,128,128]{3,2,1,0:T(8,128)S(1)}, u32[]{:S(2)}, u32[]{:S(2)}) collective-permute-start(f32[5,8,128,128]{3,2,1,0:T(8,128)S(1)} %pack.1.own), channel_id=1, source_target_pairs={{1,0},{2,1},{3,2},{5,4},{6,5},{7,6},{9,8},{10,9},{11,10},{13,12},{... | collective-permute-start | bytes 7864328 | tf_op jit(solution)/shard_map/ppermute | solution.py:581
  39.5 5.2 %collective-permute-start.4 = (f32[5,8,128,128]{3,2,1,0:T(8,128)S(1)}, f32[5,8,128,128]{3,2,1,0:T(8,128)S(1)}, u32[]{:S(2)}, u32[]{:S(2)}) collective-permute-start(f32[5,8,128,128]{3,2,1,0:T(8,128)S(1)} %pack.1.own), channel_id=1, source_target_pairs={{0,1},{1,2},{2,3},{4,5},{5,6},{6,7},{8,9},{9,10},{10,11},{12,13},{... | collective-permute-start | bytes 7864328 | tf_op jit(solution)/shard_map/ppermute | solution.py:581
  44.7 2.0 %collective-permute-start.8 = (f32[264,128]{1,0:T(8,128)S(1)}, f32[264,128]{1,0:T(8,128)S(1)}, u32[]{:S(2)}, u32[]{:S(2)}) collective-permute-start(f32[264,128]{1,0:T(8,128)S(1)} %get-tuple-element.24.tail), channel_id=1, source_target_pairs={{0,8},{4,12},{8,0},{12,4},{1,9},{5,13},{9,1},{13,5},{2,10},{6,14},... | collective-permute-start | bytes 405512 | tf_op jit(solution)/shard_map/ppermute | solution.py:599
  46.7 2.1 %collective-permute-start.6 = (f32[264,128]{1,0:T(8,128)S(1)}, f32[264,128]{1,0:T(8,128)S(1)}, u32[]{:S(2)}, u32[]{:S(2)}) collective-permute-start(f32[264,128]{1,0:T(8,128)S(1)} %get-tuple-element.24.tail), channel_id=1, source_target_pairs={{0,4},{4,8},{8,12},{12,0},{1,5},{5,9},{9,13},{13,1},{2,6},{6,10},{... | collective-permute-start | bytes 405512 | tf_op jit(solution)/shard_map/ppermute | solution.py:599
  48.8 2.4 %collective-permute-done.8.refs_2_ = f32[264,128]{1,0:T(8,128)S(1)} collective-permute-done((f32[264,128]{1,0:T(8,128)S(1)}, f32[264,128]{1,0:T(8,128)S(1)}, u32[]{:S(2)}, u32[]{:S(2)}) %collective-permute-start.8) | collective-permute-done | bytes 135200 | tf_op jit(solution)/shard_map/ppermute | solution.py:599
  51.2 1.6 %collective-permute-done.6.refs_0_ = f32[264,128]{1,0:T(8,128)S(1)} collective-permute-done((f32[264,128]{1,0:T(8,128)S(1)}, f32[264,128]{1,0:T(8,128)S(1)}, u32[]{:S(2)}, u32[]{:S(2)}) %collective-permute-start.6) | collective-permute-done | bytes 135200 | tf_op jit(solution)/shard_map/ppermute | solution.py:599
  52.8 0.5 collective-permute-start.10
  53.3 0.8 collective-permute-done.7.refs_1_
  54.1 0.2 collective-permute-done.10.refs_5_
  54.3 1.4 %chain_level_1.1 = (f32[264,128]{1,0:T(8,128)S(1)}, f32[8,64,128]{2,1,0:T(8,128)S(1)}, f32[8,64,128]{2,1,0:T(8,128)S(1)}) custom-call(s32[5]{0:T(128)S(1)} %stack.23.info, f32[8,64,128]{2,1,0:T(8,128)S(1)} %get-tuple-element.27.own.before.field, f32[264,128]{1,0:T(8,128)S(1)} %get-tuple-element.24.tail, ...), custom_call_target="tpu_custom_call" | custom-call | tf_op jit(solution)/shard_map/chain_level_1/pallas_call | solution.py:363
  55.7 0.1 collective-permute-start.15
  55.8 13.0 %collective-permute-start.13 = (f32[264,128]{1,0:T(8,128)S(1)}, f32[264,128]{1,0:T(8,128)S(1)}, u32[]{:S(2)}, u32[]{:S(2)}) collective-permute-start(f32[264,128]{1,0:T(8,128)S(1)} %get-tuple-element.31.tail), channel_id=1, source_target_pairs={{0,32},{16,48},{32,0},{48,16},{1,33},{17,49},{33,1},{49,17},{2,34}... | collective-permute-start | bytes 405512 | tf_op jit(solution)/shard_map/ppermute | solution.py:599
  68.8 2.7 %collective-permute-done.15.refs_4_ = f32[264,128]{1,0:T(8,128)S(1)} collective-permute-done((f32[264,128]{1,0:T(8,128)S(1)}, f32[264,128]{1,0:T(8,128)S(1)}, u32[]{:S(2)}, u32[]{:S(2)}) %collective-permute-start.15) | collective-permute-done | bytes 135200 | tf_op jit(solution)/shard_map/ppermute | solution.py:599
  71.5 0.7 collective-permute-start.16
  72.2 3.1 %collective-permute-done.13.refs_2_ = f32[264,128]{1,0:T(8,128)S(1)} collective-permute-done((f32[264,128]{1,0:T(8,128)S(1)}, f32[264,128]{1,0:T(8,128)S(1)}, u32[]{:S(2)}, u32[]{:S(2)}) %collective-permute-start.13) | collective-permute-done | bytes 135200 | tf_op jit(solution)/shard_map/ppermute | solution.py:599
  75.2 1.0 collective-permute-start.14
  76.2 0.0 collective-permute-start.12
  76.2 1.0 collective-permute-done.14.refs_3_
  77.2 0.4 collective-permute-done.12.refs_1_
  77.6 4.1 %chain_level_4.1 = (f32[272,128]{1,0:T(8,128)S(1)}, f32[8,64,128]{2,1,0:T(8,128)}, f32[8,64,128]{2,1,0:T(8,128)S(1)}) custom-call(s32[5]{0:T(128)S(1)} %stack.23.info, f32[8,64,128]{2,1,0:T(8,128)S(1)} %get-tuple-element.30.own, f32[264,128]{1,0:T(8,128)S(1)} %get-tuple-element.31.tail, f32[8,64,128]{2,1,0:T(8,128)S(1)} %get-tuple-element.32.before, ...), custom_call_target="tpu_custom_call" | custom-call | tf_op jit(solution)/shard_map/chain_level_4/pallas_call | solution.py:363
  81.7 3.7 %collective-permute-start.21 = (f32[272,128]{1,0:T(8,128)S(1)}, f32[272,128]{1,0:T(8,128)S(1)}, u32[]{:S(2)}, u32[]{:S(2)}) collective-permute-start(f32[272,128]{1,0:T(8,128)S(1)} %get-tuple-element.33.tail), channel_id=1, source_target_pairs={{0,192},{64,0},{128,64},{192,128},{1,193},{65,1},{129,65},{193,129... | collective-permute-start | bytes 417800 | tf_op jit(solution)/shard_map/ppermute | solution.py:599
  85.4 2.0 %collective-permute-start.19 = (f32[272,128]{1,0:T(8,128)S(1)}, f32[272,128]{1,0:T(8,128)S(1)}, u32[]{:S(2)}, u32[]{:S(2)}) collective-permute-start(f32[272,128]{1,0:T(8,128)S(1)} %get-tuple-element.33.tail), channel_id=1, source_target_pairs={{0,128},{64,192},{128,0},{192,64},{1,129},{65,193},{129,1},{193,65... | collective-permute-start | bytes 417800 | tf_op jit(solution)/shard_map/ppermute | solution.py:599
  87.3 3.6 %collective-permute-start.17 = (f32[272,128]{1,0:T(8,128)S(1)}, f32[272,128]{1,0:T(8,128)S(1)}, u32[]{:S(2)}, u32[]{:S(2)}) collective-permute-start(f32[272,128]{1,0:T(8,128)S(1)} %get-tuple-element.33.tail), channel_id=1, source_target_pairs={{0,64},{64,128},{128,192},{192,0},{1,65},{65,129},{129,193},{193,1... | collective-permute-start | bytes 417800 | tf_op jit(solution)/shard_map/ppermute | solution.py:599
  90.9 4.9 %collective-permute-done.21.p4 = f32[272,128]{1,0:T(8,128)S(1)} collective-permute-done((f32[272,128]{1,0:T(8,128)S(1)}, f32[272,128]{1,0:T(8,128)S(1)}, u32[]{:S(2)}, u32[]{:S(2)}) %collective-permute-start.21) | collective-permute-done | bytes 139296 | tf_op jit(solution)/shard_map/ppermute | solution.py:599
  95.8 0.5 collective-permute-start.22
  96.3 3.4 %collective-permute-done.19.p2 = f32[272,128]{1,0:T(8,128)S(1)} collective-permute-done((f32[272,128]{1,0:T(8,128)S(1)}, f32[272,128]{1,0:T(8,128)S(1)}, u32[]{:S(2)}, u32[]{:S(2)}) %collective-permute-start.19) | collective-permute-done | bytes 139296 | tf_op jit(solution)/shard_map/ppermute | solution.py:599
  99.8 0.7 collective-permute-start.20
  100.5 0.7 collective-permute-start.18
  101.2 0.3 collective-permute-done.20.p3
  101.5 0.7 collective-permute-done.18.p1
  102.2 17.5 %fine_sweeps.1 = f32[1,5,8,128,128]{4,3,2,1,0:T(8,128)} custom-call(s32[5]{0:T(128)S(1)} %stack.23.info, f32[4]{0:T(128)S(1)} %copy-done.5, f32[5,8,128,128]{3,2,1,0:T(8,128)S(1)} %pack.1.own, f32[5,8,128,128]{3,2,1,0:T(8,128)S(1)} %collective-permute-done.4.low, f32[5,8,128,128]{3,2,1,0:T(8,128)S(1)} %collective-permute-done.5.high, ...), custom_call_target="tpu_custom_call" | custom-call | tf_op jit(solution)/shard_map/fine_sweeps/pallas_call | solution.py:551
  (22 shorter events, 0.0 us)
Async XLA Ops:
  0.0 18.0 %copy-start.3 = (s32[8,128,128]{2,1,0:T(8,128)S(1)}, s32[8,128,128]{2,1,0:T(8,128)}, u32[]{:S(2)}) copy-start(s32[8,128,128]{2,1,0:T(8,128)} %labels.5) | copy-start | bytes 1572868
  0.0 18.0 %copy-start.5 = (f32[4]{0:T(128)S(1)}, f32[4]{0:T(128)}, u32[]{:S(2)}) copy-start(f32[4]{0:T(128)} %table.5) | copy-start | bytes 52
  0.0 18.0 %copy-start.6 = (s32[1,128]{1,0:T(1,128)S(1)}, s32[1,128]{1,0:T(1,128)}, u32[]{:S(2)}) copy-start(s32[1,128]{1,0:T(1,128)} %shift.5) | copy-start | bytes 1540
  1.2 16.8 %collective-permute-start = (f32[8,128,128]{2,1,0:T(8,128)S(1)}, f32[8,128,128]{2,1,0:T(8,128)S(1)}, u32[]{:S(2)}, u32[]{:S(2)}) collective-permute-start(f32[8,128,128]{2,1,0:T(8,128)S(1)} %slice_bitcast_fusion), channel_id=1, source_target_pairs={{0,4},{1,5},{2,6},{3,7},{4,8},{5,9},{6,10},{7,11},{8,12},{9,13},{1... | collective-permute-start | bytes 1572872 | tf_op jit(solution)/shard_map/ppermute | solution.py:589
  4.3 13.7 %collective-permute-start.2 = (s32[8,128,128]{2,1,0:T(8,128)}, s32[8,128,128]{2,1,0:T(8,128)S(1)}, u32[]{:S(2)}, u32[]{:S(2)}) collective-permute-start(s32[8,128,128]{2,1,0:T(8,128)} %labels.5), channel_id=1, source_target_pairs={{1,0},{2,1},{3,2},{5,4},{6,5},{7,6},{9,8},{10,9},{11,10},{13,12},{... | collective-permute-start | bytes 1572872 | tf_op jit(solution)/shard_map/ppermute | solution.py:581
  7.2 10.8 %collective-permute-start.1 = (s32[8,128,128]{2,1,0:T(8,128)}, s32[8,128,128]{2,1,0:T(8,128)S(1)}, u32[]{:S(2)}, u32[]{:S(2)}) collective-permute-start(s32[8,128,128]{2,1,0:T(8,128)} %labels.5), channel_id=1, source_target_pairs={{0,1},{1,2},{2,3},{4,5},{5,6},{6,7},{8,9},{9,10},{10,11},{12,13},{... | collective-permute-start | bytes 1572872 | tf_op jit(solution)/shard_map/ppermute | solution.py:581
  10.0 1.7 %copy-start = (f32[1,5,8,128,128]{4,3,2,1,0:T(8,128)S(1)}, f32[1,5,8,128,128]{4,3,2,1,0:T(8,128)}, u32[]{:S(2)}) copy-start(f32[1,5,8,128,128]{4,3,2,1,0:T(8,128)} %nodes.3) | copy-start | bytes 7864324
  11.7 1.0 copy-start.2
  12.7 0.7 copy-start.4
  13.4 4.6 %copy-start.1 = (f32[1,5,8,128,128]{4,3,2,1,0:T(8,128)S(1)}, f32[1,5,8,128,128]{4,3,2,1,0:T(8,128)}, u32[]{:S(2)}) copy-start(f32[1,5,8,128,128]{4,3,2,1,0:T(8,128)} %nodes.3) | copy-start | bytes 7864324
  29.3 6.9 %collective-permute-start.3 = (f32[264,128]{1,0:T(8,128)S(1)}, f32[264,128]{1,0:T(8,128)S(1)}, u32[]{:S(2)}, u32[]{:S(2)}) collective-permute-start(f32[264,128]{1,0:T(8,128)S(1)} %get-tuple-element.24.tail), channel_id=1, source_target_pairs={{0,12},{4,0},{8,4},{12,8},{1,13},{5,1},{9,5},{13,9},{2,14},{6,2},{... | collective-permute-start | bytes 405512 | tf_op jit(solution)/shard_map/ppermute | solution.py:599
  36.2 66.0 %collective-permute-start.5 = (f32[5,8,128,128]{3,2,1,0:T(8,128)S(1)}, f32[5,8,128,128]{3,2,1,0:T(8,128)S(1)}, u32[]{:S(2)}, u32[]{:S(2)}) collective-permute-start(f32[5,8,128,128]{3,2,1,0:T(8,128)S(1)} %pack.1.own), channel_id=1, source_target_pairs={{1,0},{2,1},{3,2},{5,4},{6,5},{7,6},{9,8},{10,9},{11,10},{13,12},{... | collective-permute-start | bytes 7864328 | tf_op jit(solution)/shard_map/ppermute | solution.py:581
  39.5 62.8 %collective-permute-start.4 = (f32[5,8,128,128]{3,2,1,0:T(8,128)S(1)}, f32[5,8,128,128]{3,2,1,0:T(8,128)S(1)}, u32[]{:S(2)}, u32[]{:S(2)}) collective-permute-start(f32[5,8,128,128]{3,2,1,0:T(8,128)S(1)} %pack.1.own), channel_id=1, source_target_pairs={{0,1},{1,2},{2,3},{4,5},{5,6},{6,7},{8,9},{9,10},{10,11},{12,13},{... | collective-permute-start | bytes 7864328 | tf_op jit(solution)/shard_map/ppermute | solution.py:581
  44.7 6.5 %collective-permute-start.8 = (f32[264,128]{1,0:T(8,128)S(1)}, f32[264,128]{1,0:T(8,128)S(1)}, u32[]{:S(2)}, u32[]{:S(2)}) collective-permute-start(f32[264,128]{1,0:T(8,128)S(1)} %get-tuple-element.24.tail), channel_id=1, source_target_pairs={{0,8},{4,12},{8,0},{12,4},{1,9},{5,13},{9,1},{13,5},{2,10},{6,14},... | collective-permute-start | bytes 405512 | tf_op jit(solution)/shard_map/ppermute | solution.py:599
  46.7 6.1 %collective-permute-start.6 = (f32[264,128]{1,0:T(8,128)S(1)}, f32[264,128]{1,0:T(8,128)S(1)}, u32[]{:S(2)}, u32[]{:S(2)}) collective-permute-start(f32[264,128]{1,0:T(8,128)S(1)} %get-tuple-element.24.tail), channel_id=1, source_target_pairs={{0,4},{4,8},{8,12},{12,0},{1,5},{5,9},{9,13},{13,1},{2,6},{6,10},{... | collective-permute-start | bytes 405512 | tf_op jit(solution)/shard_map/ppermute | solution.py:599
  51.2 2.1 %collective-permute-start.9 = (f32[264,128]{1,0:T(8,128)S(1)}, f32[264,128]{1,0:T(8,128)S(1)}, u32[]{:S(2)}, u32[]{:S(2)}) collective-permute-start(f32[264,128]{1,0:T(8,128)S(1)} %collective-permute-done.8.refs_2_), channel_id=1, source_target_pairs={{0,1},{1,0},{2,3},{3,2},{4,5},{5,4},{6,7},{7,6},{8,9},{9,8},{10,11... | collective-permute-start | bytes 405512 | tf_op jit(solution)/shard_map/ppermute | solution.py:593
  52.8 1.4 %collective-permute-start.7 = (f32[264,128]{1,0:T(8,128)S(1)}, f32[264,128]{1,0:T(8,128)S(1)}, u32[]{:S(2)}, u32[]{:S(2)}) collective-permute-start(f32[264,128]{1,0:T(8,128)S(1)} %collective-permute-done.6.refs_0_), channel_id=1, source_target_pairs={{0,1},{1,0},{2,3},{3,2},{4,5},{5,4},{6,7},{7,6},{8,9},{9,8},{10,11... | collective-permute-start | bytes 405512 | tf_op jit(solution)/shard_map/ppermute | solution.py:593
  52.8 1.5 %collective-permute-start.10 = (f32[264,128]{1,0:T(8,128)S(1)}, f32[264,128]{1,0:T(8,128)S(1)}, u32[]{:S(2)}, u32[]{:S(2)}) collective-permute-start(f32[264,128]{1,0:T(8,128)S(1)} %collective-permute-done.3.refs_4_), channel_id=1, source_target_pairs={{0,1},{1,0},{2,3},{3,2},{4,5},{5,4},{6,7},{7,6},{8,9},{9,8},{10,11... | collective-permute-start | bytes 405512 | tf_op jit(solution)/shard_map/ppermute | solution.py:593
  55.7 15.8 %collective-permute-start.15 = (f32[264,128]{1,0:T(8,128)S(1)}, f32[264,128]{1,0:T(8,128)S(1)}, u32[]{:S(2)}, u32[]{:S(2)}) collective-permute-start(f32[264,128]{1,0:T(8,128)S(1)} %get-tuple-element.31.tail), channel_id=1, source_target_pairs={{0,48},{16,0},{32,16},{48,32},{1,49},{17,1},{33,17},{49,33},{2,50}... | collective-permute-start | bytes 405512 | tf_op jit(solution)/shard_map/ppermute | solution.py:599
  55.8 19.5 %collective-permute-start.13 = (f32[264,128]{1,0:T(8,128)S(1)}, f32[264,128]{1,0:T(8,128)S(1)}, u32[]{:S(2)}, u32[]{:S(2)}) collective-permute-start(f32[264,128]{1,0:T(8,128)S(1)} %get-tuple-element.31.tail), channel_id=1, source_target_pairs={{0,32},{16,48},{32,0},{48,16},{1,33},{17,49},{33,1},{49,17},{2,34}... | collective-permute-start | bytes 405512 | tf_op jit(solution)/shard_map/ppermute | solution.py:599
  68.8 7.4 %collective-permute-start.11 = (f32[264,128]{1,0:T(8,128)S(1)}, f32[264,128]{1,0:T(8,128)S(1)}, u32[]{:S(2)}, u32[]{:S(2)}) collective-permute-start(f32[264,128]{1,0:T(8,128)S(1)} %get-tuple-element.31.tail), channel_id=1, source_target_pairs={{0,16},{16,32},{32,48},{48,0},{1,17},{17,33},{33,49},{49,1},{2,18}... | collective-permute-start | bytes 405512 | tf_op jit(solution)/shard_map/ppermute | solution.py:599
  71.5 4.8 %collective-permute-start.16 = (f32[264,128]{1,0:T(8,128)S(1)}, f32[264,128]{1,0:T(8,128)S(1)}, u32[]{:S(2)}, u32[]{:S(2)}) collective-permute-start(f32[264,128]{1,0:T(8,128)S(1)} %collective-permute-done.15.refs_4_), channel_id=1, source_target_pairs={{0,1},{1,0},{2,3},{3,2},{4,5},{5,4},{6,7},{7,6},{8,9},{9,8},{10,11... | collective-permute-start | bytes 405512 | tf_op jit(solution)/shard_map/ppermute | solution.py:593
  75.2 2.0 %collective-permute-start.14 = (f32[264,128]{1,0:T(8,128)S(1)}, f32[264,128]{1,0:T(8,128)S(1)}, u32[]{:S(2)}, u32[]{:S(2)}) collective-permute-start(f32[264,128]{1,0:T(8,128)S(1)} %collective-permute-done.13.refs_2_), channel_id=1, source_target_pairs={{0,1},{1,0},{2,3},{3,2},{4,5},{5,4},{6,7},{7,6},{8,9},{9,8},{10,11... | collective-permute-start | bytes 405512 | tf_op jit(solution)/shard_map/ppermute | solution.py:593
  76.2 1.4 %collective-permute-start.12 = (f32[264,128]{1,0:T(8,128)S(1)}, f32[264,128]{1,0:T(8,128)S(1)}, u32[]{:S(2)}, u32[]{:S(2)}) collective-permute-start(f32[264,128]{1,0:T(8,128)S(1)} %collective-permute-done.11.refs_0_), channel_id=1, source_target_pairs={{0,1},{1,0},{2,3},{3,2},{4,5},{5,4},{6,7},{7,6},{8,9},{9,8},{10,11... | collective-permute-start | bytes 405512 | tf_op jit(solution)/shard_map/ppermute | solution.py:593
  81.7 14.2 %collective-permute-start.21 = (f32[272,128]{1,0:T(8,128)S(1)}, f32[272,128]{1,0:T(8,128)S(1)}, u32[]{:S(2)}, u32[]{:S(2)}) collective-permute-start(f32[272,128]{1,0:T(8,128)S(1)} %get-tuple-element.33.tail), channel_id=1, source_target_pairs={{0,192},{64,0},{128,64},{192,128},{1,193},{65,1},{129,65},{193,129... | collective-permute-start | bytes 417800 | tf_op jit(solution)/shard_map/ppermute | solution.py:599
  85.4 14.4 %collective-permute-start.19 = (f32[272,128]{1,0:T(8,128)S(1)}, f32[272,128]{1,0:T(8,128)S(1)}, u32[]{:S(2)}, u32[]{:S(2)}) collective-permute-start(f32[272,128]{1,0:T(8,128)S(1)} %get-tuple-element.33.tail), channel_id=1, source_target_pairs={{0,128},{64,192},{128,0},{192,64},{1,129},{65,193},{129,1},{193,65... | collective-permute-start | bytes 417800 | tf_op jit(solution)/shard_map/ppermute | solution.py:599
  87.3 13.2 %collective-permute-start.17 = (f32[272,128]{1,0:T(8,128)S(1)}, f32[272,128]{1,0:T(8,128)S(1)}, u32[]{:S(2)}, u32[]{:S(2)}) collective-permute-start(f32[272,128]{1,0:T(8,128)S(1)} %get-tuple-element.33.tail), channel_id=1, source_target_pairs={{0,64},{64,128},{128,192},{192,0},{1,65},{65,129},{129,193},{193,1... | collective-permute-start | bytes 417800 | tf_op jit(solution)/shard_map/ppermute | solution.py:599
  95.8 5.4 %collective-permute-start.22 = (f32[272,128]{1,0:T(8,128)S(1)}, f32[272,128]{1,0:T(8,128)S(1)}, u32[]{:S(2)}, u32[]{:S(2)}) collective-permute-start(f32[272,128]{1,0:T(8,128)S(1)} %collective-permute-done.21.p4), channel_id=1, source_target_pairs={{0,1},{1,0},{2,3},{3,2},{4,5},{5,4},{6,7},{7,6},{8,9},{9,8},{10,11... | collective-permute-start | bytes 417800 | tf_op jit(solution)/shard_map/ppermute | solution.py:593
  99.8 1.7 %collective-permute-start.20 = (f32[272,128]{1,0:T(8,128)S(1)}, f32[272,128]{1,0:T(8,128)S(1)}, u32[]{:S(2)}, u32[]{:S(2)}) collective-permute-start(f32[272,128]{1,0:T(8,128)S(1)} %collective-permute-done.19.p2), channel_id=1, source_target_pairs={{0,1},{1,0},{2,3},{3,2},{4,5},{5,4},{6,7},{7,6},{8,9},{9,8},{10,11... | collective-permute-start | bytes 417800 | tf_op jit(solution)/shard_map/ppermute | solution.py:593
  100.5 1.7 %collective-permute-start.18 = (f32[272,128]{1,0:T(8,128)S(1)}, f32[272,128]{1,0:T(8,128)S(1)}, u32[]{:S(2)}, u32[]{:S(2)}) collective-permute-start(f32[272,128]{1,0:T(8,128)S(1)} %collective-permute-done.17.p0), channel_id=1, source_target_pairs={{0,1},{1,0},{2,3},{3,2},{4,5},{5,4},{6,7},{7,6},{8,9},{9,8},{10,11... | collective-permute-start | bytes 417800 | tf_op jit(solution)/shard_map/ppermute | solution.py:593

commit v4 on v3

--- a/solution.py
+++ b/solution.py
@@ -403,7 +403,7 @@
         return 0
 
     def group(g, _):
-        lax.fori_loop(8 * g, 8 * g + 8, pair, 0)
+        lax.fori_loop(0, 8, lambda i, _: pair(8 * g + i, 0), 0, unroll=4)
         add_layers(ping, members.at[g], nz)
         return 0
 
@@ -593,10 +593,11 @@
     return lax.ppermute(value, "space", [(0, 1), (1, 0), (2, 3), (3, 2)])
 
 
-def gather_axis(packet, axis):
+def gather_axis(packet, axis, cyclic=True):
     packets = []
     for k in range(1, 4):
-        got = lax.ppermute(packet, axis, [(i, (i + k) % 4) for i in range(4)])
+        pairs = [(i, (i + k) % 4) for i in range(4) if cyclic or i + k < 4]
+        got = lax.ppermute(packet, axis, pairs)
         packets += [got, swap_core(got)]
     return packets
 
@@ -622,7 +623,7 @@
     packet, field4, prefix = chain_level(1, 3, info, field, packet, field, kappa, packets)
     packets = gather_axis(packet, "y")
     packet, _, prefix = chain_level(4, 2, info, field4, packet, prefix, kappa, packets)
-    packets = gather_axis(packet, "zh")
+    packets = gather_axis(packet, "zh", False)
     return fine_sweeps(
         info,
         diffusivity,

time: 120 us -> 119 us (level)
  starting transfers between devices: 52.1 us -> 46 us
  waiting for transfers between devices: 26.3 us -> 32.4 us
    ppermute x9, waiting for transfers between devices: 19.4 us -> 25.5 us  [gather_axis(): got = lax.ppermute(packet, axis, pairs)]
    ppermute x9, starting transfers between devices: 30.9 us -> 25.7 us  [gather_axis(): got = lax.ppermute(packet, axis, pairs)]
where the time goes in v4:
time: 119 us
  starting transfers between devices  46 us (39%)
  waiting for transfers between devices  32.4 us (27%)
  Pallas kernels  26.1 us (22%)
  blocking collectives  9.51 us (8%)
  local copies, waits for them, and re-layouts  4.67 us (4%)
    ppermute x9, starting transfers between devices, gather_axis(): got = lax.ppermute(packet, axis, pairs)  25.7 us
    ppermute x9, waiting for transfers between devices, gather_axis(): got = lax.ppermute(packet, axis, pairs)  25.5 us
    pallas_call x1, Pallas kernels, fine_sweeps(): pl.pallas_call(sweeps_kernel, in_specs=[SMEM, SMEM] + [ANY] * 6 + [VMEM]...  16.6 us
    ppermute x4, starting transfers between devices, to_space(): lax.ppermute(value, 'space', [(i, i + by) for i in range(4) if 0 <= i + b...  14 us
    all_gather x1, blocking collectives, shards(): gathered = lax.all_gather(coarse, 'space', axis=0, tiled=False)  9.51 us
    pallas_call x2, Pallas kernels, chain_level(): pl.pallas_call(functools.partial(level_kernel, length, axis), in_specs=[S...  5.44 us
    ppermute x1, waiting for transfers between devices, to_next(): return lax.ppermute(value, axes, pairs)  3.5 us
    unnamed x14, local copies, waits for them, and re-layouts  3.45 us
  transfers between devices with their start and end apart: 23, of which 14 were waited for; matrix products, arithmetic and copies ran while one was open for 0% of the time, Pallas kernels for 6%

profile of v4, /device:TPU:217, one launch (start us, length us, event | category | flops | bytes accessed | tf_op | source)
XLA Modules:
  0.0 119.0 jit_solution(11975268951598373227)
XLA Ops:
  0.0 1.1 slice_bitcast_fusion
  1.2 3.1 %collective-permute-start = (f32[8,128,128]{2,1,0:T(8,128)S(1)}, f32[8,128,128]{2,1,0:T(8,128)S(1)}, u32[]{:S(2)}, u32[]{:S(2)}) collective-permute-start(f32[8,128,128]{2,1,0:T(8,128)S(1)} %slice_bitcast_fusion), channel_id=1, source_target_pairs={{0,4},{1,5},{2,6},{3,7},{4,8},{5,9},{6,10},{7,11},{8,12},{9,13},{1... | collective-permute-start | bytes 1572872 | tf_op jit(solution)/shard_map/ppermute | solution.py:589
  4.3 2.9 %collective-permute-start.2 = (s32[8,128,128]{2,1,0:T(8,128)}, s32[8,128,128]{2,1,0:T(8,128)S(1)}, u32[]{:S(2)}, u32[]{:S(2)}) collective-permute-start(s32[8,128,128]{2,1,0:T(8,128)} %labels.5), channel_id=1, source_target_pairs={{1,0},{2,1},{3,2},{5,4},{6,5},{7,6},{9,8},{10,9},{11,10},{13,12},{... | collective-permute-start | bytes 1572872 | tf_op jit(solution)/shard_map/ppermute | solution.py:581
  7.2 2.7 %collective-permute-start.1 = (s32[8,128,128]{2,1,0:T(8,128)}, s32[8,128,128]{2,1,0:T(8,128)S(1)}, u32[]{:S(2)}, u32[]{:S(2)}) collective-permute-start(s32[8,128,128]{2,1,0:T(8,128)} %labels.5), channel_id=1, source_target_pairs={{0,1},{1,2},{2,3},{4,5},{5,6},{6,7},{8,9},{9,10},{10,11},{12,13},{... | collective-permute-start | bytes 1572872 | tf_op jit(solution)/shard_map/ppermute | solution.py:581
  9.9 0.1 stack.23.info
  10.0 1.7 %copy-done = f32[1,5,8,128,128]{4,3,2,1,0:T(8,128)S(1)} copy-done((f32[1,5,8,128,128]{4,3,2,1,0:T(8,128)S(1)}, f32[1,5,8,128,128]{4,3,2,1,0:T(8,128)}, u32[]{:S(2)}) %copy-start) | copy-done | bytes 2621464
  11.7 1.0 copy-done.2
  12.7 0.7 copy-done.4
  13.4 1.0 weigh.1
  14.4 3.5 %collective-permute-done.arrived = f32[8,128,128]{2,1,0:T(8,128)S(1)} collective-permute-done((f32[8,128,128]{2,1,0:T(8,128)S(1)}, f32[8,128,128]{2,1,0:T(8,128)S(1)}, u32[]{:S(2)}, u32[]{:S(2)}) %collective-permute-start) | collective-permute-done | bytes 524320 | tf_op jit(solution)/shard_map/ppermute | solution.py:589
  18.0 1.2 %residual.1 = (f32[6,64,128]{2,1,0:T(8,128)S(1)}, f32[8,128,128]{2,1,0:T(8,128)S(1)}) custom-call(s32[5]{0:T(128)S(1)} %stack.23.info, f32[4]{0:T(128)S(1)} %copy-done.5, f32[8,128,128]{2,1,0:T(8,128)S(1)} %get-tuple-element.20.weighted, f32[8,128,128]{2,1,0:T(8,128)S(1)} %collective-permute-done.arrived, f32[1,5,8,128,128]{4,3,2,1,0:T(8,128)S(1)} %copy-done.1, ...), custom_call_target="tpu_custom_call" | custom-call | tf_op jit(solution)/shard_map/residual/pallas_call | solution.py:173
  19.2 9.5 %all-gather = f32[24,64,128]{2,1,0:T(8,128)S(1)} all-gather(f32[6,64,128]{2,1,0:T(8,128)S(1)} %get-tuple-element.23), channel_id=2, replica_groups=mesh['zh'=4,'y'=4,'x'=4,'space'=4] {'space'}, dimensions={0}, use_global_device_ids=true | all-gather | bytes 983040 | tf_op jit(solution)/shard_map/all_gather | solution.py:616
  28.7 0.6 chain_entry.1
  29.3 4.5 %collective-permute-start.3 = (f32[264,128]{1,0:T(8,128)S(1)}, f32[264,128]{1,0:T(8,128)S(1)}, u32[]{:S(2)}, u32[]{:S(2)}) collective-permute-start(f32[264,128]{1,0:T(8,128)S(1)} %get-tuple-element.24.tail), channel_id=1, source_target_pairs={{0,12},{4,0},{8,4},{12,8},{1,13},{5,1},{9,5},{13,9},{2,14},{6,2},{... | collective-permute-start | bytes 405512 | tf_op jit(solution)/shard_map/ppermute | solution.py:600
  33.8 1.2 pack.1.own
  34.9 1.3 %collective-permute-done.3.refs_4_ = f32[264,128]{1,0:T(8,128)S(1)} collective-permute-done((f32[264,128]{1,0:T(8,128)S(1)}, f32[264,128]{1,0:T(8,128)S(1)}, u32[]{:S(2)}, u32[]{:S(2)}) %collective-permute-start.3) | collective-permute-done | bytes 135200 | tf_op jit(solution)/shard_map/ppermute | solution.py:600
  36.2 3.2 %collective-permute-start.5 = (f32[5,8,128,128]{3,2,1,0:T(8,128)S(1)}, f32[5,8,128,128]{3,2,1,0:T(8,128)S(1)}, u32[]{:S(2)}, u32[]{:S(2)}) collective-permute-start(f32[5,8,128,128]{3,2,1,0:T(8,128)S(1)} %pack.1.own), channel_id=1, source_target_pairs={{1,0},{2,1},{3,2},{5,4},{6,5},{7,6},{9,8},{10,9},{11,10},{13,12},{... | collective-permute-start | bytes 7864328 | tf_op jit(solution)/shard_map/ppermute | solution.py:581
  39.5 5.2 %collective-permute-start.4 = (f32[5,8,128,128]{3,2,1,0:T(8,128)S(1)}, f32[5,8,128,128]{3,2,1,0:T(8,128)S(1)}, u32[]{:S(2)}, u32[]{:S(2)}) collective-permute-start(f32[5,8,128,128]{3,2,1,0:T(8,128)S(1)} %pack.1.own), channel_id=1, source_target_pairs={{0,1},{1,2},{2,3},{4,5},{5,6},{6,7},{8,9},{9,10},{10,11},{12,13},{... | collective-permute-start | bytes 7864328 | tf_op jit(solution)/shard_map/ppermute | solution.py:581
  44.7 2.0 %collective-permute-start.8 = (f32[264,128]{1,0:T(8,128)S(1)}, f32[264,128]{1,0:T(8,128)S(1)}, u32[]{:S(2)}, u32[]{:S(2)}) collective-permute-start(f32[264,128]{1,0:T(8,128)S(1)} %get-tuple-element.24.tail), channel_id=1, source_target_pairs={{0,8},{4,12},{8,0},{12,4},{1,9},{5,13},{9,1},{13,5},{2,10},{6,14},... | collective-permute-start | bytes 405512 | tf_op jit(solution)/shard_map/ppermute | solution.py:600
  46.7 2.1 %collective-permute-start.6 = (f32[264,128]{1,0:T(8,128)S(1)}, f32[264,128]{1,0:T(8,128)S(1)}, u32[]{:S(2)}, u32[]{:S(2)}) collective-permute-start(f32[264,128]{1,0:T(8,128)S(1)} %get-tuple-element.24.tail), channel_id=1, source_target_pairs={{0,4},{4,8},{8,12},{12,0},{1,5},{5,9},{9,13},{13,1},{2,6},{6,10},{... | collective-permute-start | bytes 405512 | tf_op jit(solution)/shard_map/ppermute | solution.py:600
  48.8 2.4 %collective-permute-done.8.refs_2_ = f32[264,128]{1,0:T(8,128)S(1)} collective-permute-done((f32[264,128]{1,0:T(8,128)S(1)}, f32[264,128]{1,0:T(8,128)S(1)}, u32[]{:S(2)}, u32[]{:S(2)}) %collective-permute-start.8) | collective-permute-done | bytes 135200 | tf_op jit(solution)/shard_map/ppermute | solution.py:600
  51.2 1.6 %collective-permute-done.6.refs_0_ = f32[264,128]{1,0:T(8,128)S(1)} collective-permute-done((f32[264,128]{1,0:T(8,128)S(1)}, f32[264,128]{1,0:T(8,128)S(1)}, u32[]{:S(2)}, u32[]{:S(2)}) %collective-permute-start.6) | collective-permute-done | bytes 135200 | tf_op jit(solution)/shard_map/ppermute | solution.py:600
  52.8 0.0 collective-permute-start.7
  52.8 0.5 collective-permute-start.10
  53.3 0.8 collective-permute-done.7.refs_1_
  54.1 0.2 collective-permute-done.10.refs_5_
  54.3 1.4 %chain_level_1.1 = (f32[264,128]{1,0:T(8,128)S(1)}, f32[8,64,128]{2,1,0:T(8,128)S(1)}, f32[8,64,128]{2,1,0:T(8,128)S(1)}) custom-call(s32[5]{0:T(128)S(1)} %stack.23.info, f32[8,64,128]{2,1,0:T(8,128)S(1)} %get-tuple-element.27.own.before.field, f32[264,128]{1,0:T(8,128)S(1)} %get-tuple-element.24.tail, ...), custom_call_target="tpu_custom_call" | custom-call | tf_op jit(solution)/shard_map/chain_level_1/pallas_call | solution.py:363
  55.7 0.1 collective-permute-start.15
  55.8 13.0 %collective-permute-start.13 = (f32[264,128]{1,0:T(8,128)S(1)}, f32[264,128]{1,0:T(8,128)S(1)}, u32[]{:S(2)}, u32[]{:S(2)}) collective-permute-start(f32[264,128]{1,0:T(8,128)S(1)} %get-tuple-element.31.tail), channel_id=1, source_target_pairs={{0,32},{16,48},{32,0},{48,16},{1,33},{17,49},{33,1},{49,17},{2,34}... | collective-permute-start | bytes 405512 | tf_op jit(solution)/shard_map/ppermute | solution.py:600
  68.8 2.7 %collective-permute-done.15.refs_4_ = f32[264,128]{1,0:T(8,128)S(1)} collective-permute-done((f32[264,128]{1,0:T(8,128)S(1)}, f32[264,128]{1,0:T(8,128)S(1)}, u32[]{:S(2)}, u32[]{:S(2)}) %collective-permute-start.15) | collective-permute-done | bytes 135200 | tf_op jit(solution)/shard_map/ppermute | solution.py:600
  71.5 0.7 collective-permute-start.16
  72.2 3.1 %collective-permute-done.13.refs_2_ = f32[264,128]{1,0:T(8,128)S(1)} collective-permute-done((f32[264,128]{1,0:T(8,128)S(1)}, f32[264,128]{1,0:T(8,128)S(1)}, u32[]{:S(2)}, u32[]{:S(2)}) %collective-permute-start.13) | collective-permute-done | bytes 135200 | tf_op jit(solution)/shard_map/ppermute | solution.py:600
  75.2 1.0 collective-permute-start.14
  76.2 0.0 collective-permute-start.12
  76.2 1.0 collective-permute-done.14.refs_3_
  77.2 0.4 collective-permute-done.12.refs_1_
  77.6 4.1 %chain_level_4.1 = (f32[272,128]{1,0:T(8,128)S(1)}, f32[8,64,128]{2,1,0:T(8,128)}, f32[8,64,128]{2,1,0:T(8,128)S(1)}) custom-call(s32[5]{0:T(128)S(1)} %stack.23.info, f32[8,64,128]{2,1,0:T(8,128)S(1)} %get-tuple-element.30.own, f32[264,128]{1,0:T(8,128)S(1)} %get-tuple-element.31.tail, f32[8,64,128]{2,1,0:T(8,128)S(1)} %get-tuple-element.32.before, ...), custom_call_target="tpu_custom_call" | custom-call | tf_op jit(solution)/shard_map/chain_level_4/pallas_call | solution.py:363
  81.7 1.5 %collective-permute-start.21 = (f32[272,128]{1,0:T(8,128)S(1)}, f32[272,128]{1,0:T(8,128)S(1)}, u32[]{:S(2)}, u32[]{:S(2)}) collective-permute-start(f32[272,128]{1,0:T(8,128)S(1)} %get-tuple-element.33.tail), channel_id=1, source_target_pairs={{0,192},{1,193},{2,194},{3,195},{4,196},{5,197},{6,198},{7,199},{8... | collective-permute-start | bytes 417800 | tf_op jit(solution)/shard_map/ppermute | solution.py:600
  83.1 1.3 %collective-permute-start.19 = (f32[272,128]{1,0:T(8,128)S(1)}, f32[272,128]{1,0:T(8,128)S(1)}, u32[]{:S(2)}, u32[]{:S(2)}) collective-permute-start(f32[272,128]{1,0:T(8,128)S(1)} %get-tuple-element.33.tail), channel_id=1, source_target_pairs={{0,128},{64,192},{1,129},{65,193},{2,130},{66,194},{3,131},{67,195... | collective-permute-start | bytes 417800 | tf_op jit(solution)/shard_map/ppermute | solution.py:600
  84.4 1.3 %collective-permute-start.17 = (f32[272,128]{1,0:T(8,128)S(1)}, f32[272,128]{1,0:T(8,128)S(1)}, u32[]{:S(2)}, u32[]{:S(2)}) collective-permute-start(f32[272,128]{1,0:T(8,128)S(1)} %get-tuple-element.33.tail), channel_id=1, source_target_pairs={{0,64},{64,128},{128,192},{1,65},{65,129},{129,193},{2,66},{66,130... | collective-permute-start | bytes 417800 | tf_op jit(solution)/shard_map/ppermute | solution.py:600
  85.7 14.4 %collective-permute-done.21.p4 = f32[272,128]{1,0:T(8,128)S(1)} collective-permute-done((f32[272,128]{1,0:T(8,128)S(1)}, f32[272,128]{1,0:T(8,128)S(1)}, u32[]{:S(2)}, u32[]{:S(2)}) %collective-permute-start.21) | collective-permute-done | bytes 139296 | tf_op jit(solution)/shard_map/ppermute | solution.py:600
  100.1 0.5 collective-permute-start.22
  100.7 0.0 collective-permute-start.20
  100.7 0.5 collective-permute-start.18
  101.2 0.5 collective-permute-done.22.p5
  101.7 0.4 collective-permute-done.20.p3
  102.0 0.2 collective-permute-done.18.p1
  102.3 16.6 %fine_sweeps.1 = f32[1,5,8,128,128]{4,3,2,1,0:T(8,128)} custom-call(s32[5]{0:T(128)S(1)} %stack.23.info, f32[4]{0:T(128)S(1)} %copy-done.5, f32[5,8,128,128]{3,2,1,0:T(8,128)S(1)} %pack.1.own, f32[5,8,128,128]{3,2,1,0:T(8,128)S(1)} %collective-permute-done.4.low, f32[5,8,128,128]{3,2,1,0:T(8,128)S(1)} %collective-permute-done.5.high, ...), custom_call_target="tpu_custom_call" | custom-call | tf_op jit(solution)/shard_map/fine_sweeps/pallas_call | solution.py:551
  (22 shorter events, 0.0 us)
Async XLA Ops:
  0.0 18.0 %copy-start.3 = (s32[8,128,128]{2,1,0:T(8,128)S(1)}, s32[8,128,128]{2,1,0:T(8,128)}, u32[]{:S(2)}) copy-start(s32[8,128,128]{2,1,0:T(8,128)} %labels.5) | copy-start | bytes 1572868
  0.0 18.0 %copy-start.5 = (f32[4]{0:T(128)S(1)}, f32[4]{0:T(128)}, u32[]{:S(2)}) copy-start(f32[4]{0:T(128)} %table.5) | copy-start | bytes 52
  0.0 18.0 %copy-start.6 = (s32[1,128]{1,0:T(1,128)S(1)}, s32[1,128]{1,0:T(1,128)}, u32[]{:S(2)}) copy-start(s32[1,128]{1,0:T(1,128)} %shift.5) | copy-start | bytes 1540
  1.2 16.8 %collective-permute-start = (f32[8,128,128]{2,1,0:T(8,128)S(1)}, f32[8,128,128]{2,1,0:T(8,128)S(1)}, u32[]{:S(2)}, u32[]{:S(2)}) collective-permute-start(f32[8,128,128]{2,1,0:T(8,128)S(1)} %slice_bitcast_fusion), channel_id=1, source_target_pairs={{0,4},{1,5},{2,6},{3,7},{4,8},{5,9},{6,10},{7,11},{8,12},{9,13},{1... | collective-permute-start | bytes 1572872 | tf_op jit(solution)/shard_map/ppermute | solution.py:589
  4.3 13.7 %collective-permute-start.2 = (s32[8,128,128]{2,1,0:T(8,128)}, s32[8,128,128]{2,1,0:T(8,128)S(1)}, u32[]{:S(2)}, u32[]{:S(2)}) collective-permute-start(s32[8,128,128]{2,1,0:T(8,128)} %labels.5), channel_id=1, source_target_pairs={{1,0},{2,1},{3,2},{5,4},{6,5},{7,6},{9,8},{10,9},{11,10},{13,12},{... | collective-permute-start | bytes 1572872 | tf_op jit(solution)/shard_map/ppermute | solution.py:581
  7.2 10.8 %collective-permute-start.1 = (s32[8,128,128]{2,1,0:T(8,128)}, s32[8,128,128]{2,1,0:T(8,128)S(1)}, u32[]{:S(2)}, u32[]{:S(2)}) collective-permute-start(s32[8,128,128]{2,1,0:T(8,128)} %labels.5), channel_id=1, source_target_pairs={{0,1},{1,2},{2,3},{4,5},{5,6},{6,7},{8,9},{9,10},{10,11},{12,13},{... | collective-permute-start | bytes 1572872 | tf_op jit(solution)/shard_map/ppermute | solution.py:581
  10.0 1.7 %copy-start = (f32[1,5,8,128,128]{4,3,2,1,0:T(8,128)S(1)}, f32[1,5,8,128,128]{4,3,2,1,0:T(8,128)}, u32[]{:S(2)}) copy-start(f32[1,5,8,128,128]{4,3,2,1,0:T(8,128)} %nodes.3) | copy-start | bytes 7864324
  11.7 1.0 copy-start.2
  12.7 0.7 copy-start.4
  13.4 4.6 %copy-start.1 = (f32[1,5,8,128,128]{4,3,2,1,0:T(8,128)S(1)}, f32[1,5,8,128,128]{4,3,2,1,0:T(8,128)}, u32[]{:S(2)}) copy-start(f32[1,5,8,128,128]{4,3,2,1,0:T(8,128)} %nodes.3) | copy-start | bytes 7864324
  29.3 6.9 %collective-permute-start.3 = (f32[264,128]{1,0:T(8,128)S(1)}, f32[264,128]{1,0:T(8,128)S(1)}, u32[]{:S(2)}, u32[]{:S(2)}) collective-permute-start(f32[264,128]{1,0:T(8,128)S(1)} %get-tuple-element.24.tail), channel_id=1, source_target_pairs={{0,12},{4,0},{8,4},{12,8},{1,13},{5,1},{9,5},{13,9},{2,14},{6,2},{... | collective-permute-start | bytes 405512 | tf_op jit(solution)/shard_map/ppermute | solution.py:600
  36.2 66.0 %collective-permute-start.5 = (f32[5,8,128,128]{3,2,1,0:T(8,128)S(1)}, f32[5,8,128,128]{3,2,1,0:T(8,128)S(1)}, u32[]{:S(2)}, u32[]{:S(2)}) collective-permute-start(f32[5,8,128,128]{3,2,1,0:T(8,128)S(1)} %pack.1.own), channel_id=1, source_target_pairs={{1,0},{2,1},{3,2},{5,4},{6,5},{7,6},{9,8},{10,9},{11,10},{13,12},{... | collective-permute-start | bytes 7864328 | tf_op jit(solution)/shard_map/ppermute | solution.py:581
  39.5 62.8 %collective-permute-start.4 = (f32[5,8,128,128]{3,2,1,0:T(8,128)S(1)}, f32[5,8,128,128]{3,2,1,0:T(8,128)S(1)}, u32[]{:S(2)}, u32[]{:S(2)}) collective-permute-start(f32[5,8,128,128]{3,2,1,0:T(8,128)S(1)} %pack.1.own), channel_id=1, source_target_pairs={{0,1},{1,2},{2,3},{4,5},{5,6},{6,7},{8,9},{9,10},{10,11},{12,13},{... | collective-permute-start | bytes 7864328 | tf_op jit(solution)/shard_map/ppermute | solution.py:581
  44.7 6.5 %collective-permute-start.8 = (f32[264,128]{1,0:T(8,128)S(1)}, f32[264,128]{1,0:T(8,128)S(1)}, u32[]{:S(2)}, u32[]{:S(2)}) collective-permute-start(f32[264,128]{1,0:T(8,128)S(1)} %get-tuple-element.24.tail), channel_id=1, source_target_pairs={{0,8},{4,12},{8,0},{12,4},{1,9},{5,13},{9,1},{13,5},{2,10},{6,14},... | collective-permute-start | bytes 405512 | tf_op jit(solution)/shard_map/ppermute | solution.py:600
  46.7 6.1 %collective-permute-start.6 = (f32[264,128]{1,0:T(8,128)S(1)}, f32[264,128]{1,0:T(8,128)S(1)}, u32[]{:S(2)}, u32[]{:S(2)}) collective-permute-start(f32[264,128]{1,0:T(8,128)S(1)} %get-tuple-element.24.tail), channel_id=1, source_target_pairs={{0,4},{4,8},{8,12},{12,0},{1,5},{5,9},{9,13},{13,1},{2,6},{6,10},{... | collective-permute-start | bytes 405512 | tf_op jit(solution)/shard_map/ppermute | solution.py:600
  51.2 2.1 %collective-permute-start.9 = (f32[264,128]{1,0:T(8,128)S(1)}, f32[264,128]{1,0:T(8,128)S(1)}, u32[]{:S(2)}, u32[]{:S(2)}) collective-permute-start(f32[264,128]{1,0:T(8,128)S(1)} %collective-permute-done.8.refs_2_), channel_id=1, source_target_pairs={{0,1},{1,0},{2,3},{3,2},{4,5},{5,4},{6,7},{7,6},{8,9},{9,8},{10,11... | collective-permute-start | bytes 405512 | tf_op jit(solution)/shard_map/ppermute | solution.py:593
  52.8 1.4 %collective-permute-start.7 = (f32[264,128]{1,0:T(8,128)S(1)}, f32[264,128]{1,0:T(8,128)S(1)}, u32[]{:S(2)}, u32[]{:S(2)}) collective-permute-start(f32[264,128]{1,0:T(8,128)S(1)} %collective-permute-done.6.refs_0_), channel_id=1, source_target_pairs={{0,1},{1,0},{2,3},{3,2},{4,5},{5,4},{6,7},{7,6},{8,9},{9,8},{10,11... | collective-permute-start | bytes 405512 | tf_op jit(solution)/shard_map/ppermute | solution.py:593
  52.8 1.5 %collective-permute-start.10 = (f32[264,128]{1,0:T(8,128)S(1)}, f32[264,128]{1,0:T(8,128)S(1)}, u32[]{:S(2)}, u32[]{:S(2)}) collective-permute-start(f32[264,128]{1,0:T(8,128)S(1)} %collective-permute-done.3.refs_4_), channel_id=1, source_target_pairs={{0,1},{1,0},{2,3},{3,2},{4,5},{5,4},{6,7},{7,6},{8,9},{9,8},{10,11... | collective-permute-start | bytes 405512 | tf_op jit(solution)/shard_map/ppermute | solution.py:593
  55.7 15.8 %collective-permute-start.15 = (f32[264,128]{1,0:T(8,128)S(1)}, f32[264,128]{1,0:T(8,128)S(1)}, u32[]{:S(2)}, u32[]{:S(2)}) collective-permute-start(f32[264,128]{1,0:T(8,128)S(1)} %get-tuple-element.31.tail), channel_id=1, source_target_pairs={{0,48},{16,0},{32,16},{48,32},{1,49},{17,1},{33,17},{49,33},{2,50}... | collective-permute-start | bytes 405512 | tf_op jit(solution)/shard_map/ppermute | solution.py:600
  55.8 19.5 %collective-permute-start.13 = (f32[264,128]{1,0:T(8,128)S(1)}, f32[264,128]{1,0:T(8,128)S(1)}, u32[]{:S(2)}, u32[]{:S(2)}) collective-permute-start(f32[264,128]{1,0:T(8,128)S(1)} %get-tuple-element.31.tail), channel_id=1, source_target_pairs={{0,32},{16,48},{32,0},{48,16},{1,33},{17,49},{33,1},{49,17},{2,34}... | collective-permute-start | bytes 405512 | tf_op jit(solution)/shard_map/ppermute | solution.py:600
  68.8 7.4 %collective-permute-start.11 = (f32[264,128]{1,0:T(8,128)S(1)}, f32[264,128]{1,0:T(8,128)S(1)}, u32[]{:S(2)}, u32[]{:S(2)}) collective-permute-start(f32[264,128]{1,0:T(8,128)S(1)} %get-tuple-element.31.tail), channel_id=1, source_target_pairs={{0,16},{16,32},{32,48},{48,0},{1,17},{17,33},{33,49},{49,1},{2,18}... | collective-permute-start | bytes 405512 | tf_op jit(solution)/shard_map/ppermute | solution.py:600
  71.5 4.8 %collective-permute-start.16 = (f32[264,128]{1,0:T(8,128)S(1)}, f32[264,128]{1,0:T(8,128)S(1)}, u32[]{:S(2)}, u32[]{:S(2)}) collective-permute-start(f32[264,128]{1,0:T(8,128)S(1)} %collective-permute-done.15.refs_4_), channel_id=1, source_target_pairs={{0,1},{1,0},{2,3},{3,2},{4,5},{5,4},{6,7},{7,6},{8,9},{9,8},{10,11... | collective-permute-start | bytes 405512 | tf_op jit(solution)/shard_map/ppermute | solution.py:593
  75.2 2.0 %collective-permute-start.14 = (f32[264,128]{1,0:T(8,128)S(1)}, f32[264,128]{1,0:T(8,128)S(1)}, u32[]{:S(2)}, u32[]{:S(2)}) collective-permute-start(f32[264,128]{1,0:T(8,128)S(1)} %collective-permute-done.13.refs_2_), channel_id=1, source_target_pairs={{0,1},{1,0},{2,3},{3,2},{4,5},{5,4},{6,7},{7,6},{8,9},{9,8},{10,11... | collective-permute-start | bytes 405512 | tf_op jit(solution)/shard_map/ppermute | solution.py:593
  76.2 1.4 %collective-permute-start.12 = (f32[264,128]{1,0:T(8,128)S(1)}, f32[264,128]{1,0:T(8,128)S(1)}, u32[]{:S(2)}, u32[]{:S(2)}) collective-permute-start(f32[264,128]{1,0:T(8,128)S(1)} %collective-permute-done.11.refs_0_), channel_id=1, source_target_pairs={{0,1},{1,0},{2,3},{3,2},{4,5},{5,4},{6,7},{7,6},{8,9},{9,8},{10,11... | collective-permute-start | bytes 405512 | tf_op jit(solution)/shard_map/ppermute | solution.py:593
  81.7 18.5 %collective-permute-start.21 = (f32[272,128]{1,0:T(8,128)S(1)}, f32[272,128]{1,0:T(8,128)S(1)}, u32[]{:S(2)}, u32[]{:S(2)}) collective-permute-start(f32[272,128]{1,0:T(8,128)S(1)} %get-tuple-element.33.tail), channel_id=1, source_target_pairs={{0,192},{1,193},{2,194},{3,195},{4,196},{5,197},{6,198},{7,199},{8... | collective-permute-start | bytes 417800 | tf_op jit(solution)/shard_map/ppermute | solution.py:600
  83.1 17.6 %collective-permute-start.19 = (f32[272,128]{1,0:T(8,128)S(1)}, f32[272,128]{1,0:T(8,128)S(1)}, u32[]{:S(2)}, u32[]{:S(2)}) collective-permute-start(f32[272,128]{1,0:T(8,128)S(1)} %get-tuple-element.33.tail), channel_id=1, source_target_pairs={{0,128},{64,192},{1,129},{65,193},{2,130},{66,194},{3,131},{67,195... | collective-permute-start | bytes 417800 | tf_op jit(solution)/shard_map/ppermute | solution.py:600
  84.4 16.3 %collective-permute-start.17 = (f32[272,128]{1,0:T(8,128)S(1)}, f32[272,128]{1,0:T(8,128)S(1)}, u32[]{:S(2)}, u32[]{:S(2)}) collective-permute-start(f32[272,128]{1,0:T(8,128)S(1)} %get-tuple-element.33.tail), channel_id=1, source_target_pairs={{0,64},{64,128},{128,192},{1,65},{65,129},{129,193},{2,66},{66,130... | collective-permute-start | bytes 417800 | tf_op jit(solution)/shard_map/ppermute | solution.py:600
  100.1 1.5 %collective-permute-start.22 = (f32[272,128]{1,0:T(8,128)S(1)}, f32[272,128]{1,0:T(8,128)S(1)}, u32[]{:S(2)}, u32[]{:S(2)}) collective-permute-start(f32[272,128]{1,0:T(8,128)S(1)} %collective-permute-done.21.p4), channel_id=1, source_target_pairs={{0,1},{1,0},{2,3},{3,2},{4,5},{5,4},{6,7},{7,6},{8,9},{9,8},{10,11... | collective-permute-start | bytes 417800 | tf_op jit(solution)/shard_map/ppermute | solution.py:593
  100.7 1.4 %collective-permute-start.20 = (f32[272,128]{1,0:T(8,128)S(1)}, f32[272,128]{1,0:T(8,128)S(1)}, u32[]{:S(2)}, u32[]{:S(2)}) collective-permute-start(f32[272,128]{1,0:T(8,128)S(1)} %collective-permute-done.19.p2), channel_id=1, source_target_pairs={{0,1},{1,0},{2,3},{3,2},{4,5},{5,4},{6,7},{7,6},{8,9},{9,8},{10,11... | collective-permute-start | bytes 417800 | tf_op jit(solution)/shard_map/ppermute | solution.py:593
  100.7 1.6 %collective-permute-start.18 = (f32[272,128]{1,0:T(8,128)S(1)}, f32[272,128]{1,0:T(8,128)S(1)}, u32[]{:S(2)}, u32[]{:S(2)}) collective-permute-start(f32[272,128]{1,0:T(8,128)S(1)} %collective-permute-done.17.p0), channel_id=1, source_target_pairs={{0,1},{1,0},{2,3},{3,2},{4,5},{5,4},{6,7},{7,6},{8,9},{9,8},{10,11... | collective-permute-start | bytes 417800 | tf_op jit(solution)/shard_map/ppermute | solution.py:593
